TPU v7x, 32 devices: a whole 2x2x4 slice. The times are simulated.
32 devices in a mesh: batch: 4 (over z), gran: 4 (over y, x), ffn: 2 (over core).
Axes of the slice: x: 2, y: 2, z: 4, core: 2. Of those that a mesh axis runs over, the one named last changes fastest.
Arguments:
- tokens: bfloat16 [4096, 1536], P(('batch', 'gran', 'ffn')), may hold values from -26 to 26
- seq_ids: int32 [4096], P(('batch', 'gran', 'ffn')), may hold values from 0 to 3, as said below
- granularity: int32 [128], P(('batch', 'gran', 'ffn')), may hold values from 0 to 3
- w_qkv: bfloat16 [1536, 4608], P('batch'), may hold values from -0.15625 to 0.15625
- w_out: bfloat16 [1536, 1536], P('batch'), may hold values from -1.75 to 1.75
- gain_attn: bfloat16 [1536], P('batch'), may hold values from 0.5 to 1.5
- gain_ffn: bfloat16 [1536], P('batch'), may hold values from 0.5 to 1.5
- w_gate: bfloat16 [1536, 2, 3072], P('batch', 'ffn'), may hold values from -0.15625 to 0.15625
- w_up: bfloat16 [1536, 2, 3072], P('batch', 'ffn'), may hold values from -0.15625 to 0.15625
- w_down: bfloat16 [3072, 2, 1536], P('batch', 'ffn'), may hold values from -0.21875 to 0.21875
- out_cotangent: bfloat16 [4096, 1536], P(('batch', 'gran', 'ffn')), may hold values from -6 to 6
Outputs:
- outputs: bfloat16 [4096, 1536], P(('batch', 'gran', 'ffn'))
- input_grad: bfloat16 [4096, 1536], P(('batch', 'gran', 'ffn'))
- grad_w_qkv: float32 [1536, 4608], P('batch')
- grad_w_out: float32 [1536, 1536], P('batch')
- grad_gain_attn: float32 [1536], P('batch')
- grad_gain_ffn: float32 [1536], P('batch')
- grad_w_gate: float32 [1536, 2, 3072], P('batch', 'ffn')
- grad_w_up: float32 [1536, 2, 3072], P('batch', 'ffn')
- grad_w_down: float32 [3072, 2, 1536], P('batch', 'ffn')
Inputs may be any that keep to these rules, and one draw needn't show every extreme that they name: `seq_ids`: within each device's block of 128 rows the ids never fall; a sequence may have no rows; on some device one sequence fills all 128 rows, and on some device every sequence has rows. `granularity`: entry i is the group of sequence i mod 4 of the device holding the sequence ids of block i // 4.
All inputs are finite; a program needn't handle non-finite values.
Results may differ from a plain program's by a relative error of at most 0.02.
Values may be sent and summed in bfloat16 or wider, within the bound.
No kernel may reach another device: no remote copies, remote signals or barrier semaphores. Data moves between devices by JAX's collectives and lax.ppermute only.
A program may use at most 256 MiB of HBM per device.

v0:
```python
import math

import jax
import jax.numpy as jnp
from jax import lax
from jax.sharding import PartitionSpec as P

H = 12


EPSILON = 1e-06
NEG_FILL = -1e30
ROPE_BASE = 10000.0


def seq_positions(seq_rows, seq_count):
    labels = jnp.arange(seq_count, dtype=jnp.int32)
    member = (seq_rows[:, None] == labels[None, :]).astype(jnp.int32)
    lengths = jnp.sum(member, axis=0)
    starts = jnp.cumsum(lengths) - lengths
    first_row = jnp.sum(member * starts[None, :], axis=1)
    return jnp.arange(seq_rows.shape[0], dtype=jnp.int32) - first_row


def route_rows(seq_rows, seq_groups, batch_index, batch_count, group_count, capacity):
    labels = jnp.arange(seq_groups.shape[0], dtype=jnp.int32)
    member = (seq_rows[:, None] == labels[None, :]).astype(jnp.int32)
    group_id = jnp.sum(member * seq_groups[None, :], axis=1)
    onehot = (group_id[:, None] == jnp.arange(group_count, dtype=jnp.int32)[None, :]).astype(
        jnp.int32
    )
    before = jnp.cumsum(onehot, axis=0) - onehot
    order_rank = jnp.sum(before * onehot, axis=1)
    keep_row = order_rank < capacity * batch_count
    target = (batch_index + order_rank) % batch_count
    slot_index = order_rank // batch_count
    return (group_id, keep_row, target, slot_index)


def rotate_half(vectors, cosines, sines):
    half_size = vectors.shape[-1] // 2
    front_half = vectors[..., :half_size]
    back_part = vectors[..., half_size:]
    return jnp.concatenate(
        [front_half * cosines - back_part * sines, back_part * cosines + front_half * sines],
        axis=-1,
    )


def rotate_back(vectors, cosines, sines):
    half_size = vectors.shape[-1] // 2
    front_half = vectors[..., :half_size]
    back_part = vectors[..., half_size:]
    return jnp.concatenate(
        [front_half * cosines + back_part * sines, back_part * cosines - front_half * sines],
        axis=-1,
    )


def contract_rows(left, right):
    return lax.dot_general(
        left, right, (((0,), (0,)), ((), ())), preferred_element_type=jnp.float32
    )


def contract_cols(left, right):
    return lax.dot_general(
        left, right, (((1,), (1,)), ((), ())), preferred_element_type=jnp.float32
    )


def norm_back(grad_normed, unit_rows, inverse_rms, gain):
    scaled = grad_normed * gain
    return inverse_rms * (scaled - unit_rows * jnp.mean(scaled * unit_rows, axis=-1, keepdims=True))


def local(
    tokens,
    seq_ids,
    granularity,
    w_qkv,
    w_out,
    gain_attn,
    gain_ffn,
    w_gate,
    w_up,
    w_down,
    out_cotangent,
):
    batch_count = lax.axis_size("batch")
    group_count = lax.axis_size("gran")
    batch_index = lax.axis_index("batch")
    my_group = lax.axis_index("gran")
    row_count, feature_count = tokens.shape
    head_size = feature_count // H
    half_units = w_gate.shape[2]
    capacity = max(
        2, (5 * row_count + 4 * batch_count * group_count - 1) // (4 * batch_count * group_count)
    )
    slots = batch_count * group_count * capacity
    full_qkv, full_out, full_gain_attn, full_gain_ffn, full_gate, full_up, full_down = (
        lax.all_gather(w_qkv, "batch", axis=0, tiled=True),
        lax.all_gather(w_out, "batch", axis=0, tiled=True),
        lax.all_gather(gain_attn, "batch", axis=0, tiled=True),
        lax.all_gather(gain_ffn, "batch", axis=0, tiled=True),
        lax.all_gather(w_gate, "batch", axis=0, tiled=True),
        lax.all_gather(w_up, "batch", axis=0, tiled=True),
        lax.all_gather(w_down, "batch", axis=0, tiled=True),
    )
    gate_matrix = full_gate[:, 0, :]
    up_matrix = full_up[:, 0, :]
    down_matrix = full_down[:, 0, :]
    gain_first = full_gain_attn.astype(jnp.float32)
    gain_second = full_gain_ffn.astype(jnp.float32)
    residual = tokens.astype(jnp.float32)
    inverse_first = lax.rsqrt(jnp.mean(residual * residual, axis=-1, keepdims=True) + EPSILON)
    unit_first = residual * inverse_first
    normed = (unit_first * gain_first).astype(jnp.bfloat16)
    packed = jnp.dot(normed, full_qkv, preferred_element_type=jnp.float32).reshape(
        row_count, 3, H, head_size
    )
    positions = seq_positions(seq_ids, granularity.shape[0])
    frequencies = ROPE_BASE ** (-(2.0 * jnp.arange(head_size // 2, dtype=jnp.float32)) / head_size)
    angles = positions.astype(jnp.float32)[:, None] * frequencies
    cosines = jnp.cos(angles)[:, None, :]
    sines = jnp.sin(angles)[:, None, :]
    score_scale = 1.0 / math.sqrt(head_size)
    queries = (rotate_half(packed[:, 0], cosines, sines) * score_scale).astype(jnp.bfloat16)
    keys_rot = rotate_half(packed[:, 1], cosines, sines).astype(jnp.bfloat16)
    values = packed[:, 2].astype(jnp.bfloat16)
    row_index = jnp.arange(row_count, dtype=jnp.int32)
    allowed = (seq_ids[:, None] == seq_ids[None, :]) & (row_index[:, None] >= row_index[None, :])
    scores = jnp.einsum("qhe,khe->hqk", queries, keys_rot, preferred_element_type=jnp.float32)
    scores = jnp.where(allowed[None], scores, NEG_FILL)
    top_score = jnp.max(scores, axis=-1, keepdims=True)
    exponent = jnp.exp(scores - top_score)
    probs = exponent / jnp.sum(exponent, axis=-1, keepdims=True)
    prob_weights = probs.astype(jnp.bfloat16)
    attended = jnp.einsum("hqk,khe->qhe", prob_weights, values, preferred_element_type=jnp.float32)
    attended = attended.reshape(row_count, feature_count).astype(jnp.bfloat16)
    branch_attn = jnp.dot(attended, full_out, preferred_element_type=jnp.float32)
    middle = residual + branch_attn
    inverse_second = lax.rsqrt(jnp.mean(middle * middle, axis=-1, keepdims=True) + EPSILON)
    unit_second = middle * inverse_second
    normed_ffn = (unit_second * gain_second).astype(jnp.bfloat16)
    group_id, keep_row, target, slot_index = route_rows(
        seq_ids, granularity, batch_index, batch_count, group_count, capacity
    )
    send_place = jnp.where(
        keep_row, (target * group_count + group_id) * capacity + slot_index, slots
    )
    safe_place = jnp.minimum(send_place, slots - 1)
    send_rows = (
        jnp.zeros((slots, feature_count), jnp.bfloat16).at[send_place].set(normed_ffn, mode="drop")
    )
    send_grads = (
        jnp.zeros((slots, feature_count), jnp.bfloat16)
        .at[send_place]
        .set(out_cotangent, mode="drop")
    )
    recv_rows, recv_grads = (
        lax.all_to_all(send_rows, ("batch", "gran"), split_axis=0, concat_axis=0, tiled=True),
        lax.all_to_all(send_grads, ("batch", "gran"), split_axis=0, concat_axis=0, tiled=True),
    )
    group_rows, group_grads = (
        lax.all_gather(recv_rows, "ffn", axis=0, tiled=True),
        lax.all_gather(recv_grads, "ffn", axis=0, tiled=True),
    )
    prefix = jnp.right_shift(jnp.int32(half_units), 3 - my_group)
    live_cols = (jnp.arange(half_units, dtype=jnp.int32) < prefix)[None, :]
    gate_pre = jnp.dot(group_rows, gate_matrix, preferred_element_type=jnp.float32)
    lifted = jnp.dot(group_rows, up_matrix, preferred_element_type=jnp.float32)
    sigmoid_gate = jax.nn.sigmoid(gate_pre)
    activated = gate_pre * sigmoid_gate
    hidden = jnp.where(
        live_cols, (activated * lifted).astype(jnp.bfloat16), jnp.zeros((), jnp.bfloat16)
    )
    ffn_rows = lax.psum_scatter(
        jnp.dot(hidden, down_matrix, preferred_element_type=jnp.float32).astype(jnp.bfloat16),
        "ffn",
        scatter_dimension=0,
        tiled=True,
    )
    returned = lax.all_to_all(ffn_rows, ("batch", "gran"), split_axis=0, concat_axis=0, tiled=True)
    branch_ffn = jnp.where(
        keep_row[:, None], jnp.take(returned, safe_place, axis=0), jnp.zeros((), jnp.bfloat16)
    ).astype(jnp.float32)
    result = middle + branch_ffn
    outputs = result.astype(jnp.bfloat16)
    grad_hidden = jnp.where(live_cols, contract_cols(group_grads, down_matrix), 0.0)
    grad_gate = (
        grad_hidden * lifted * sigmoid_gate * (1.0 + gate_pre * (1.0 - sigmoid_gate))
    ).astype(jnp.bfloat16)
    grad_lifted = (grad_hidden * activated).astype(jnp.bfloat16)
    grad_down_w = contract_rows(hidden, group_grads)
    grad_gate_w = contract_rows(group_rows, grad_gate)
    grad_up_w = contract_rows(group_rows, grad_lifted)
    input_rows = lax.psum_scatter(
        contract_cols(grad_gate, gate_matrix) + contract_cols(grad_lifted, up_matrix),
        "ffn",
        scatter_dimension=0,
        tiled=True,
    )
    returned_grads = lax.all_to_all(
        input_rows.astype(jnp.bfloat16), ("batch", "gran"), split_axis=0, concat_axis=0, tiled=True
    )
    grad_normed_ffn = jnp.where(
        keep_row[:, None], jnp.take(returned_grads, safe_place, axis=0), jnp.zeros((), jnp.bfloat16)
    ).astype(jnp.float32)
    grad_gain_ffn = jnp.sum(grad_normed_ffn * unit_second, axis=0)
    grad_middle = out_cotangent.astype(jnp.float32) + norm_back(
        grad_normed_ffn, unit_second, inverse_second, gain_second
    )
    grad_branch = grad_middle.astype(jnp.bfloat16)
    grad_out_w = contract_rows(attended, grad_branch)
    grad_attended = (
        contract_cols(grad_branch, full_out).astype(jnp.bfloat16).reshape(row_count, H, head_size)
    )
    grad_probs = jnp.einsum(
        "qhe,khe->hqk", grad_attended, values, preferred_element_type=jnp.float32
    )
    grad_scores = (
        probs * (grad_probs - jnp.sum(probs * grad_probs, axis=-1, keepdims=True))
    ).astype(jnp.bfloat16)
    grad_queries = jnp.einsum(
        "hqk,khe->qhe", grad_scores, keys_rot, preferred_element_type=jnp.float32
    ).astype(jnp.bfloat16)
    grad_keys = jnp.einsum(
        "hqk,qhe->khe", grad_scores, queries, preferred_element_type=jnp.float32
    ).astype(jnp.bfloat16)
    grad_values = jnp.einsum(
        "hqk,qhe->khe", prob_weights, grad_attended, preferred_element_type=jnp.float32
    ).astype(jnp.bfloat16)
    grad_packed = (
        jnp.stack(
            [
                rotate_back(grad_queries.astype(jnp.float32) * score_scale, cosines, sines),
                rotate_back(grad_keys.astype(jnp.float32), cosines, sines),
                grad_values.astype(jnp.float32),
            ],
            axis=1,
        )
        .reshape(row_count, 3 * feature_count)
        .astype(jnp.bfloat16)
    )
    grad_qkv_w = contract_rows(normed, grad_packed)
    grad_normed = contract_cols(grad_packed, full_qkv)
    grad_gain_attn = jnp.sum(grad_normed * unit_first, axis=0)
    input_grad = (
        grad_middle + norm_back(grad_normed, unit_first, inverse_first, gain_first)
    ).astype(jnp.bfloat16)
    share_qkv, share_out, share_gain_attn, share_gain_ffn, share_gate, share_up, share_down = (
        lax.psum_scatter(
            grad_qkv_w.astype(jnp.bfloat16), "batch", scatter_dimension=0, tiled=True
        ).astype(jnp.float32),
        lax.psum_scatter(
            grad_out_w.astype(jnp.bfloat16), "batch", scatter_dimension=0, tiled=True
        ).astype(jnp.float32),
        lax.psum_scatter(
            grad_gain_attn.astype(jnp.bfloat16), "batch", scatter_dimension=0, tiled=True
        ).astype(jnp.float32),
        lax.psum_scatter(
            grad_gain_ffn.astype(jnp.bfloat16), "batch", scatter_dimension=0, tiled=True
        ).astype(jnp.float32),
        lax.psum_scatter(
            grad_gate_w.astype(jnp.bfloat16), "batch", scatter_dimension=0, tiled=True
        ).astype(jnp.float32),
        lax.psum_scatter(
            grad_up_w.astype(jnp.bfloat16), "batch", scatter_dimension=0, tiled=True
        ).astype(jnp.float32),
        lax.psum_scatter(
            grad_down_w.astype(jnp.bfloat16), "batch", scatter_dimension=0, tiled=True
        ).astype(jnp.float32),
    )
    share_qkv, share_out, share_gain_attn, share_gain_ffn, share_gate, share_up, share_down = (
        lax.psum(share_qkv.astype(jnp.bfloat16), "gran").astype(jnp.float32),
        lax.psum(share_out.astype(jnp.bfloat16), "gran").astype(jnp.float32),
        lax.psum(share_gain_attn.astype(jnp.bfloat16), "gran").astype(jnp.float32),
        lax.psum(share_gain_ffn.astype(jnp.bfloat16), "gran").astype(jnp.float32),
        lax.psum(share_gate.astype(jnp.bfloat16), "gran").astype(jnp.float32),
        lax.psum(share_up.astype(jnp.bfloat16), "gran").astype(jnp.float32),
        lax.psum(share_down.astype(jnp.bfloat16), "gran").astype(jnp.float32),
    )
    share_qkv, share_out, share_gain_attn, share_gain_ffn = (
        lax.psum(share_qkv.astype(jnp.bfloat16), "ffn").astype(jnp.float32),
        lax.psum(share_out.astype(jnp.bfloat16), "ffn").astype(jnp.float32),
        lax.psum(share_gain_attn.astype(jnp.bfloat16), "ffn").astype(jnp.float32),
        lax.psum(share_gain_ffn.astype(jnp.bfloat16), "ffn").astype(jnp.float32),
    )
    return (
        outputs,
        input_grad,
        share_qkv,
        share_out,
        share_gain_attn,
        share_gain_ffn,
        share_gate[:, None, :],
        share_up[:, None, :],
        share_down[:, None, :],
    )


def solution(mesh):
    in_specs = (
        P(("batch", "gran", "ffn"), None),
        P(("batch", "gran", "ffn")),
        P(("batch", "gran", "ffn")),
        P("batch", None),
        P("batch", None),
        P("batch"),
        P("batch"),
        P("batch", "ffn", None),
        P("batch", "ffn", None),
        P("batch", "ffn", None),
        P(("batch", "gran", "ffn"), None),
    )
    out_specs = (
        P(("batch", "gran", "ffn"), None),
        P(("batch", "gran", "ffn"), None),
        P("batch", None),
        P("batch", None),
        P("batch"),
        P("batch"),
        P("batch", "ffn", None),
        P("batch", "ffn", None),
        P("batch", "ffn", None),
    )
    return jax.shard_map(local, mesh=mesh, in_specs=in_specs, out_specs=out_specs, check_vma=False)
```

profile of v0, /device:TPU:0, one launch (start us, length us, event | category | flops | bytes accessed | tf_op | source)
XLA Modules:
  0.0 2095.4 jit_solution(7463493287109571449)
XLA Ops:
  23.4 55.1 %all-gather = bf16[4,1,384]{2,1,0:T(2,128)(2,1)S(1)} all-gather(bf16[1,1,384]{2,1,0:T(2,128)(2,1)S(1)} %reshape.363), channel_id=1, replica_groups=mesh['batch'=4,'gran'=4,'ffn'=2] {'batch'}, dimensions={0}, use_global_device_ids=true | all-gather | bytes 3840 | tf_op jit(solution)/shard_map/all_gather | solution.py:104
  78.4 19.2 all-gather.1
  101.1 170.7 %all-gather.8.cloned.1.call-done = bf16[1536,4608]{1,0:T(8,128)(2,1)} async-done(((bf16[384,4608]{1,0:T(8,128)(2,1)}), bf16[1536,4608]{1,0:T(8,128)(2,1)}) %all-gather.8.cloned.1.call-update) | async-done | bytes 14155792 | tf_op jit(solution)/shard_map/all_gather | solution.py:102
  271.8 9.0 fusion.66
  285.9 75.9 %all-gather.10.cloned.1.call-done = bf16[1536,1536]{1,0:T(8,128)(2,1)} async-done(((bf16[384,1536]{1,0:T(8,128)(2,1)}), bf16[1536,1536]{1,0:T(8,128)(2,1)}) %all-gather.10.cloned.1.call-update) | async-done | bytes 4718608 | tf_op jit(solution)/shard_map/all_gather | solution.py:103
  371.9 172.3 %all-gather.16.cloned.1.call-done = bf16[3072,1,1536]{2,0,1:T(8,128)(2,1)} async-done(((bf16[768,1,1536]{2,0,1:T(8,128)(2,1)}), bf16[3072,1,1536]{2,0,1:T(8,128)(2,1)}) %all-gather.16.cloned.1.call-update) | async-done | bytes 9437200 | tf_op jit(solution)/shard_map/all_gather | solution.py:108
  544.2 9.2 fusion.13
  556.1 155.4 %all-gather.14.cloned.1.call-done = bf16[1536,1,3072]{2,0,1:T(8,128)(2,1)} async-done(((bf16[384,1,3072]{2,0,1:T(8,128)(2,1)}), bf16[1536,1,3072]{2,0,1:T(8,128)(2,1)}) %all-gather.14.cloned.1.call-update) | async-done | bytes 9437200 | tf_op jit(solution)/shard_map/all_gather | solution.py:107
  711.5 8.9 fusion.7
  720.4 157.5 %all-gather.12.cloned.1.call-done = bf16[1536,1,3072]{2,0,1:T(8,128)(2,1)} async-done(((bf16[384,1,3072]{2,0,1:T(8,128)(2,1)}), bf16[1536,1,3072]{2,0,1:T(8,128)(2,1)}) %all-gather.12.cloned.1.call-update) | async-done | bytes 9437200 | tf_op jit(solution)/shard_map/all_gather | solution.py:106
  877.9 11.1 multiply_convert_fusion.1
  925.0 15.7 all-to-all-done.1
  947.6 16.7 all-to-all-done.3
  973.1 9.1 convolution_convert_fusion.3
  982.5 9.1 convolution_convert_fusion.2
  1018.6 38.0 %reduce-scatter.14.cloned.1.call-done = bf16[384,1536]{1,0:T(8,128)(2,1)} async-done(((bf16[1536,1536]{1,0:T(8,128)(2,1)}), bf16[384,1536]{1,0:T(8,128)(2,1)}) %reduce-scatter.14.cloned.1.call-update) | async-done | bytes 1179664 | tf_op jit(solution)/shard_map/reduce_scatter | solution.py:256
  1056.6 164.2 %reduce-scatter.16.cloned.1.call-done = bf16[384,3072]{1,0:T(8,128)(2,1)} async-done(((bf16[1536,3072]{1,0:T(8,128)(2,1)}), bf16[384,3072]{1,0:T(8,128)(2,1)}) %reduce-scatter.16.cloned.1.call-update) | async-done | bytes 2359312 | tf_op jit(solution)/shard_map/reduce_scatter | solution.py:265
  1220.8 164.4 %reduce-scatter.18.cloned.1.call-done = bf16[384,3072]{1,0:T(8,128)(2,1)} async-done(((bf16[1536,3072]{1,0:T(8,128)(2,1)}), bf16[384,3072]{1,0:T(8,128)(2,1)}) %reduce-scatter.18.cloned.1.call-update) | async-done | bytes 2359312 | tf_op jit(solution)/shard_map/reduce_scatter | solution.py:268
  1385.2 164.5 %reduce-scatter.20.cloned.1.call-done = bf16[768,1536]{1,0:T(8,128)(2,1)} async-done(((bf16[3072,1536]{1,0:T(8,128)(2,1)}), bf16[768,1536]{1,0:T(8,128)(2,1)}) %reduce-scatter.20.cloned.1.call-update) | async-done | bytes 2359312 | tf_op jit(solution)/shard_map/reduce_scatter | solution.py:271
  1549.7 240.3 %reduce-scatter.12.cloned.1.call-done = bf16[384,4608]{1,0:T(8,128)(2,1)} async-done(((bf16[1536,4608]{1,0:T(8,128)(2,1)}), bf16[384,4608]{1,0:T(8,128)(2,1)}) %reduce-scatter.12.cloned.1.call-update) | async-done | bytes 3538960 | tf_op jit(solution)/shard_map/reduce_scatter | solution.py:253
  1790.1 234.5 %all-reduce.10.cloned.1.call-done = (bf16[384,1,3072]{2,0,1:T(8,128)(2,1)}, bf16[384,1,3072]{2,0,1:T(8,128)(2,1)}, bf16[768,1,1536]{2,0,1:T(8,128)(2,1)}, bf16[384,4608]{1,0:T(8,128)(2,1)}, bf16[384,1536]{1,0:T(8,128)(2,1)}) async-done(((bf16[384,1,3072]{2,0,1:T(8,128)(2,1)}, bf16[384,1,3072]{2,0,1:T(8,128)(2,1)}, bf16[768,1,1536]{2,0,1:T(8,128)(2,1)}, bf16[384,4608]{1,0:T(8,128)(2,1)}, ...) | async-done | bytes 11796496 | tf_op jit(solution)/shard_map/psum | solution.py:280
  2025.9 9.9 fusion.48
  2035.8 11.9 all-reduce.4
  2047.8 8.9 all-reduce.2
  (210 shorter events, 148.2 us)
Async XLA Ops:
  7.2 264.6 %all-gather.8.cloned.1.call-start = ((), (), s32[]{:S(2)}) async-start(), calls=%async_computation.11 | async-start | bytes 17694720 | tf_op jit(solution)/shard_map/all_gather | solution.py:102
  7.9 353.9 %all-gather.10.cloned.1.call-start = ((), (), s32[]{:S(2)}) async-start(), calls=%async_computation.12 | async-start | bytes 5898240 | tf_op jit(solution)/shard_map/all_gather | solution.py:103
  8.7 535.6 %all-gather.16.cloned.1.call-start = ((), (), s32[]{:S(2)}) async-start(), calls=%async_computation.15 | async-start | bytes 11796480 | tf_op jit(solution)/shard_map/all_gather | solution.py:108
  9.4 702.1 %all-gather.14.cloned.1.call-start = ((), (), s32[]{:S(2)}) async-start(), calls=%async_computation.14 | async-start | bytes 11796480 | tf_op jit(solution)/shard_map/all_gather | solution.py:107
  10.0 867.9 %all-gather.12.cloned.1.call-start = ((), (), s32[]{:S(2)}) async-start(), calls=%async_computation.13 | async-start | bytes 11796480 | tf_op jit(solution)/shard_map/all_gather | solution.py:106
  15.0 83.3 %all-to-all-start.2 = ((bf16[16,10,1536]{2,1,0:T(8,128)(2,1)}), bf16[16,10,1536]{2,1,0:T(8,128)(2,1)S(1)}, u32[]{:S(2)}, u32[]{:S(2)}) async-start(bf16[16,10,1536]{2,1,0:T(8,128)(2,1)} %all_to_all.38), calls=%async_computation.3 | async-start | bytes 1572864 | tf_op jit(solution)/shard_map/all_to_all | solution.py:163
  97.9 183.0 %copy-start.27 = (f32[128]{0:T(128)}, f32[128]{0:T(128)S(1)}, u32[]{:S(2)}) copy-start(f32[128]{0:T(128)S(1)} %add_rsqrt_fusion.1) | copy-start | bytes 1540
  98.3 184.5 %copy-start.21 = (f32[128,64]{1,0:T(8,128)}, f32[128,64]{1,0:T(8,128)S(1)}, u32[]{:S(2)}) copy-start(f32[128,64]{1,0:T(8,128)S(1)} %get-tuple-element.76) | copy-start | bytes 98308
  98.3 184.5 %copy-start.23 = (f32[128,64]{1,0:T(8,128)}, f32[128,64]{1,0:T(8,128)S(1)}, u32[]{:S(2)}) copy-start(f32[128,64]{1,0:T(8,128)S(1)} %get-tuple-element.77) | copy-start | bytes 98308
  365.1 188.3 %copy-start.37 = (f32[128]{0:T(128)}, f32[128]{0:T(128)S(1)}, u32[]{:S(2)}) copy-start(f32[128]{0:T(128)S(1)} %add_rsqrt_fusion) | copy-start | bytes 1540
  367.6 185.8 %all-to-all-start = ((bf16[16,10,1536]{2,1,0:T(8,128)(2,1)}), bf16[16,10,1536]{2,1,0:T(8,128)(2,1)S(1)}, u32[]{:S(2)}, u32[]{:S(2)}) async-start(bf16[16,10,1536]{2,1,0:T(8,128)(2,1)} %all_to_all.32), calls=%async_computation | async-start | bytes 1572864 | tf_op jit(solution)/shard_map/all_to_all | solution.py:162
  371.7 543.1 %reduce-scatter.8.cloned.1.call-start = ((), (), s32[]{:S(2)}) async-start(), calls=%async_computation.16 | async-start | bytes 1474560 | tf_op jit(solution)/shard_map/reduce_scatter | solution.py:178
  556.1 321.8 %copy-start.17 = (bf16[320,1536]{1,0:T(8,128)(2,1)}, bf16[320,1536]{1,0:T(8,128)(2,1)S(1)}, u32[]{:S(2)}) copy-start(bf16[320,1536]{1,0:T(8,128)(2,1)S(1)} %all_gather.31) | copy-start | bytes 2949124
  899.3 23.4 %reduce-scatter.10.cloned.1.call-start = ((), (), s32[]{:S(2)}) async-start(), calls=%async_computation.17 | async-start | bytes 2949120 | tf_op jit(solution)/shard_map/reduce_scatter | solution.py:198
  916.8 23.9 %all-to-all-start.1 = ((bf16[16,10,1536]{2,1,0:T(8,128)(2,1)}), bf16[16,10,1536]{2,1,0:T(8,128)(2,1)S(1)}, u32[]{:S(2)}, u32[]{:S(2)}) async-start(bf16[16,10,1536]{2,1,0:T(8,128)(2,1)} %all_to_all.35), calls=%async_computation.2 | async-start | bytes 1572864 | tf_op jit(solution)/shard_map/all_to_all | solution.py:184
  940.7 23.6 %all-to-all-start.3 = ((bf16[16,10,1536]{2,1,0:T(8,128)(2,1)}), bf16[16,10,1536]{2,1,0:T(8,128)(2,1)S(1)}, u32[]{:S(2)}, u32[]{:S(2)}) async-start(bf16[16,10,1536]{2,1,0:T(8,128)(2,1)} %all_to_all.41), calls=%async_computation.5 | async-start | bytes 1572864 | tf_op jit(solution)/shard_map/all_to_all | solution.py:204
  945.7 110.9 %reduce-scatter.14.cloned.1.call-start = ((), (), s32[]{:S(2)}) async-start(), calls=%async_computation.19 | async-start | bytes 5898240 | tf_op jit(solution)/shard_map/reduce_scatter | solution.py:256
  971.9 248.9 %reduce-scatter.16.cloned.1.call-start = ((), (), s32[]{:S(2)}) async-start(), calls=%async_computation.20 | async-start | bytes 11796480 | tf_op jit(solution)/shard_map/reduce_scatter | solution.py:265
  982.2 402.9 %reduce-scatter.18.cloned.1.call-start = ((), (), s32[]{:S(2)}) async-start(), calls=%async_computation.21 | async-start | bytes 11796480 | tf_op jit(solution)/shard_map/reduce_scatter | solution.py:268
  991.6 558.1 %reduce-scatter.20.cloned.1.call-start = ((), (), s32[]{:S(2)}) async-start(), calls=%async_computation.22 | async-start | bytes 11796480 | tf_op jit(solution)/shard_map/reduce_scatter | solution.py:271
  1001.9 788.1 %reduce-scatter.12.cloned.1.call-start = ((), (), s32[]{:S(2)}) async-start(), calls=%async_computation.18 | async-start | bytes 17694720 | tf_op jit(solution)/shard_map/reduce_scatter | solution.py:253
  1018.5 1006.1 %all-reduce.10.cloned.1.call-start = ((), (), s32[]{:S(2)}) async-start(), calls=%async_computation.23 | async-start | bytes 23592960 | tf_op jit(solution)/shard_map/psum | solution.py:280
  1790.0 234.6 %copy-start.44 = (u32[32]{0:T(128)S(1)}, u32[32]{0:T(128)}, u32[]{:S(2)}) copy-start(u32[32]{0:T(128)} %constant.107) | copy-start | bytes 388
  1790.0 290.9 %all-reduce.12.cloned.1.call-start = ((), (), s32[]{:S(2)}) async-start(), calls=%async_computation.24 | async-start | bytes 9437184 | tf_op jit(solution)/shard_map/psum | solution.py:285
  (40 other events, 729.9 us)
Sparse Core Ops, SparseCore 0:
  9.6 262.1 all-gather.7
  273.4 88.4 all-gather.9
  363.4 180.7 all-gather.15
  545.7 165.7 all-gather.13
  712.9 164.9 all-gather.11
  899.4 6.6 reduce-scatter.7
  914.8 7.8 reduce-scatter.9
  972.0 84.5 reduce-scatter.13
  1059.0 161.8 reduce-scatter.15
  1223.0 162.1 reduce-scatter.17
  1387.5 162.1 reduce-scatter.19
  1551.9 238.0 reduce-scatter.11
  1794.3 230.2 all-reduce.9
  2027.2 29.2 all-reduce.11
where the time goes:
time: 2100 us
  waiting for transfers between devices  1780 us (85%)
  matrix products  120 us (6%)
  blocking collectives  103 us (5%)
  local copies, waits for them, and re-layouts  38 us (2%)
  starting transfers between devices  22.7 us (1%)
    reduce_scatter x1, waiting for transfers between devices, local(): lax.psum_scatter(grad_qkv_w.astype(jnp.bfloat16), 'batch', scatter_dimens...  240 us
    psum x1, waiting for transfers between devices, local(): lax.psum(share_gate.astype(jnp.bfloat16), 'gran').astype(jnp.float32)  235 us
    all_gather x1, waiting for transfers between devices, local(): lax.all_gather(w_down, 'batch', axis=0, tiled=True)  172 us
    all_gather x1, waiting for transfers between devices, local(): lax.all_gather(w_qkv, 'batch', axis=0, tiled=True)  171 us
    reduce_scatter x1, waiting for transfers between devices, local(): lax.psum_scatter(grad_down_w.astype(jnp.bfloat16), 'batch', scatter_dimen...  165 us
    reduce_scatter x1, waiting for transfers between devices, local(): lax.psum_scatter(grad_up_w.astype(jnp.bfloat16), 'batch', scatter_dimensi...  164 us
    reduce_scatter x1, waiting for transfers between devices, local(): lax.psum_scatter(grad_gate_w.astype(jnp.bfloat16), 'batch', scatter_dimen...  164 us
    all_gather x1, waiting for transfers between devices, local(): lax.all_gather(w_gate, 'batch', axis=0, tiled=True)  157 us
  transfers between devices with their start and end apart: 18, of which 14 were waited for; matrix products, arithmetic and copies ran while one was open for 6% of the time, Pallas kernels for 0%

commit v1 on v0

v1 whole, which is shorter than its diff:
```python
import math

import jax
import jax.numpy as jnp
from jax import lax
from jax.sharding import PartitionSpec as P

H = 12


EPSILON = 1e-06
NEG_FILL = -1e30
ROPE_BASE = 10000.0
BF = jnp.bfloat16
F32 = jnp.float32


def seq_positions(seq_rows):
    first_row = jnp.sum((seq_rows[None, :] < seq_rows[:, None]).astype(jnp.int32), axis=1)
    return jnp.arange(seq_rows.shape[0], dtype=jnp.int32) - first_row


def row_limits(seq_rows, seq_groups, kept_rows, half_units):
    labels = jnp.arange(seq_groups.shape[0], dtype=jnp.int32)
    member = (seq_rows[:, None] == labels[None, :]).astype(jnp.int32)
    group_id = jnp.sum(member * seq_groups[None, :], axis=1)
    index = jnp.arange(seq_rows.shape[0], dtype=jnp.int32)
    earlier = (group_id[None, :] == group_id[:, None]) & (index[None, :] < index[:, None])
    rank = jnp.sum(earlier.astype(jnp.int32), axis=1)
    return jnp.where(rank < kept_rows, jnp.right_shift(jnp.int32(half_units), 3 - group_id), 0)


def rotate_half(vectors, cosines, sines):
    half_size = vectors.shape[-1] // 2
    front_half = vectors[..., :half_size]
    back_part = vectors[..., half_size:]
    return jnp.concatenate(
        [front_half * cosines - back_part * sines, back_part * cosines + front_half * sines],
        axis=-1,
    )


def rotate_back(vectors, cosines, sines):
    return rotate_half(vectors, cosines, -sines)


def dot(left, right):
    return jnp.dot(left, right, preferred_element_type=F32)


def contract_rows(left, right):
    return lax.dot_general(left, right, (((0,), (0,)), ((), ())), preferred_element_type=F32)


def contract_cols(left, right):
    return lax.dot_general(left, right, (((1,), (1,)), ((), ())), preferred_element_type=F32)


def norm_back(grad_normed, unit_rows, inverse_rms, gain):
    scaled = grad_normed * gain
    return inverse_rms * (scaled - unit_rows * jnp.mean(scaled * unit_rows, axis=-1, keepdims=True))


def after(value, *others):
    return lax.optimization_barrier((value, *others))[0]


def local(
    tokens,
    seq_ids,
    granularity,
    w_qkv,
    w_out,
    gain_attn,
    gain_ffn,
    w_gate,
    w_up,
    w_down,
    out_cotangent,
):
    n = lax.axis_size("batch")
    g = lax.axis_size("gran")
    z = lax.axis_index("batch")
    p = lax.axis_index("gran")
    c = lax.axis_index("ffn")
    rows, width = tokens.shape
    head = width // H
    heads = H // g
    mine = heads * head
    depth = w_qkv.shape[0]
    units = w_gate.shape[2]
    capacity = max(2, (5 * rows + 4 * n * g - 1) // (4 * n * g))

    def hop(x, r):
        return lax.ppermute(x, "gran", [(i, i ^ r) for i in range(g)])

    def pair(x):
        return lax.ppermute(x, "batch", [(i, i ^ 1) for i in range(n)])

    def core(x):
        return lax.ppermute(x, "ffn", [(0, 1), (1, 0)])

    def ring(x, s):
        return lax.ppermute(x, "batch", [(i, (i + s) % n) for i in range(n)])

    def plane_gather(x):
        half = x.shape[0] // 2
        one, two = hop(x, 1), hop(x, 2)
        three = jnp.concatenate([hop(one[:half], 2), hop(two[half:], 1)], axis=0)
        return jnp.stack([x, one, two, three])

    def plane_reduce(parts):
        got = [parts[0]] + [hop(parts[r], r) for r in range(1, g)]
        return sum(v.astype(F32) for v in got)

    def ring_gather(part_for):
        own = part_for(0)
        out = jnp.zeros((n, *own.shape), own.dtype)
        out = lax.dynamic_update_index_in_dim(out, own, z, 0)
        got = []
        for s in range(1, n):
            got.append(ring(part_for(s % 2), s))
        for s in range(1, n):
            out = lax.dynamic_update_index_in_dim(out, got[s - 1], (z - s) % n, 0)
        return out

    positions = seq_positions(seq_ids)
    limits = row_limits(seq_ids, granularity, capacity * n, units)
    about = jnp.stack([seq_ids, positions, limits], axis=0).astype(F32)
    about = jnp.concatenate([about, jnp.zeros((5, rows), F32)], axis=0)
    about = jnp.concatenate([about, pair(about)], axis=0)
    about = jnp.stack([about] + [hop(about, r) for r in range(1, g)])
    block_ids = about[:, 0].astype(jnp.int32)
    block_positions = about[:, 1]
    block_limits = jnp.stack([about[:, 2], about[:, 10]], axis=1).reshape(2 * g * rows, 1)
    block_limits = block_limits.astype(jnp.int32)

    gains = ring_gather(lambda odd: jnp.stack([gain_attn, gain_ffn]))
    gain_first = gains[:, 0].reshape(width).astype(F32)
    gain_second = gains[:, 1].reshape(width).astype(F32)

    half_depth = depth // 2
    qkv_part = lax.dynamic_slice(
        w_qkv.reshape(depth, 3, g, mine), (c * half_depth, 0, p, 0), (half_depth, 3, 1, mine)
    ).reshape(half_depth, 3 * mine)
    qkv_half = ring_gather(lambda odd: qkv_part)
    qkv_other = core(qkv_half)
    qkv_first = jnp.where(c == 0, qkv_half, qkv_other)
    qkv_second = jnp.where(c == 0, qkv_other, qkv_half)
    my_qkv = jnp.concatenate([qkv_first, qkv_second], axis=1).reshape(width, 3 * mine)

    sub = depth // g
    half_sub = sub // 2
    out_part = lax.dynamic_slice(w_out, (p * sub + c * half_sub, 0), (half_sub, width))
    out_part = after(out_part, qkv_half)
    out_half = ring_gather(lambda odd: out_part).reshape(g, n // g, half_sub, width)

    def for_member(stacked, r):
        return lax.dynamic_index_in_dim(stacked, p ^ r, 0, keepdims=False)

    def by_member(pieces):
        out = jnp.zeros((g, *pieces[0].shape), pieces[0].dtype)
        for r in range(g):
            out = lax.dynamic_update_index_in_dim(out, pieces[r], p ^ r, 0)
        return out

    out_pieces = by_member(
        [for_member(out_half, 0)] + [hop(for_member(out_half, r), r) for r in range(1, g)]
    )
    out_other = core(out_pieces)
    out_first = jnp.where(c == 0, out_pieces, out_other)
    out_second = jnp.where(c == 0, out_other, out_pieces)
    my_out = (
        jnp.stack([out_first, out_second], axis=2)
        .transpose(1, 0, 2, 3, 4)
        .reshape(mine, width)
    )

    shares = 2 * g
    strip = units // n // shares
    share = p * 2 + z % 2

    def columns(w, odd):
        picked = lax.dynamic_index_in_dim(
            w.reshape(depth, n, shares, strip), share ^ odd, 2, keepdims=False
        )
        return picked.reshape(depth, n * strip)

    gate_parts = [columns(w_gate, odd) for odd in (0, 1)]
    up_parts = [columns(w_up, odd) for odd in (0, 1)]
    down_rows = w_down.reshape(shares, strip, width)
    down_parts = [
        lax.dynamic_index_in_dim(down_rows, share ^ odd, 0, keepdims=False) for odd in (0, 1)
    ]
    gate_parts = [after(v, out_half) for v in gate_parts]
    my_gate = ring_gather(lambda odd: gate_parts[odd]).reshape(width, n * strip)
    up_parts = [after(v, my_gate) for v in up_parts]
    my_up = ring_gather(lambda odd: up_parts[odd]).reshape(width, n * strip)
    down_parts = [after(v, my_up) for v in down_parts]
    my_down = ring_gather(lambda odd: down_parts[odd]).reshape(n * strip, width)
    gate_matrix = jnp.concatenate([my_gate, core(my_gate)], axis=1)
    up_matrix = jnp.concatenate([my_up, core(my_up)], axis=1)
    down_matrix = jnp.concatenate([my_down, core(my_down)], axis=0)
    span = n * strip
    index = jnp.arange(2 * span, dtype=jnp.int32) % span
    unit_index = (index // strip) * (strip * shares) + share * strip + index % strip

    residual = tokens.astype(F32)
    inverse_first = lax.rsqrt(jnp.mean(residual * residual, axis=-1, keepdims=True) + EPSILON)
    unit_first = residual * inverse_first
    normed = (unit_first * gain_first).astype(BF)
    all_normed = plane_gather(normed).reshape(g * rows, width)
    packed = dot(all_normed, my_qkv).reshape(g, rows, 3, heads, head)
    frequencies = ROPE_BASE ** (-(2.0 * jnp.arange(head // 2, dtype=F32)) / head)
    angles = block_positions[:, :, None] * frequencies
    cosines = jnp.cos(angles)[:, :, None, :]
    sines = jnp.sin(angles)[:, :, None, :]
    score_scale = 1.0 / math.sqrt(head)
    queries = (rotate_half(packed[:, :, 0], cosines, sines) * score_scale).astype(BF)
    keys_rot = rotate_half(packed[:, :, 1], cosines, sines).astype(BF)
    values = packed[:, :, 2].astype(BF)
    row_index = jnp.arange(rows, dtype=jnp.int32)
    allowed = (block_ids[:, :, None] == block_ids[:, None, :]) & (
        row_index[:, None] >= row_index[None, :]
    )
    scores = jnp.einsum("bqhe,bkhe->bhqk", queries, keys_rot, preferred_element_type=F32)
    scores = jnp.where(allowed[:, None], scores, NEG_FILL)
    top_score = jnp.max(scores, axis=-1, keepdims=True)
    exponent = jnp.exp(scores - top_score)
    probs = exponent / jnp.sum(exponent, axis=-1, keepdims=True)
    prob_weights = probs.astype(BF)
    attended = jnp.einsum("bhqk,bkhe->bqhe", prob_weights, values, preferred_element_type=F32)
    attended = attended.reshape(g * rows, mine).astype(BF)
    partial_attn = dot(attended, my_out).astype(BF).reshape(g, rows, width)
    middle = residual + plane_reduce(partial_attn)
    inverse_second = lax.rsqrt(jnp.mean(middle * middle, axis=-1, keepdims=True) + EPSILON)
    unit_second = middle * inverse_second
    normed_ffn = (unit_second * gain_second).astype(BF)

    def gather_rows(x):
        both = jnp.concatenate([x, pair(x)], axis=0)
        return plane_gather(both).reshape(2 * g * rows, width)

    def reduce_rows(x):
        both = plane_reduce(x.reshape(g, 2 * rows, width))
        return both[:rows] + pair(both[rows:].astype(BF)).astype(F32)

    group_grads = gather_rows(after(out_cotangent, all_normed))
    group_rows = gather_rows(normed_ffn)
    live = unit_index[None, :] < block_limits
    gate_pre = dot(group_rows, gate_matrix)
    lifted = dot(group_rows, up_matrix)
    sigmoid_gate = jax.nn.sigmoid(gate_pre)
    activated = gate_pre * sigmoid_gate
    hidden = jnp.where(live, (activated * lifted).astype(BF), jnp.zeros((), BF))
    grad_hidden = jnp.where(live, contract_cols(group_grads, down_matrix), 0.0)
    grad_gate = (
        grad_hidden * lifted * sigmoid_gate * (1.0 + gate_pre * (1.0 - sigmoid_gate))
    ).astype(BF)
    grad_lifted = (grad_hidden * activated).astype(BF)
    partial_input = (
        contract_cols(grad_gate, gate_matrix) + contract_cols(grad_lifted, up_matrix)
    ).astype(BF)
    grad_normed_ffn = reduce_rows(partial_input).astype(BF).astype(F32)

    def core_sum(left, right, split_left):
        if split_left:
            theirs = contract_rows(left[:, span:], right).astype(BF)
            return (contract_rows(left[:, :span], right) + core(theirs).astype(F32)).astype(BF)
        theirs = contract_rows(left, right[:, span:]).astype(BF)
        return (contract_rows(left, right[:, :span]) + core(theirs).astype(F32)).astype(BF)

    def ring_reduce(parts):
        even = lax.dynamic_index_in_dim(parts, z, 0, keepdims=False).astype(F32)
        odd = 0.0
        for s in range(1, n):
            got = ring(lax.dynamic_index_in_dim(parts, (z + s) % n, 0, keepdims=False), s)
            if s % 2:
                odd = odd + got.astype(F32)
            else:
                even = even + got.astype(F32)
        return even, odd

    def all_shares(parts):
        even, odd = ring_reduce(parts)
        flip = z % 2
        first = jnp.where(flip == 0, even, odd).astype(BF)
        second = jnp.where(flip == 0, odd, even).astype(BF)
        gathered = plane_gather(jnp.stack([first, second]))
        return by_member([gathered[r] for r in range(g)]).reshape(shares, *first.shape)

    def columns_back(pieces):
        return (
            pieces.reshape(shares, depth, n, strip)
            .transpose(1, 2, 0, 3)
            .reshape(depth, units)
            .astype(F32)
        )

    gate_sum = core_sum(group_rows, grad_gate, False).reshape(n, depth, span)
    up_sum = core_sum(group_rows, grad_lifted, False).reshape(n, depth, span)
    down_sum = core_sum(hidden, group_grads, True).reshape(n, strip, width)
    share_gate = columns_back(all_shares(gate_sum))
    share_up = columns_back(all_shares(up_sum))
    share_down = all_shares(down_sum).reshape(units // n, width).astype(F32)

    partial_ffn = dot(hidden, down_matrix).astype(BF)
    branch_ffn = reduce_rows(partial_ffn).astype(BF).astype(F32)
    outputs = (middle + branch_ffn).astype(BF)

    grad_middle = out_cotangent.astype(F32) + norm_back(
        grad_normed_ffn, unit_second, inverse_second, gain_second
    )
    grad_branch = plane_gather(grad_middle.astype(BF)).reshape(g * rows, width)
    out_grad = contract_rows(attended, grad_branch)
    grad_attended = contract_cols(grad_branch, my_out).astype(BF).reshape(g, rows, heads, head)
    grad_probs = jnp.einsum("bqhe,bkhe->bhqk", grad_attended, values, preferred_element_type=F32)
    grad_scores = (
        probs * (grad_probs - jnp.sum(probs * grad_probs, axis=-1, keepdims=True))
    ).astype(BF)
    grad_queries = jnp.einsum(
        "bhqk,bkhe->bqhe", grad_scores, keys_rot, preferred_element_type=F32
    ).astype(BF)
    grad_keys = jnp.einsum(
        "bhqk,bqhe->bkhe", grad_scores, queries, preferred_element_type=F32
    ).astype(BF)
    grad_values = jnp.einsum(
        "bhqk,bqhe->bkhe", prob_weights, grad_attended, preferred_element_type=F32
    ).astype(BF)
    grad_packed = (
        jnp.stack(
            [
                rotate_back(grad_queries.astype(F32) * score_scale, cosines, sines),
                rotate_back(grad_keys.astype(F32), cosines, sines),
                grad_values.astype(F32),
            ],
            axis=2,
        )
        .reshape(g * rows, 3 * mine)
        .astype(BF)
    )
    partial_normed = contract_cols(grad_packed, my_qkv).astype(BF).reshape(g, rows, width)
    grad_normed = plane_reduce(partial_normed)
    input_grad = (
        grad_middle + norm_back(grad_normed, unit_first, inverse_first, gain_first)
    ).astype(BF)

    def my_half(x, which):
        return lax.dynamic_index_in_dim(x, which, 1, keepdims=False)

    qkv_grad = contract_rows(all_normed, grad_packed).astype(BF).reshape(n, 2, half_depth, -1)
    qkv_sum = my_half(qkv_grad, c).astype(F32) + core(my_half(qkv_grad, 1 - c)).astype(F32)
    even, odd = ring_reduce(qkv_sum.astype(BF))
    qkv_all = plane_gather((even + odd).astype(BF))
    qkv_all = by_member([qkv_all[r] for r in range(g)])
    qkv_far = core(qkv_all)
    qkv_both = jnp.stack(
        [jnp.where(c == 0, qkv_all, qkv_far), jnp.where(c == 0, qkv_far, qkv_all)]
    )
    share_qkv = (
        qkv_both.reshape(2, g, half_depth, 3, mine)
        .transpose(0, 2, 3, 1, 4)
        .reshape(depth, 3 * width)
        .astype(F32)
    )

    out_grad = out_grad.astype(BF).reshape(n // g, g, 2, half_sub, width)
    out_mine = lax.dynamic_index_in_dim(out_grad, c, 2, keepdims=False)
    out_theirs = lax.dynamic_index_in_dim(out_grad, 1 - c, 2, keepdims=False)
    out_sum = (out_mine.astype(F32) + core(out_theirs).astype(F32)).astype(BF)

    def member_part(r):
        return lax.dynamic_index_in_dim(out_sum, p ^ r, 1, keepdims=False)

    out_sum = by_member([member_part(0)] + [hop(member_part(r), r) for r in range(1, g)])
    even, odd = ring_reduce(out_sum.reshape(n, half_sub, width))
    out_all = plane_gather((even + odd).astype(BF))
    out_all = by_member([out_all[r] for r in range(g)])
    out_far = core(out_all)
    share_out = (
        jnp.stack(
            [jnp.where(c == 0, out_all, out_far), jnp.where(c == 0, out_far, out_all)], axis=1
        )
        .reshape(depth, width)
        .astype(F32)
    )

    share_gain_attn = jnp.sum(share_qkv * w_qkv.astype(F32), axis=1) / gain_attn.astype(F32)
    ffn_part = jnp.sum(
        share_gate * w_gate[:, 0].astype(F32) + share_up * w_up[:, 0].astype(F32), axis=1
    )
    share_gain_ffn = (ffn_part + core(ffn_part)) / gain_ffn.astype(F32)
    return (
        outputs,
        input_grad,
        share_qkv,
        share_out,
        share_gain_attn,
        share_gain_ffn,
        share_gate[:, None, :],
        share_up[:, None, :],
        share_down[:, None, :],
    )


def solution(mesh):
    in_specs = (
        P(("batch", "gran", "ffn"), None),
        P(("batch", "gran", "ffn")),
        P(("batch", "gran", "ffn")),
        P("batch", None),
        P("batch", None),
        P("batch"),
        P("batch"),
        P("batch", "ffn", None),
        P("batch", "ffn", None),
        P("batch", "ffn", None),
        P(("batch", "gran", "ffn"), None),
    )
    out_specs = (
        P(("batch", "gran", "ffn"), None),
        P(("batch", "gran", "ffn"), None),
        P("batch", None),
        P("batch", None),
        P("batch"),
        P("batch"),
        P("batch", "ffn", None),
        P("batch", "ffn", None),
        P("batch", "ffn", None),
    )
    return jax.shard_map(local, mesh=mesh, in_specs=in_specs, out_specs=out_specs, check_vma=False)
```

time: 2100 us -> 706 us (0.34)
  waiting for transfers between devices: 1780 us -> 293 us
  starting transfers between devices: 22.7 us -> 156 us
  local copies, waits for them, and re-layouts: 38 us -> 149 us
  blocking collectives: 103 us -> 0 us
  matrix products: 120 us -> 48.8 us
  other arithmetic: 20.3 us -> 46.5 us
    reduce_scatter x7 -> x0, waiting for transfers between devices: 773 us -> none  [the longest x1 240 us: local(): lax.psum_scatter(grad_qkv_w.astype(jnp.bfloat16), 'batch', scatter_dimens...]
    all_gather x5 -> x0, waiting for transfers between devices: 732 us -> none  [the longest x1 172 us: local(): lax.all_gather(w_down, 'batch', axis=0, tiled=True)]
    ppermute x0 -> x108, waiting for transfers between devices: none -> 293 us  [the longest x57 166 us: hop(): return lax.ppermute(x, 'gran', [(i, i ^ r) for i in range(g)])]
    psum x2 -> x0, waiting for transfers between devices: 235 us -> none  [the longest x1 235 us: local(): lax.psum(share_gate.astype(jnp.bfloat16), 'gran').astype(jnp.float32)]
    ppermute x0 -> x108, starting transfers between devices: none -> 156 us  [the longest x33 71 us: ring(): return lax.ppermute(x, 'batch', [(i, (i + s) % n) for i in range(n)])]
    all_gather x4 -> x0, blocking collectives: 79.4 us -> none  [the longest x1 55.1 us: local(): lax.all_gather(gain_attn, 'batch', axis=0, tiled=True)]
    all_to_all x4 -> x0, waiting for transfers between devices: 32.4 us -> none  [the longest x1 16.7 us: local(): lax.all_to_all(input_rows.astype(jnp.bfloat16), ('batch', 'gran'), split_...]
    convert_element_type x3 -> x8, local copies, waits for them, and re-layouts: 0.24 us -> 29.5 us  [the longest x2 16.1 us: local(): share_qkv = qkv_both.reshape(2, g, half_depth, 3, mine).transpose(0, 2, 3...]
  transfers between devices with their start and end apart: 18 -> 108, of which waited for: 14 -> 48; matrix products, arithmetic and copies ran while one was open for 6% -> 26% of each run, Pallas kernels for 0% -> 0%
where the time goes in v1:
time: 706 us; the launch traced here: 696 us
  waiting for transfers between devices  293 us (42%)
  starting transfers between devices  156 us (22%)
  local copies, waits for them, and re-layouts  149 us (21%)
  matrix products  48.8 us (7%)
  other arithmetic  46.5 us (7%)
    ppermute x57, waiting for transfers between devices, hop(): return lax.ppermute(x, 'gran', [(i, i ^ r) for i in range(g)])  166 us
    ppermute x33, waiting for transfers between devices, ring(): return lax.ppermute(x, 'batch', [(i, (i + s) % n) for i in range(n)])  101 us
    ppermute x33, starting transfers between devices, ring(): return lax.ppermute(x, 'batch', [(i, (i + s) % n) for i in range(n)])  71 us
    ppermute x57, starting transfers between devices, hop(): return lax.ppermute(x, 'gran', [(i, i ^ r) for i in range(g)])  69.1 us
    unnamed x143, local copies, waits for them, and re-layouts  42.8 us
    ppermute x5, waiting for transfers between devices, pair(): return lax.ppermute(x, 'batch', [(i, i ^ 1) for i in range(n)])  25.9 us
    convert_element_type x2, local copies, waits for them, and re-layouts, local(): share_qkv = qkv_both.reshape(2, g, half_depth, 3, mine).transpose(0, 2, 3...  16.1 us
    ppermute x5, starting transfers between devices, pair(): return lax.ppermute(x, 'batch', [(i, i ^ 1) for i in range(n)])  15.6 us
  transfers between devices with their start and end apart: 108, of which 48 were waited for; matrix products, arithmetic and copies ran while one was open for 26% of the time, Pallas kernels for 0%

profile of v1, /device:TPU:0, one launch (start us, length us, event | category | flops | bytes accessed | tf_op | source)
XLA Modules:
  0.0 696.0 jit_solution(2560313634563493911)
XLA Ops:
  130.1 9.5 %collective-permute-done.35 = bf16[384,384]{1,0:T(8,128)(2,1)S(1)} collective-permute-done((bf16[384,384]{1,0:T(8,128)(2,1)S(1)}, bf16[384,384]{1,0:T(8,128)(2,1)S(1)}, u32[]{:S(2)}, u32[]{:S(2)}) %collective-permute-start.35) | collective-permute-done | bytes 294944 | tf_op jit(solution)/shard_map/ppermute | solution.py:104
  165.7 9.3 %collective-permute-done.24 = bf16[128,1536]{1,0:T(8,128)(2,1)S(1)} collective-permute-done((bf16[128,1536]{1,0:T(8,128)(2,1)S(1)}, bf16[128,1536]{1,0:T(8,128)(2,1)S(1)}, u32[]{:S(2)}, u32[]{:S(2)}) %collective-permute-start.24) | collective-permute-done | bytes 393248 | tf_op jit(solution)/shard_map/ppermute | solution.py:95
  196.3 8.4 %collective-permute-start.25 = (bf16[128,1536]{1,0:T(8,128)(2,1)S(1)}, bf16[128,1536]{1,0:T(8,128)(2,1)S(1)}, u32[]{:S(2)}, u32[]{:S(2)}) collective-permute-start(bf16[128,1536]{1,0:T(8,128)(2,1)S(1)} %multiply_convert_fusion.4), channel_id=1, source_target_pairs={{0,8},{8,0},{16,24},{24,16},{1,9},{9,1},{17,25},{25,17},{2,10},{10... | collective-permute-start | bytes 1179656 | tf_op jit(solution)/shard_map/ppermute | solution.py:98
  204.7 9.1 %collective-permute-done.25 = bf16[128,1536]{1,0:T(8,128)(2,1)S(1)} collective-permute-done((bf16[128,1536]{1,0:T(8,128)(2,1)S(1)}, bf16[128,1536]{1,0:T(8,128)(2,1)S(1)}, u32[]{:S(2)}, u32[]{:S(2)}) %collective-permute-start.25) | collective-permute-done | bytes 393248 | tf_op jit(solution)/shard_map/ppermute | solution.py:98
  220.4 14.0 %collective-permute-done.27 = bf16[256,1536]{1,0:T(8,128)(2,1)S(1)} collective-permute-done((bf16[256,1536]{1,0:T(8,128)(2,1)S(1)}, bf16[256,1536]{1,0:T(8,128)(2,1)S(1)}, u32[]{:S(2)}, u32[]{:S(2)}) %collective-permute-start.27) | collective-permute-done | bytes 786464 | tf_op jit(solution)/shard_map/ppermute | solution.py:95
  281.3 8.5 %collective-permute-done.53 = bf16[256,1536]{1,0:T(8,128)(2,1)S(1)} collective-permute-done((bf16[256,1536]{1,0:T(8,128)(2,1)S(1)}, bf16[256,1536]{1,0:T(8,128)(2,1)S(1)}, u32[]{:S(2)}, u32[]{:S(2)}) %collective-permute-start.53) | collective-permute-done | bytes 786464 | tf_op jit(solution)/shard_map/ppermute | solution.py:95
  292.2 14.5 %collective-permute-done.52 = bf16[256,1536]{1,0:T(8,128)(2,1)S(1)} collective-permute-done((bf16[256,1536]{1,0:T(8,128)(2,1)S(1)}, bf16[256,1536]{1,0:T(8,128)(2,1)S(1)}, u32[]{:S(2)}, u32[]{:S(2)}) %collective-permute-start.52) | collective-permute-done | bytes 786464 | tf_op jit(solution)/shard_map/ppermute | solution.py:95
  307.6 15.9 %collective-permute-done.44 = bf16[256,1536]{1,0:T(8,128)(2,1)S(1)} collective-permute-done((bf16[256,1536]{1,0:T(8,128)(2,1)S(1)}, bf16[256,1536]{1,0:T(8,128)(2,1)S(1)}, u32[]{:S(2)}, u32[]{:S(2)}) %collective-permute-start.44) | collective-permute-done | bytes 786464 | tf_op jit(solution)/shard_map/ppermute | solution.py:95
  323.6 12.7 %collective-permute-done.43 = bf16[256,1536]{1,0:T(8,128)(2,1)S(1)} collective-permute-done((bf16[256,1536]{1,0:T(8,128)(2,1)S(1)}, bf16[256,1536]{1,0:T(8,128)(2,1)S(1)}, u32[]{:S(2)}, u32[]{:S(2)}) %collective-permute-start.43) | collective-permute-done | bytes 786464 | tf_op jit(solution)/shard_map/ppermute | solution.py:95
  338.7 9.5 %collective-permute-done.54 = bf16[128,1536]{1,0:T(8,128)(2,1)S(1)} collective-permute-done((bf16[128,1536]{1,0:T(8,128)(2,1)S(1)}, bf16[128,1536]{1,0:T(8,128)(2,1)S(1)}, u32[]{:S(2)}, u32[]{:S(2)}) %collective-permute-start.54) | collective-permute-done | bytes 393248 | tf_op jit(solution)/shard_map/ppermute | solution.py:98
  394.2 8.0 %collective-permute-done.86 = bf16[384,384]{0,1:T(8,128)(2,1)S(1)} collective-permute-done((bf16[384,384]{0,1:T(8,128)(2,1)}, bf16[384,384]{0,1:T(8,128)(2,1)S(1)}, u32[]{:S(2)}, u32[]{:S(2)}) %collective-permute-start.86) | collective-permute-done | bytes 294944 | tf_op jit(solution)/shard_map/ppermute | solution.py:104
  404.8 12.1 %collective-permute-start.93 = (bf16[384,384]{0,1:T(8,128)(2,1)}, bf16[384,384]{0,1:T(8,128)(2,1)S(1)}, u32[]{:S(2)}, u32[]{:S(2)}) collective-permute-start(bf16[384,384]{0,1:T(8,128)(2,1)} %bitcast.141), channel_id=1, source_target_pairs={{0,8},{8,16},{16,24},{24,0},{1,9},{9,17},{17,25},{25,1},{2,10},{10... | collective-permute-start | bytes 884744 | tf_op jit(solution)/shard_map/ppermute | solution.py:104
  427.2 13.1 %collective-permute-done.92 = bf16[384,384]{0,1:T(8,128)(2,1)S(1)} collective-permute-done((bf16[384,384]{0,1:T(8,128)(2,1)}, bf16[384,384]{0,1:T(8,128)(2,1)S(1)}, u32[]{:S(2)}, u32[]{:S(2)}) %collective-permute-start.92) | collective-permute-done | bytes 294944 | tf_op jit(solution)/shard_map/ppermute | solution.py:104
  448.1 12.2 %collective-permute-done.58 = bf16[64,1536]{1,0:T(8,128)(2,1)S(1)} collective-permute-done((bf16[64,1536]{1,0:T(8,128)(2,1)S(1)}, bf16[64,1536]{1,0:T(8,128)(2,1)S(1)}, u32[]{:S(2)}, u32[]{:S(2)}) %collective-permute-start.58) | collective-permute-done | bytes 196640 | tf_op jit(solution)/shard_map/ppermute | solution.py:95
  501.7 8.7 %collective-permute-done.105 = bf16[2,96,1536]{2,1,0:T(8,128)(2,1)S(1)} collective-permute-done((bf16[2,96,1536]{2,1,0:T(8,128)(2,1)}, bf16[2,96,1536]{2,1,0:T(8,128)(2,1)S(1)}, u32[]{:S(2)}, u32[]{:S(2)}) %collective-permute-start.105) | collective-permute-done | bytes 589856 | tf_op jit(solution)/shard_map/ppermute | solution.py:95
  521.2 8.3 %collective-permute-done.72 = bf16[1,48,1536]{2,1,0:T(8,128)(2,1)S(1)} collective-permute-done((bf16[1,48,1536]{2,1,0:T(8,128)(2,1)S(1)}, bf16[1,48,1536]{2,1,0:T(8,128)(2,1)S(1)}, u32[]{:S(2)}, u32[]{:S(2)}) %collective-permute-start.72) | collective-permute-done | bytes 147488 | tf_op jit(solution)/shard_map/ppermute | solution.py:95
  565.8 15.2 %collective-permute-done.65 = bf16[192,1152]{1,0:T(8,128)(2,1)S(1)} collective-permute-done((bf16[192,1152]{1,0:T(8,128)(2,1)S(1)}, bf16[192,1152]{1,0:T(8,128)(2,1)S(1)}, u32[]{:S(2)}, u32[]{:S(2)}) %collective-permute-start.65) | collective-permute-done | bytes 442400 | tf_op jit(solution)/shard_map/ppermute | solution.py:104
  585.9 13.1 %collective-permute-done.63 = bf16[192,1152]{1,0:T(8,128)(2,1)S(1)} collective-permute-done((bf16[192,1152]{1,0:T(8,128)(2,1)S(1)}, bf16[192,1152]{1,0:T(8,128)(2,1)S(1)}, u32[]{:S(2)}, u32[]{:S(2)}) %collective-permute-start.63) | collective-permute-done | bytes 442400 | tf_op jit(solution)/shard_map/ppermute | solution.py:104
  604.4 10.9 %collective-permute-done.67 = bf16[192,1152]{1,0:T(8,128)(2,1)S(1)} collective-permute-done((bf16[192,1152]{1,0:T(8,128)(2,1)S(1)}, bf16[192,1152]{1,0:T(8,128)(2,1)S(1)}, u32[]{:S(2)}, u32[]{:S(2)}) %collective-permute-start.67) | collective-permute-done | bytes 442400 | tf_op jit(solution)/shard_map/ppermute | solution.py:95
  629.1 11.0 %copy.162 = f32[384,1,3072]{2,1,0:T(1,128)} copy(f32[384,1,3072]{0,2,1:T(8,128)} %bitcast.370) | data formatting | bytes 9437184
  640.2 11.0 %copy.163 = f32[384,1,3072]{2,1,0:T(1,128)} copy(f32[384,1,3072]{0,2,1:T(8,128)} %bitcast.371) | data formatting | bytes 9437184
  651.2 7.4 %reshape.462 = f32[768,1,1536]{2,1,0:T(1,128)} reshape(bf16[4,2,96,1536]{3,2,1,0:T(8,128)(2,1)S(1)} %copy-done.13) | data formatting | bytes 7077888 | tf_op jit(solution)/shard_map/convert_element_type | solution.py:305
  674.2 7.5 %copy.150 = f32[2,192,3,4,384]{4,3,2,1,0:T(4,128)} copy(f32[2,192,3,4,384]{4,2,1,3,0:T(4,128)S(1)} %convert_bitcast_fusion) | data formatting | bytes 14155776 | tf_op jit(solution)/shard_map/convert_element_type | solution.py:364
  681.7 8.6 %reshape.453 = f32[384,4608]{1,0:T(8,128)} reshape(f32[2,192,3,4,384]{4,3,2,1,0:T(4,128)} %copy.150) | data formatting | bytes 14155776 | tf_op jit(solution)/shard_map/convert_element_type | solution.py:364
  (560 shorter events, 434.7 us)
Async XLA Ops:
  10.1 55.2 %collective-permute-start.7 = (bf16[192,1152]{1,0:T(8,128)(2,1)}, bf16[192,1152]{1,0:T(8,128)(2,1)}, u32[]{:S(2)}, u32[]{:S(2)}) collective-permute-start(bf16[192,1152]{1,0:T(8,128)(2,1)} %bitcast.193), channel_id=1, source_target_pairs={{0,8},{8,16},{16,24},{24,0},{1,9},{9,17},{17,25},{25,1},{2,10},{10... | collective-permute-start | bytes 1327112 | tf_op jit(solution)/shard_map/ppermute | solution.py:104
  13.1 53.3 %collective-permute-start.8 = (bf16[192,1152]{1,0:T(8,128)(2,1)}, bf16[192,1152]{1,0:T(8,128)(2,1)}, u32[]{:S(2)}, u32[]{:S(2)}) collective-permute-start(bf16[192,1152]{1,0:T(8,128)(2,1)} %bitcast.193), channel_id=1, source_target_pairs={{0,16},{8,24},{16,0},{24,8},{1,17},{9,25},{17,1},{25,9},{2,18},{10... | collective-permute-start | bytes 1327112 | tf_op jit(solution)/shard_map/ppermute | solution.py:104
  74.6 69.4 %collective-permute-start.10 = (bf16[4,192,1152]{2,1,0:T(8,128)(2,1)S(1)}, bf16[4,192,1152]{2,1,0:T(8,128)(2,1)}, u32[]{:S(2)}, u32[]{:S(2)}) collective-permute-start(bf16[4,192,1152]{2,1,0:T(8,128)(2,1)S(1)} %bitcast_dynamic-update-slice_fusion.12), channel_id=1, source_target_pairs={{0,1},{1,0},{2,3},{3,2},{4,5},{5,4},{6,7},{7,6},{8,9},{9,8},{10,11... | collective-permute-start | bytes 5308424 | tf_op jit(solution)/shard_map/ppermute | solution.py:101
  128.0 89.1 %collective-permute-start.48 = (bf16[256,1536]{1,0:T(8,128)(2,1)}, bf16[256,1536]{1,0:T(8,128)(2,1)}, u32[]{:S(2)}, u32[]{:S(2)}) collective-permute-start(bf16[256,1536]{1,0:T(8,128)(2,1)} %constant_dynamic-update-slice_fusion.12), channel_id=1, source_target_pairs={{0,4},{2,6},{4,0},{6,2},{1,5},{3,7},{5,1},{7,3},{8,12},{10,14},{12... | collective-permute-start | bytes 2359304 | tf_op jit(solution)/shard_map/ppermute | solution.py:95
  139.5 78.7 %collective-permute-start.47 = (bf16[256,1536]{1,0:T(8,128)(2,1)}, bf16[256,1536]{1,0:T(8,128)(2,1)}, u32[]{:S(2)}, u32[]{:S(2)}) collective-permute-start(bf16[256,1536]{1,0:T(8,128)(2,1)} %constant_dynamic-update-slice_fusion.12), channel_id=1, source_target_pairs={{0,2},{2,0},{4,6},{6,4},{1,3},{3,1},{5,7},{7,5},{8,10},{10,8},{12,... | collective-permute-start | bytes 2359304 | tf_op jit(solution)/shard_map/ppermute | solution.py:95
  175.1 40.9 %collective-permute-start.39 = (bf16[96,1536]{1,0:T(8,128)(2,1)S(1)}, bf16[96,1536]{1,0:T(8,128)(2,1)S(1)}, u32[]{:S(2)}, u32[]{:S(2)}) collective-permute-start(bf16[96,1536]{1,0:T(8,128)(2,1)S(1)} %copy-done.38), channel_id=1, source_target_pairs={{0,16},{8,24},{16,0},{24,8},{1,17},{9,25},{17,1},{25,9},{2,18},{10... | collective-permute-start | bytes 884744 | tf_op jit(solution)/shard_map/ppermute | solution.py:104
  269.5 37.3 %collective-permute-start.52 = (bf16[256,1536]{1,0:T(8,128)(2,1)S(1)}, bf16[256,1536]{1,0:T(8,128)(2,1)S(1)}, u32[]{:S(2)}, u32[]{:S(2)}) collective-permute-start(bf16[256,1536]{1,0:T(8,128)(2,1)S(1)} %get-tuple-element.72), channel_id=1, source_target_pairs={{0,4},{2,6},{4,0},{6,2},{1,5},{3,7},{5,1},{7,3},{8,12},{10,14},{12... | collective-permute-start | bytes 2359304 | tf_op jit(solution)/shard_map/ppermute | solution.py:95
  275.1 48.5 %collective-permute-start.44 = (bf16[256,1536]{1,0:T(8,128)(2,1)S(1)}, bf16[256,1536]{1,0:T(8,128)(2,1)S(1)}, u32[]{:S(2)}, u32[]{:S(2)}) collective-permute-start(bf16[256,1536]{1,0:T(8,128)(2,1)S(1)} %get-tuple-element.74), channel_id=1, source_target_pairs={{0,6},{2,4},{4,2},{6,0},{1,7},{3,5},{5,3},{7,1},{8,14},{10,12},{12... | collective-permute-start | bytes 2359304 | tf_op jit(solution)/shard_map/ppermute | solution.py:95
  276.2 60.0 %collective-permute-start.43 = (bf16[256,1536]{1,0:T(8,128)(2,1)S(1)}, bf16[256,1536]{1,0:T(8,128)(2,1)S(1)}, u32[]{:S(2)}, u32[]{:S(2)}) collective-permute-start(bf16[256,1536]{1,0:T(8,128)(2,1)S(1)} %get-tuple-element.75), channel_id=1, source_target_pairs={{0,4},{2,6},{4,0},{6,2},{1,5},{3,7},{5,1},{7,3},{8,12},{10,14},{12... | collective-permute-start | bytes 2359304 | tf_op jit(solution)/shard_map/ppermute | solution.py:95
  289.8 47.2 %collective-permute-start.42 = (bf16[256,1536]{1,0:T(8,128)(2,1)S(1)}, bf16[256,1536]{1,0:T(8,128)(2,1)S(1)}, u32[]{:S(2)}, u32[]{:S(2)}) collective-permute-start(bf16[256,1536]{1,0:T(8,128)(2,1)S(1)} %get-tuple-element.73), channel_id=1, source_target_pairs={{0,2},{2,0},{4,6},{6,4},{1,3},{3,1},{5,7},{7,5},{8,10},{10,8},{12,... | collective-permute-start | bytes 2359304 | tf_op jit(solution)/shard_map/ppermute | solution.py:95
  306.7 58.8 %collective-permute-start.91 = (bf16[1536,384]{1,0:T(8,128)(2,1)S(1)}, bf16[1536,384]{1,0:T(8,128)(2,1)S(1)}, u32[]{:S(2)}, u32[]{:S(2)}) collective-permute-start(bf16[1536,384]{1,0:T(8,128)(2,1)S(1)} %convolution_convert_fusion.6), channel_id=1, source_target_pairs={{0,1},{1,0},{2,3},{3,2},{4,5},{5,4},{6,7},{7,6},{8,9},{9,8},{10,11... | collective-permute-start | bytes 3538952 | tf_op jit(solution)/shard_map/ppermute | solution.py:101
  306.7 60.9 %collective-permute-start.83 = (bf16[1536,384]{1,0:T(8,128)(2,1)S(1)}, bf16[1536,384]{1,0:T(8,128)(2,1)S(1)}, u32[]{:S(2)}, u32[]{:S(2)}) collective-permute-start(bf16[1536,384]{1,0:T(8,128)(2,1)S(1)} %convolution_convert_fusion.7), channel_id=1, source_target_pairs={{0,1},{1,0},{2,3},{3,2},{4,5},{5,4},{6,7},{7,6},{8,9},{9,8},{10,11... | collective-permute-start | bytes 3538952 | tf_op jit(solution)/shard_map/ppermute | solution.py:101
  357.0 86.7 %collective-permute-start.56 = (bf16[128,1536]{1,0:T(8,128)(2,1)}, bf16[128,1536]{1,0:T(8,128)(2,1)}, u32[]{:S(2)}, u32[]{:S(2)}) collective-permute-start(bf16[128,1536]{1,0:T(8,128)(2,1)} %get-tuple-element.58), channel_id=1, source_target_pairs={{0,4},{2,6},{4,0},{6,2},{1,5},{3,7},{5,1},{7,3},{8,12},{10,14},{12... | collective-permute-start | bytes 1179656 | tf_op jit(solution)/shard_map/ppermute | solution.py:95
  357.9 87.8 %collective-permute-start.55 = (bf16[128,1536]{1,0:T(8,128)(2,1)}, bf16[128,1536]{1,0:T(8,128)(2,1)}, u32[]{:S(2)}, u32[]{:S(2)}) collective-permute-start(bf16[128,1536]{1,0:T(8,128)(2,1)} %get-tuple-element.58), channel_id=1, source_target_pairs={{0,2},{2,0},{4,6},{6,4},{1,3},{3,1},{5,7},{7,5},{8,10},{10,8},{12,... | collective-permute-start | bytes 1179656 | tf_op jit(solution)/shard_map/ppermute | solution.py:95
  425.0 61.0 %collective-permute-start.87 = (bf16[2,384,384]{1,2,0:T(8,128)(2,1)}, bf16[2,384,384]{1,2,0:T(8,128)(2,1)}, u32[]{:S(2)}, u32[]{:S(2)}) collective-permute-start(bf16[2,384,384]{1,2,0:T(8,128)(2,1)} %pad_maximum_fusion.18), channel_id=1, source_target_pairs={{0,2},{2,0},{4,6},{6,4},{1,3},{3,1},{5,7},{7,5},{8,10},{10,8},{12,... | collective-permute-start | bytes 1769480 | tf_op jit(solution)/shard_map/ppermute | solution.py:95
  426.1 62.1 %collective-permute-start.88 = (bf16[2,384,384]{1,2,0:T(8,128)(2,1)}, bf16[2,384,384]{1,2,0:T(8,128)(2,1)}, u32[]{:S(2)}, u32[]{:S(2)}) collective-permute-start(bf16[2,384,384]{1,2,0:T(8,128)(2,1)} %pad_maximum_fusion.18), channel_id=1, source_target_pairs={{0,4},{2,6},{4,0},{6,2},{1,5},{3,7},{5,1},{7,3},{8,12},{10,14},{12... | collective-permute-start | bytes 1769480 | tf_op jit(solution)/shard_map/ppermute | solution.py:95
  441.4 49.5 %collective-permute-start.95 = (bf16[2,384,384]{1,2,0:T(8,128)(2,1)}, bf16[2,384,384]{1,2,0:T(8,128)(2,1)}, u32[]{:S(2)}, u32[]{:S(2)}) collective-permute-start(bf16[2,384,384]{1,2,0:T(8,128)(2,1)} %pad_maximum_fusion.19), channel_id=1, source_target_pairs={{0,2},{2,0},{4,6},{6,4},{1,3},{3,1},{5,7},{7,5},{8,10},{10,8},{12,... | collective-permute-start | bytes 1769480 | tf_op jit(solution)/shard_map/ppermute | solution.py:95
  461.4 38.2 %collective-permute-start.104 = (bf16[2,96,1536]{2,1,0:T(8,128)(2,1)}, bf16[2,96,1536]{2,1,0:T(8,128)(2,1)}, u32[]{:S(2)}, u32[]{:S(2)}) collective-permute-start(bf16[2,96,1536]{2,1,0:T(8,128)(2,1)} %pad_maximum_fusion.20), channel_id=1, source_target_pairs={{0,2},{2,0},{4,6},{6,4},{1,3},{3,1},{5,7},{7,5},{8,10},{10,8},{12,... | collective-permute-start | bytes 1769480 | tf_op jit(solution)/shard_map/ppermute | solution.py:95
  499.6 62.7 %collective-permute-start.62 = (bf16[4,192,1152]{2,1,0:T(8,128)(2,1)S(1)}, bf16[4,192,1152]{2,1,0:T(8,128)(2,1)S(1)}, u32[]{:S(2)}, u32[]{:S(2)}) collective-permute-start(bf16[4,192,1152]{2,1,0:T(8,128)(2,1)S(1)} %dynamic-slice_bitcast_fusion), channel_id=1, source_target_pairs={{0,1},{1,0},{2,3},{3,2},{4,5},{5,4},{6,7},{7,6},{8,9},{9,8},{10,11... | collective-permute-start | bytes 5308424 | tf_op jit(solution)/shard_map/ppermute | solution.py:101
  547.5 75.9 %collective-permute-start.107 = (bf16[1,96,1536]{2,1,0:T(8,128)(2,1)S(1)}, bf16[1,96,1536]{2,1,0:T(8,128)(2,1)S(1)}, u32[]{:S(2)}, u32[]{:S(2)}) collective-permute-start(bf16[1,96,1536]{2,1,0:T(8,128)(2,1)S(1)} %slice.319), channel_id=1, source_target_pairs={{0,2},{2,0},{4,6},{6,4},{1,3},{3,1},{5,7},{7,5},{8,10},{10,8},{12,... | collective-permute-start | bytes 884744 | tf_op jit(solution)/shard_map/ppermute | solution.py:95
  561.1 42.0 %collective-permute-start.81 = (bf16[24,1536]{1,0:T(8,128)(2,1)S(1)}, bf16[24,1536]{1,0:T(8,128)(2,1)S(1)}, u32[]{:S(2)}, u32[]{:S(2)}) collective-permute-start(bf16[24,1536]{1,0:T(8,128)(2,1)S(1)} %slice.307), channel_id=1, source_target_pairs={{0,2},{2,0},{4,6},{6,4},{1,3},{3,1},{5,7},{7,5},{8,10},{10,8},{12,... | collective-permute-start | bytes 221192 | tf_op jit(solution)/shard_map/ppermute | solution.py:95
  604.4 54.2 %collective-permute-start.99 = (f32[384]{0:T(512)S(1)}, f32[384]{0:T(512)S(1)}, u32[]{:S(2)}, u32[]{:S(2)}) collective-permute-start(f32[384]{0:T(512)S(1)} %fusion.2), channel_id=1, source_target_pairs={{0,1},{1,0},{2,3},{3,2},{4,5},{5,4},{6,7},{7,6},{8,9},{9,8},{10,11... | collective-permute-start | bytes 4616 | tf_op jit(solution)/shard_map/ppermute | solution.py:101
  621.3 37.8 %collective-permute-start.82 = (bf16[4,48,1536]{2,1,0:T(8,128)(2,1)S(1)}, bf16[4,48,1536]{2,1,0:T(8,128)(2,1)S(1)}, u32[]{:S(2)}, u32[]{:S(2)}) collective-permute-start(bf16[4,48,1536]{2,1,0:T(8,128)(2,1)S(1)} %fusion.77), channel_id=1, source_target_pairs={{0,1},{1,0},{2,3},{3,2},{4,5},{5,4},{6,7},{7,6},{8,9},{9,8},{10,11... | collective-permute-start | bytes 1769480 | tf_op jit(solution)/shard_map/ppermute | solution.py:101
  623.3 37.8 %collective-permute-start.70 = (bf16[4,192,1152]{2,1,0:T(8,128)(2,1)}, bf16[4,192,1152]{2,1,0:T(8,128)(2,1)}, u32[]{:S(2)}, u32[]{:S(2)}) collective-permute-start(bf16[4,192,1152]{2,1,0:T(8,128)(2,1)} %fusion.58), channel_id=1, source_target_pairs={{0,1},{1,0},{2,3},{3,2},{4,5},{5,4},{6,7},{7,6},{8,9},{9,8},{10,11... | collective-permute-start | bytes 5308424 | tf_op jit(solution)/shard_map/ppermute | solution.py:101
  (151 other events, 2031.4 us)

commit v2 on v1

v2 whole, which is shorter than its diff:
```python
import functools
import math

import jax
import jax.numpy as jnp
from jax import lax
from jax.experimental import pallas as pl
from jax.experimental.pallas import tpu as pltpu
from jax.sharding import PartitionSpec as P

H = 12


EPSILON = 1e-06
NEG_FILL = -1e30
ROPE_BASE = 10000.0
BF = jnp.bfloat16
F32 = jnp.float32


def row_groups(seq_rows, seq_groups, kept_rows):
    labels = jnp.arange(seq_groups.shape[0], dtype=jnp.int32)
    member = (seq_rows[:, None] == labels[None, :]).astype(jnp.int32)
    group_id = jnp.sum(member * seq_groups[None, :], axis=1)
    index = jnp.arange(seq_rows.shape[0], dtype=jnp.int32)
    earlier = (group_id[None, :] == group_id[:, None]) & (index[None, :] < index[:, None])
    rank = jnp.sum(earlier.astype(jnp.int32), axis=1)
    return jnp.where(rank < kept_rows, group_id, -1)


def dot(left, right):
    return jnp.dot(left, right, preferred_element_type=F32)


def contract_rows(left, right):
    return lax.dot_general(left, right, (((0,), (0,)), ((), ())), preferred_element_type=F32)


def contract_cols(left, right):
    return lax.dot_general(left, right, (((1,), (1,)), ((), ())), preferred_element_type=F32)


def norm_back(grad_normed, unit_rows, inverse_rms, gain):
    scaled = grad_normed * gain
    return inverse_rms * (scaled - unit_rows * jnp.mean(scaled * unit_rows, axis=-1, keepdims=True))


def first_rows(values, count, width):
    return jnp.pad(values.astype(BF)[None, :], ((0, count - 1), (0, width - values.shape[0])))


def after(value, *others):
    return lax.optimization_barrier((value, *others))[0]


def small_cost():
    return pl.CostEstimate(flops=1, bytes_accessed=1, transcendentals=0)


VMEM_LIMIT = 56 * 1024 * 1024


def call(kernel, outs, scratch=(), ins=(), operands=()):
    kinds = {
        "v": pl.BlockSpec(memory_space=pltpu.VMEM),
        "h": pl.BlockSpec(memory_space=pl.ANY),
        "s": pl.BlockSpec(memory_space=pltpu.SMEM),
    }
    return pl.pallas_call(
        kernel,
        out_shape=[jax.ShapeDtypeStruct(shape, dtype) for shape, dtype in outs],
        in_specs=[kinds[k] for k in ins],
        out_specs=[kinds["v"]] * len(outs),
        scratch_shapes=list(scratch),
        compiler_params=pltpu.CompilerParams(vmem_limit_bytes=VMEM_LIMIT),
        cost_estimate=small_cost(),
    )(*operands)


def split_parts(value, rows, to_one, to_two, own, two_low, one_high):
    half = rows // 2
    to_one[:half] = value[rows : rows + half].astype(BF)
    to_one[half:] = value[3 * rows : 3 * rows + half].astype(BF)
    to_two[:half] = value[2 * rows + half : 3 * rows].astype(BF)
    to_two[half:] = value[3 * rows + half :].astype(BF)
    own[...] = value[:rows]
    two_low[...] = value[2 * rows : 2 * rows + half].astype(BF)
    one_high[...] = value[rows + half : 2 * rows].astype(BF)


def split_shapes(rows, width):
    half = rows // 2
    return [
        ((rows, width), BF),
        ((rows, width), BF),
        ((rows, width), F32),
        ((half, width), BF),
        ((half, width), BF),
    ]


def attend_kernel(n, rows, depth, mine, head, place, freq, *refs):
    tokens, refs = refs[:5], refs[5:]
    here, there, refs = refs[:n], refs[n : 2 * n], refs[2 * n :]
    normed, weight, queries, keys, values, attended, cosines, sines, bias, gains = refs[:10]
    gain_rows, unit_rows, sems = refs[10:]
    z, c = place[0], place[2]
    hd = depth // 2
    width = n * depth
    copies = []
    for s in range(n):
        plane = lax.rem(z - s + n, n)
        for which, pieces in ((c, here), (1 - c, there)):
            start = pl.multiple_of(plane * depth + which * hd, 8)
            for k in range(3):
                copies.append(
                    pltpu.make_async_copy(
                        pieces[s].at[pl.ds(k * hd, hd), :],
                        weight.at[pl.ds(start, hd), pl.ds(k * mine, mine)],
                        sems.at[len(copies)],
                    )
                )
        copies.append(
            pltpu.make_async_copy(
                here[s].at[pl.ds(here[s].shape[0] - 16, 16), :], gain_rows.at[plane], sems.at[len(copies)]
            )
        )
    for copy in copies:
        copy.start()

    half = rows // 2
    third = tokens[3].shape[0]
    spans = [(tokens[0], 0, 0, rows), (tokens[1], 0, rows, rows), (tokens[2], 0, 2 * rows, rows)]
    spans += [(tokens[3], 0, 3 * rows, third), (tokens[4], 0, 3 * rows + third, rows - third)]
    for ref, low, at, count in spans:
        x = ref[low : low + count, :].astype(F32)
        inverse = lax.rsqrt(jnp.mean(x * x, axis=-1, keepdims=True) + EPSILON)
        unit_rows[at : at + count] = x * inverse

    row = lax.broadcasted_iota(jnp.int32, (rows, rows), 0)
    col = lax.broadcasted_iota(jnp.int32, (rows, rows), 1)
    lane = lax.broadcasted_iota(jnp.int32, (rows, head), 1)
    sign = jnp.where(lane < head // 2, -1.0, 1.0)
    for b in range(4):
        ref, low = (tokens[b], rows) if b < 3 else (tokens[4], rows - third)
        ids = ref[low : low + 8, :rows].astype(F32)[:1]
        ids_row = jnp.broadcast_to(ids, (rows, rows))
        ids_col = jnp.sum(jnp.where(row == col, ids_row, 0.0), axis=1, keepdims=True)
        before = jnp.sum(jnp.where(ids_row < ids_col, 1.0, 0.0), axis=1, keepdims=True)
        positions = row[:, :1].astype(F32) - before
        angles = positions * freq[:1, :]
        cosines[b * rows : (b + 1) * rows] = jnp.cos(angles)
        sines[b * rows : (b + 1) * rows] = jnp.sin(angles) * sign
        bias[b * rows : (b + 1) * rows] = jnp.where(
            (ids_row == ids_col) & (row >= col), 0.0, NEG_FILL
        )

    for copy in copies:
        copy.wait()
    for k in range(n):
        block = slice(k * depth, (k + 1) * depth)
        both = gain_rows[k].astype(F32)
        gains[0:8, block] = jnp.broadcast_to(both[0:1, :depth], (8, depth))
        gains[8:16, block] = jnp.broadcast_to(both[8:9, :depth], (8, depth))
    normed[...] = (unit_rows[...] * gains[0:1, :]).astype(BF)
    x = normed[...]
    cos, sin = cosines[...], sines[...]
    scale = 1.0 / math.sqrt(head)
    for k, out in enumerate((queries, keys, values)):
        packed = dot(x, weight[:, k * mine : (k + 1) * mine])
        for h in range(mine // head):
            part = packed[:, h * head : (h + 1) * head]
            if k < 2:
                part = part * cos + pltpu.roll(part, head // 2, 1) * sin
            if k == 0:
                part = part * scale
            out[:, h * head : (h + 1) * head] = part.astype(BF)
    for b in range(4):
        for h in range(mine // head):
            here_rows, here_cols = slice(b * rows, (b + 1) * rows), slice(h * head, (h + 1) * head)
            scores = contract_cols(queries[here_rows, here_cols], keys[here_rows, here_cols])
            probs = softmax(scores + bias[here_rows])
            attended[here_rows, here_cols] = dot(
                probs.astype(BF), values[here_rows, here_cols]
            ).astype(BF)


def softmax(scores):
    exponent = jnp.exp(scores - jnp.max(scores, axis=-1, keepdims=True))
    return exponent / jnp.sum(exponent, axis=-1, keepdims=True)


def project_kernel(rows, attended, out, *parts):
    split_parts(dot(attended[...], out[...]), rows, *parts)


def attend_back_kernel(rows, mine, head, *refs):
    grads, refs = refs[:5], refs[5:]
    out, weight, queries, keys, values, cosines, sines, bias = refs[:8]
    branch, packed, *parts = refs[8:-1]
    attended_grad = refs[-1]
    third = grads[3].shape[0]
    at = 0
    for ref in grads:
        branch[at : at + ref.shape[0]] = ref[...]
        at += ref.shape[0]
    del third
    attended_grad[...] = contract_cols(branch[...], out[...]).astype(BF)
    scale = 1.0 / math.sqrt(head)
    for b in range(4):
        r = slice(b * rows, (b + 1) * rows)
        cos, sin = cosines[r], sines[r]
        for h in range(mine // head):
            cols = slice(h * head, (h + 1) * head)
            q, k, v, grad = queries[r, cols], keys[r, cols], values[r, cols], attended_grad[r, cols]
            probs = softmax(contract_cols(q, k) + bias[r])
            grad_probs = contract_cols(grad, v)
            grad_scores = probs * (
                grad_probs - jnp.sum(probs * grad_probs, axis=-1, keepdims=True)
            )
            grad_scores = grad_scores.astype(BF)
            grad_q = dot(grad_scores, k).astype(BF).astype(F32) * scale
            grad_k = contract_rows(grad_scores, q).astype(BF).astype(F32)
            grad_v = contract_rows(probs.astype(BF), grad)
            for j, part in enumerate((grad_q, grad_k, grad_v)):
                if j < 2:
                    part = part * cos - pltpu.roll(part, head // 2, 1) * sin
                packed[r, j * mine + h * head : j * mine + (h + 1) * head] = part.astype(BF)
    split_parts(contract_cols(packed[...], weight[...]), rows, *parts)


def first_part_kernel(depth, mine, members, place, w_qkv, w_out, gains, out, sems):
    p, c = place[1], place[2]
    hd, hs = depth // 2, depth // members // 2
    width = w_out.shape[1]
    moves = []
    for k in range(3):
        column = pl.multiple_of(k * width + p * mine, 128)
        moves.append((w_qkv.at[pl.ds(c * hd, hd), pl.ds(column, mine)], k * hd, hd))
    top = pl.multiple_of((p * 2 + c) * hs, 8)
    for k in range(width // mine):
        block = w_out.at[pl.ds(top, hs), pl.ds(k * mine, mine)]
        moves.append((block, 3 * hd + k * hs, hs))
    moves.append((gains, out.shape[0] - 16, 16))
    copies = [
        pltpu.make_async_copy(source, out.at[pl.ds(at, count), :], sems.at[i])
        for i, (source, at, count) in enumerate(moves)
    ]
    for copy in copies:
        copy.start()
    for copy in copies:
        copy.wait()


def out_weight_kernel(n, members, hs, mine, place, *refs):
    pieces, out, sems = refs[:members], refs[members], refs[members + 1]
    p = place[1]
    copies = []
    for r in range(members):
        for j in range(n // members):
            for half in range(2):
                top = pl.multiple_of(((j * members + (p ^ r)) * 2 + half) * hs, 8)
                for k in range(out.shape[1] // mine):
                    copies.append(
                        pltpu.make_async_copy(
                            pieces[r].at[j, half, pl.ds(k * hs, hs), :],
                            out.at[pl.ds(top, hs), pl.ds(k * mine, mine)],
                            sems.at[len(copies)],
                        )
                    )
    for copy in copies:
        copy.start()
    for copy in copies:
        copy.wait()


def unit_weights_kernel(n, depth, strip, place, *refs):
    here, there = refs[:n], refs[n : 2 * n]
    gate, up, down, sems = refs[2 * n :]
    z = place[0]
    span = n * strip
    copies = []

    def add(source, target):
        copies.append(pltpu.make_async_copy(source, target, sems.at[len(copies)]))

    for s in range(n):
        plane = lax.rem(z - s + n, n)
        top = pl.multiple_of(plane * depth, 8)
        for half, pieces in enumerate((here, there)):
            columns = pl.ds(half * span, span)
            add(pieces[s].at[pl.ds(0, depth), :], gate.at[pl.ds(top, depth), columns])
            add(pieces[s].at[pl.ds(depth, depth), :], up.at[pl.ds(top, depth), columns])
            start = pl.multiple_of(half * span + plane * strip, 8)
            for k in range(down.shape[1] // span):
                add(
                    pieces[s].at[pl.ds(2 * depth + k * strip, strip), :],
                    down.at[pl.ds(start, strip), pl.ds(k * span, span)],
                )
    for copy in copies:
        copy.start()
    for copy in copies:
        copy.wait()


def strips_of(tile, strip):
    at, out = 0, []
    while at < 128:
        share, first = divmod(tile * 128 + at, strip)
        count = min(strip - first, 128 - at)
        out.append((share, first, at, count))
        at += count
    return out


def unit_results_kernel(n, members, depth, strip, place, *refs):
    pieces, w_gate, w_up = refs[:5], refs[5], refs[6]
    gate, up, down, gain, held, sems = refs[7:]
    shares, span = 2 * members, n * strip
    cuts = (held.shape[1] - 2 * depth) // strip
    z, p = place[0], place[1]
    parts = [(0, depth), (depth, depth), (2 * depth, cuts * strip)]
    copies = []
    for low, count in parts:
        group = []
        for r in range(members):
            for odd in range(2):
                share = (p ^ r) * 2 + (lax.rem(z, 2) ^ odd)
                if r < 3:
                    ref, top = pieces[r], odd * held.shape[1] + low
                else:
                    ref, top = pieces[3 + odd], low
                group.append(
                    pltpu.make_async_copy(
                        ref.at[pl.ds(top, count), :],
                        held.at[share, pl.ds(low, count), :],
                        sems.at[len(copies), r * 2 + odd],
                    )
                )
        for copy in group:
            copy.start()
        copies.append(group)
    lanes = lax.broadcasted_iota(jnp.int32, (depth, 128), 1)
    row_tiles = n * shares * strip // 128
    total = jnp.zeros((depth, 128), F32)
    for which, (out, weight) in enumerate(((gate, w_gate), (up, w_up))):
        for copy in copies[which]:
            copy.wait()
        rows = slice(which * depth, (which + 1) * depth)
        for k in range(n):
            for tile in range(shares * strip // 128):
                made = jnp.zeros((depth, 128), F32)
                for share, first, lane, count in strips_of(tile, strip):
                    column = k * strip + first
                    while count > 0:
                        source, offset = divmod(column, 128)
                        some = min(count, 128 - offset)
                        value = held[share, rows, source * 128 : (source + 1) * 128].astype(F32)
                        if lane != offset:
                            value = pltpu.roll(value, (lane - offset) % 128, 1)
                        made = jnp.where((lanes >= lane) & (lanes < lane + some), value, made)
                        column, lane, count = column + some, lane + some, count - some
                at = k * (shares * strip // 128) + tile
                out[pl.ds(at, depth, stride=row_tiles), :] = made
                total += made * weight[:, at * 128 : (at + 1) * 128].astype(F32)
    gain[...] = jnp.sum(total, axis=1, keepdims=True)
    for copy in copies[2]:
        copy.wait()
    wide = cuts * span // 128
    for share in range(shares):
        for k in range(cuts):
            low = 2 * depth + k * strip
            for tile in range(span // 128):
                value = held[share, low : low + strip, tile * 128 : (tile + 1) * 128].astype(F32)
                start = share * strip * wide + k * (span // 128) + tile
                down[pl.ds(start, strip, stride=wide), :] = value


def attention_results_kernel(members, depth, mine, place, *refs):
    here, there, w_qkv = refs[:5], refs[5:10], refs[10]
    qkv, out, gain, held, held_out, sems = refs[11:]
    p, c = place[1], place[2]
    hd, hs = depth // 2, depth // members // 2
    width = held_out.shape[1]
    blocks = width // mine
    copies = []

    def add(source, target):
        copies.append(pltpu.make_async_copy(source, target, sems.at[len(copies)]))

    def place_rows(ref, first, low, count, r, half):
        for k in range(3):
            top, end = max(low, k * hd), min(low + count, (k + 1) * hd)
            if top < end:
                add(
                    ref.at[pl.ds(first + top - low, end - top), :],
                    held.at[
                        pl.ds(pl.multiple_of(half * hd + top - k * hd, 8), end - top),
                        pl.ds(pl.multiple_of(k * width + (p ^ r) * mine, 128), mine),
                    ],
                )
        for k in range(blocks):
            base = 3 * hd + k * hs
            top, end = max(low, base), min(low + count, base + hs)
            if top < end:
                add(
                    ref.at[pl.ds(first + top - low, end - top), :],
                    held_out.at[
                        pl.ds(pl.multiple_of(((p ^ r) * 2 + half) * hs + top - base, 8), end - top),
                        pl.ds(k * mine, mine),
                    ],
                )

    rows = 3 * hd + blocks * hs
    for half, pieces in ((c, here), (1 - c, there)):
        for r in range(3):
            place_rows(pieces[r], 0, 0, rows, r, half)
        third = pieces[3].shape[0]
        place_rows(pieces[3], 0, 0, third, 3, half)
        place_rows(pieces[4], 0, third, rows - third, 3, half)
    for copy in copies:
        copy.start()
    for copy in copies:
        copy.wait()
    total = jnp.zeros((depth, 128), F32)
    for tile in range(3 * width // 128):
        cols = slice(tile * 128, (tile + 1) * 128)
        value = held[:, cols].astype(F32)
        qkv[:, cols] = value
        total += value * w_qkv[:, cols].astype(F32)
    gain[...] = jnp.sum(total, axis=1, keepdims=True)
    out[...] = held_out[...].astype(F32)


def move(kernel, outs, copies, operands, ins):
    kinds = {"h": pl.BlockSpec(memory_space=pl.ANY), "s": pl.BlockSpec(memory_space=pltpu.SMEM)}
    return pl.pallas_call(
        kernel,
        out_shape=[jax.ShapeDtypeStruct(shape, BF) for shape in outs],
        in_specs=[kinds[k] for k in ins],
        out_specs=[pl.BlockSpec(memory_space=pltpu.VMEM)] * len(outs),
        scratch_shapes=[pltpu.SemaphoreType.DMA((copies,))],
        compiler_params=pltpu.CompilerParams(vmem_limit_bytes=VMEM_LIMIT),
        cost_estimate=small_cost(),
    )(*operands)


def local(
    tokens,
    seq_ids,
    granularity,
    w_qkv,
    w_out,
    gain_attn,
    gain_ffn,
    w_gate,
    w_up,
    w_down,
    out_cotangent,
):
    n = lax.axis_size("batch")
    g = lax.axis_size("gran")
    z = lax.axis_index("batch")
    p = lax.axis_index("gran")
    c = lax.axis_index("ffn")
    rows, width = tokens.shape
    head = width // H
    heads = H // g
    mine = heads * head
    depth = w_qkv.shape[0]
    units = w_gate.shape[2]
    capacity = max(2, (5 * rows + 4 * n * g - 1) // (4 * n * g))

    def hop(x, r):
        return lax.ppermute(x, "gran", [(i, i ^ r) for i in range(g)])

    def pair(x):
        return lax.ppermute(x, "batch", [(i, i ^ 1) for i in range(n)])

    def core(x):
        return lax.ppermute(x, "ffn", [(0, 1), (1, 0)])

    def ring(x, s):
        return lax.ppermute(x, "batch", [(i, (i + s) % n) for i in range(n)])

    def gather_first(x):
        return [x, hop(x, 1), hop(x, 2)]

    def gather_rest(pieces):
        half = pieces[0].shape[0] // 32 * 16 or pieces[0].shape[0] // 2
        return [*pieces, hop(pieces[1][:half], 2), hop(pieces[2][half:], 1)]

    def plane_gather(x):
        return gather_rest(gather_first(x))

    def as_members(pieces):
        return jnp.concatenate(pieces, axis=0).reshape(g, *pieces[0].shape)

    def split_rows(x):
        half = x.shape[1] // 2
        return (
            jnp.concatenate([x[1, :half], x[3, :half]], axis=0),
            jnp.concatenate([x[2, half:], x[3, half:]], axis=0),
            x[0],
            x[2, :half],
            x[1, half:],
        )

    def plane_reduce(to_one, to_two, own, two_low, one_high):
        return plane_reduce_rest(hop(to_one, 1), hop(to_two, 2), own, two_low, one_high)

    def plane_reduce_rest(got_one, got_two, own, two_low, one_high):
        half = two_low.shape[0]
        two_low = (two_low.astype(F32) + got_one[half:].astype(F32)).astype(BF)
        one_high = (one_high.astype(F32) + got_two[half:].astype(F32)).astype(BF)
        low, high = hop(two_low, 2), hop(one_high, 1)
        got = [
            jnp.concatenate([v, w], axis=0).astype(F32)
            for v, w in ((got_one[:half], got_two[:half]), (low, high))
        ]
        return own.astype(F32) + got[0] + got[1]

    def by_member(pieces):
        out = jnp.zeros((g, *pieces[0].shape), pieces[0].dtype)
        for r in range(g):
            out = lax.dynamic_update_index_in_dim(out, pieces[r], p ^ r, 0)
        return out

    def ordered(here, there, axis):
        return jnp.stack(
            [jnp.where(c == 0, here, there), jnp.where(c == 0, there, here)], axis=axis
        )

    def cut(*values):
        return lax.optimization_barrier(values)

    def together(body, *operands):
        made = jax.eval_shape(body, *operands)
        return lax.cond(
            seq_ids[0] >= 0,
            body,
            lambda *given: jax.tree.map(lambda v: jnp.zeros(v.shape, v.dtype), made),
            *operands,
        )

    place = jnp.stack([z, p, c]).astype(jnp.int32)
    hd, sub = depth // 2, depth // g
    hs, blocks = sub // 2, width // mine
    gain_part = jnp.concatenate(
        [first_rows(gain_attn, 8, mine), first_rows(gain_ffn, 8, mine)], axis=0
    )
    token_part = jnp.concatenate([tokens, first_rows(seq_ids, 16, width)], axis=0)
    codes = row_groups(seq_ids, granularity, capacity * n)
    grad_part = jnp.concatenate([out_cotangent, first_rows(codes, 16, width)], axis=0)
    if hs % 8 == 0:
        [first_part] = move(
            functools.partial(first_part_kernel, depth, mine, g),
            [(3 * hd + blocks * hs + 16, mine)],
            blocks + 4,
            (place, w_qkv, w_out, gain_part),
            "shhh",
        )
    else:
        out_part = lax.dynamic_slice(w_out, ((p * 2 + c) * hs, 0), (hs, width))
        first_part = jnp.concatenate(
            [
                lax.dynamic_slice(w_qkv, (c * hd, k * width + p * mine), (hd, mine))
                for k in range(3)
            ]
            + [out_part[:, k * mine : (k + 1) * mine] for k in range(blocks)]
            + [gain_part],
            axis=0,
        )
    first_pieces = [first_part] + [ring(first_part, s) for s in range(1, n)]
    token_pieces = plane_gather(token_part)
    grad_all = lax.all_gather(
        jnp.concatenate([grad_part, pair(grad_part)], axis=0), "gran", axis=0
    )

    shares = 2 * g
    strip = units // n // shares
    share = p * 2 + z % 2
    span = n * strip
    cuts = width // span

    def columns(w, odd):
        return lax.dynamic_index_in_dim(
            w.reshape(depth, n, shares, strip), share ^ odd, 2, keepdims=False
        ).reshape(depth, span)

    def second_part(odd):
        rows_down = lax.dynamic_index_in_dim(
            w_down.reshape(shares, strip, width), share ^ odd, 0, keepdims=False
        )
        return jnp.concatenate(
            [columns(w_gate, odd), columns(w_up, odd)]
            + [rows_down[:, k * span : (k + 1) * span] for k in range(cuts)],
            axis=0,
        )

    even_part, odd_part, *first_pieces = cut(second_part(0), second_part(1), *first_pieces)
    second_here = [even_part] + [
        ring(odd_part if k % 2 else even_part, k) for k in range(1, n)
    ]

    all_rows = g * rows

    def unit(values):
        inverse = lax.rsqrt(jnp.mean(values * values, axis=-1, keepdims=True) + EPSILON)
        return values * inverse, inverse

    def attention(token_pieces, first_pieces):
        first_far = [core(v) for v in first_pieces[:2]]
        first_far += [core(v) for v in cut(*first_pieces[2:], *first_far)[: n - 2]]
        frequencies = ROPE_BASE ** (-(2.0 * jnp.arange(head // 2, dtype=F32)) / head)
        frequencies = jnp.broadcast_to(jnp.concatenate([frequencies, frequencies]), (8, head))
        all_normed, my_qkv, queries, keys, values, attended, cosines, sines, bias, gains = call(
            functools.partial(attend_kernel, n, rows, depth, mine, head),
            [
                ((all_rows, width), BF),
                ((width, 3 * mine), BF),
                ((all_rows, mine), BF),
                ((all_rows, mine), BF),
                ((all_rows, mine), BF),
                ((all_rows, mine), BF),
                ((all_rows, head), F32),
                ((all_rows, head), F32),
                ((all_rows, rows), F32),
                ((16, width), F32),
            ],
            [
                pltpu.VMEM((n, 16, mine), BF),
                pltpu.VMEM((all_rows, width), F32),
                pltpu.SemaphoreType.DMA((7 * n,)),
            ],
            "sv" + "v" * 5 + "h" * (2 * n),
            (place, frequencies, *token_pieces, *first_pieces, *first_far),
        )

        low, high = 3 * hd, 3 * hd + blocks * hs
        out_here = jnp.stack([v[low:high] for v in first_pieces])
        out_there = jnp.stack([v[low:high] for v in first_far])

        def out_part_for(r):
            picked = [
                ordered(*(lax.dynamic_index_in_dim(v, s, 0, keepdims=False) for v in (out_here, out_there)), 0)
                for s in [(z - (p ^ r) * (n // g) - j) % n for j in range(n // g)]
            ]
            return jnp.stack(picked)

        out_pieces = [out_part_for(0)] + [hop(out_part_for(r), r) for r in (1, 2)]
        out_pieces.append(hop(after(out_part_for(3), *out_pieces), 3))
        if hs % 8 == 0:
            [my_out] = move(
                functools.partial(out_weight_kernel, n, g, hs, mine),
                [(mine, width)],
                n * 2 * blocks,
                (place, *out_pieces),
                "s" + "h" * g,
            )
        else:
            my_out = by_member(out_pieces).reshape(g, n // g, 2, blocks, hs, mine)
            my_out = my_out.transpose(1, 0, 2, 4, 3, 5).reshape(mine, width)
        attn_parts = call(
            functools.partial(project_kernel, rows),
            split_shapes(rows, width),
            (),
            "vv",
            (attended, my_out),
        )

        middle = tokens.astype(F32) + plane_reduce(*attn_parts)
        unit_second, inverse_second = unit(middle)
        normed_ffn = (unit_second * gains[8:9]).astype(BF)
        both_rows = plane_gather(jnp.concatenate([normed_ffn, pair(normed_ffn)], axis=0))
        group_rows = jnp.concatenate(both_rows, axis=0)
        kept = (all_normed, my_qkv, my_out, queries, keys, values, attended, cosines, sines, bias)
        return kept, gains, middle, unit_second, inverse_second, group_rows

    kept, gains, middle, unit_second, inverse_second, group_rows = together(
        attention, token_pieces, first_pieces
    )
    all_normed, my_qkv, my_out, queries, keys, values, attended, cosines, sines, bias = kept
    gain_first, gain_second = gains[0:1], gains[8:9]
    residual = tokens.astype(F32)
    group_rows, grad_all, *second_here = cut(group_rows, grad_all, *second_here)
    second_far = [core(v) for v in second_here]

    if strip % 8 == 0:
        gate_matrix, up_matrix, down_matrix = move(
            functools.partial(unit_weights_kernel, n, depth, strip),
            [(width, 2 * span), (width, 2 * span), (2 * span, width)],
            2 * n * (2 + cuts),
            (place, *second_here, *second_far),
            "s" + "h" * (2 * n),
        )
    else:
        stacks = []
        for pieces in (second_here, second_far):
            out = jnp.zeros((n, *pieces[0].shape), BF)
            for s in range(n):
                out = lax.dynamic_update_index_in_dim(out, pieces[s], (z - s) % n, 0)
            stacks.append(out)
        gate_matrix, up_matrix = (
            jnp.concatenate(
                [v[:, k * depth : (k + 1) * depth].reshape(width, span) for v in stacks], axis=1
            )
            for k in (0, 1)
        )
        down_matrix = jnp.concatenate(
            [v[:, 2 * depth :].reshape(n, cuts, strip, span).transpose(0, 2, 1, 3) for v in stacks],
            axis=0,
        ).reshape(2 * span, width)
    grad_got = jnp.stack(
        [lax.dynamic_index_in_dim(grad_all, p ^ r, 0, keepdims=False) for r in range(g)]
    ).reshape(g, 2, rows + 16, width)
    group_grads = grad_got[:, :, :rows].reshape(2 * g * rows, width)
    group_codes = grad_got[:, :, rows, :rows].reshape(2 * g * rows, 1).astype(jnp.int32)
    group_limits = jnp.where(
        group_codes < 0, 0, jnp.right_shift(jnp.int32(units), jnp.minimum(3 - group_codes, 3))
    )
    index = jnp.arange(2 * span, dtype=jnp.int32) % span
    unit_index = (index // strip) * (strip * shares) + share * strip + index % strip
    live = unit_index[None, :] < group_limits
    gate_pre = dot(group_rows, gate_matrix)
    lifted = dot(group_rows, up_matrix)
    sigmoid_gate = jax.nn.sigmoid(gate_pre)
    activated = gate_pre * sigmoid_gate
    hidden = jnp.where(live, (activated * lifted).astype(BF), jnp.zeros((), BF))
    grad_hidden = jnp.where(live, contract_cols(group_grads, down_matrix), 0.0)
    grad_gate = (
        grad_hidden * lifted * sigmoid_gate * (1.0 + gate_pre * (1.0 - sigmoid_gate))
    ).astype(BF)
    grad_lifted = (grad_hidden * activated).astype(BF)
    partial_input = (
        contract_cols(grad_gate, gate_matrix) + contract_cols(grad_lifted, up_matrix)
    ).astype(BF)
    input_parts = split_rows(partial_input.reshape(g, 2 * rows, width))

    def core_sum(left, right, split_left):
        if split_left:
            theirs = contract_rows(left[:, span:], right).astype(BF)
            return (contract_rows(left[:, :span], right) + core(theirs).astype(F32)).astype(BF)
        theirs = contract_rows(left, right[:, span:]).astype(BF)
        return (contract_rows(left, right[:, :span]) + core(theirs).astype(F32)).astype(BF)

    gate_sum = core_sum(group_rows, grad_gate, False).reshape(n, depth, span)
    up_sum = core_sum(group_rows, grad_lifted, False).reshape(n, depth, span)
    down_sum = core_sum(hidden, group_grads, True).reshape(n, strip, cuts, span)

    def unit_sums(k):
        own = lax.dynamic_index_in_dim(down_sum, k, 0, keepdims=False).transpose(1, 0, 2)
        return jnp.concatenate(
            [lax.dynamic_index_in_dim(v, k, 0, keepdims=False) for v in (gate_sum, up_sum)]
            + [own.reshape(cuts * strip, span)],
            axis=0,
        )

    to_one, to_two, *waiting = input_parts
    got_one, got_two = hop(to_one, 1), hop(to_two, 2)
    messages = [unit_sums((z + k) % n) for k in range(n)]
    got_one, got_two, *messages = cut(got_one, got_two, *messages)
    sums = [messages[0].astype(F32), 0.0]
    moved = [ring(messages[k], k) for k in range(1, n)]

    def attention_back(got_one, got_two, waiting):
        halves = plane_reduce_rest(got_one, got_two, *waiting)
        grad_normed_ffn = halves[:rows] + pair(halves[rows:].astype(BF)).astype(F32)
        grad_normed_ffn = grad_normed_ffn.astype(BF).astype(F32)
        grad_middle = out_cotangent.astype(F32) + norm_back(
            grad_normed_ffn, unit_second, inverse_second, gain_second
        )
        branch_pieces = plane_gather(grad_middle.astype(BF))
        return grad_middle, call(
            functools.partial(attend_back_kernel, rows, mine, head),
            [((all_rows, width), BF), ((all_rows, 3 * mine), BF), *split_shapes(rows, width)],
            [pltpu.VMEM((all_rows, mine), BF)],
            "v" * 13,
            (*branch_pieces, my_out, my_qkv, queries, keys, values, cosines, sines, bias),
        )

    grad_middle, (grad_branch, grad_packed, *normed_parts) = together(
        attention_back, got_one, got_two, waiting
    )
    grad_branch, grad_packed, *moved = cut(grad_branch, grad_packed, *moved)
    for k in range(1, n):
        sums[k % 2] += moved[k - 1].astype(F32)
    even_sum, odd_sum = (v.astype(BF) for v in sums)

    partial_ffn = dot(hidden, down_matrix).astype(BF).reshape(g, 2 * rows, width)
    partial_ffn = by_member([partial_ffn[r] for r in range(g)]).reshape(-1, width)
    branch_sum = lax.psum_scatter(
        after(partial_ffn, got_one), "gran", scatter_dimension=0, tiled=True
    )

    def my_half(x, which, axis):
        return lax.dynamic_index_in_dim(x, which, axis, keepdims=False)

    def for_member(stacked, r, axis):
        return lax.dynamic_index_in_dim(stacked, p ^ r, axis, keepdims=False)

    out_grad = contract_rows(attended, grad_branch).astype(BF).reshape(n // g, g, 2, hs, width)
    out_sum = my_half(out_grad, c, 2).astype(F32) + core(my_half(out_grad, 1 - c, 2)).astype(F32)
    out_sum = out_sum.astype(BF)
    out_sum = by_member(
        [for_member(out_sum, 0, 1)]
        + [hop(for_member(out_sum, r, 1), r) for r in range(1, g)]
    ).reshape(n, hs, blocks, mine)
    qkv_grad = contract_rows(all_normed, grad_packed).astype(BF).reshape(n, 2, hd, 3, mine)
    qkv_sum = my_half(qkv_grad, c, 1).astype(F32) + core(my_half(qkv_grad, 1 - c, 1)).astype(F32)
    last_part = jnp.concatenate(
        [
            qkv_sum.astype(BF).transpose(0, 2, 1, 3).reshape(n, 3 * hd, mine),
            out_sum.transpose(0, 2, 1, 3).reshape(n, blocks * hs, mine),
        ],
        axis=1,
    )
    last_parts = [
        lax.dynamic_index_in_dim(last_part, (z + k) % n, 0, keepdims=False) for k in range(n)
    ]
    normed_parts, branch_sum, even_sum, odd_sum, *last_parts = cut(
        normed_parts, branch_sum, even_sum, odd_sum, *last_parts
    )
    last_moved = [ring(last_parts[k], k) for k in range(1, n)]

    def results(normed_parts, branch_sum, even_sum, odd_sum):
        grad_normed = plane_reduce(*normed_parts)
        unit_first, inverse_first = unit(residual)
        input_grad = (
            grad_middle + norm_back(grad_normed, unit_first, inverse_first, gain_first)
        ).astype(BF)
        branch_far = pair(after(branch_sum[rows:], grad_normed))
        branch_ffn = branch_sum[:rows].astype(F32) + branch_far.astype(F32)
        outputs = (middle + branch_ffn).astype(BF)
        unit_pieces = plane_gather(
            after(jnp.concatenate([even_sum, odd_sum], axis=0), branch_far)
        )
        if strip % 32 == 0:
            share_gate, share_up, share_down, ffn_part = call(
                functools.partial(unit_results_kernel, n, g, depth, strip),
                [
                    ((depth * units // 128, 128), F32),
                    ((depth * units // 128, 128), F32),
                    ((units // n * width // 128, 128), F32),
                    ((depth, 1), F32),
                ],
                [
                    pltpu.VMEM((shares, 2 * depth + cuts * strip, span), BF),
                    pltpu.SemaphoreType.DMA((3, shares)),
                ],
                "s" + "h" * 5 + "vv",
                (place, *unit_pieces, w_gate[:, 0], w_up[:, 0]),
            )
            ffn_part = ffn_part[:, 0]
        else:
            got = as_members(unit_pieces).reshape(g, 2, -1, span)
            all_units = jnp.zeros((shares, *got.shape[2:]), BF)
            for r in range(g):
                for odd in (0, 1):
                    all_units = lax.dynamic_update_index_in_dim(
                        all_units, got[r, odd], (p ^ r) * 2 + (z % 2) ^ odd, 0
                    )

            def columns_back(pieces):
                return (
                    pieces.reshape(shares, depth, n, strip)
                    .transpose(1, 2, 0, 3)
                    .reshape(depth, units)
                    .astype(F32)
                )

            share_gate = columns_back(all_units[:, :depth])
            share_up = columns_back(all_units[:, depth : 2 * depth])
            share_down = (
                all_units[:, 2 * depth :]
                .reshape(shares, cuts, strip, span)
                .transpose(0, 2, 1, 3)
                .reshape(units // n, width)
                .astype(F32)
            )
            ffn_part = jnp.sum(
                share_gate * w_gate[:, 0].astype(F32) + share_up * w_up[:, 0].astype(F32), axis=1
            )
        share_gain_ffn = (ffn_part + core(ffn_part)) / gain_ffn.astype(F32)
        return (
            outputs,
            input_grad,
            share_gain_ffn,
            share_gate.reshape(depth, 1, units),
            share_up.reshape(depth, 1, units),
            share_down.reshape(units // n, 1, width),
        )

    outputs, input_grad, share_gain_ffn, share_gate, share_up, share_down = together(
        results, normed_parts, branch_sum, even_sum, odd_sum
    )
    outputs, *last_moved = cut(outputs, *last_moved)
    last_sum = last_parts[0].astype(F32) + sum(v.astype(F32) for v in last_moved)
    last_pieces = plane_gather(last_sum.astype(BF))
    if hs % 16 == 0:
        share_qkv, share_out, attn_part = call(
            functools.partial(attention_results_kernel, g, depth, mine),
            [((depth, 3 * width), F32), ((depth, width), F32), ((depth, 1), F32)],
            [
                pltpu.VMEM((depth, 3 * width), BF),
                pltpu.VMEM((depth, width), BF),
                pltpu.SemaphoreType.DMA((2 * (g + 1) * (3 + blocks),)),
            ],
            "s" + "h" * 10 + "v",
            (place, *last_pieces, *(core(v) for v in last_pieces), w_qkv),
        )
        attn_part = attn_part[:, 0]
    else:
        last_got = as_members(last_pieces)
        last_got = by_member([last_got[r] for r in range(g)])
        last_both = ordered(last_got, core(last_got), 0)
        share_qkv = (
            last_both[:, :, : 3 * hd]
            .reshape(2, g, 3, hd, mine)
            .transpose(0, 3, 2, 1, 4)
            .reshape(depth, 3 * width)
            .astype(F32)
        )
        share_out = (
            last_both[:, :, 3 * hd :]
            .reshape(2, g, blocks, hs, mine)
            .transpose(1, 0, 3, 2, 4)
            .reshape(depth, width)
            .astype(F32)
        )
        attn_part = jnp.sum(share_qkv * w_qkv.astype(F32), axis=1)
    share_gain_attn = attn_part / gain_attn.astype(F32)
    return (
        outputs,
        input_grad,
        share_qkv,
        share_out,
        share_gain_attn,
        share_gain_ffn,
        share_gate,
        share_up,
        share_down,
    )


def solution(mesh):
    in_specs = (
        P(("batch", "gran", "ffn"), None),
        P(("batch", "gran", "ffn")),
        P(("batch", "gran", "ffn")),
        P("batch", None),
        P("batch", None),
        P("batch"),
        P("batch"),
        P("batch", "ffn", None),
        P("batch", "ffn", None),
        P("batch", "ffn", None),
        P(("batch", "gran", "ffn"), None),
    )
    out_specs = (
        P(("batch", "gran", "ffn"), None),
        P(("batch", "gran", "ffn"), None),
        P("batch", None),
        P("batch", None),
        P("batch"),
        P("batch"),
        P("batch", "ffn", None),
        P("batch", "ffn", None),
        P("batch", "ffn", None),
    )
    return jax.shard_map(local, mesh=mesh, in_specs=in_specs, out_specs=out_specs, check_vma=False)
```

time: 706 us -> 619 us (0.88)
  the two profiles are of different devices: /device:TPU:0 before, /device:TPU:27 now
where the time goes in v2:
time: 619 us; the launch traced here: 614 us
  waiting for transfers between devices  280 us (45%)
  starting transfers between devices  75.6 us (12%)
  local copies, waits for them, and re-layouts  69.9 us (11%)
  Pallas kernels  60.2 us (10%)
  other arithmetic  53.1 us (9%)
  matrix products  50.4 us (8%)
  between operations  15.3 us (2%)
  loops' own time  9.11 us (1%)
    ppermute x38, waiting for transfers between devices, hop(): return lax.ppermute(x, 'gran', [(i, i ^ r) for i in range(g)])  157 us
    ppermute x4, waiting for transfers between devices, pair(): return lax.ppermute(x, 'batch', [(i, i ^ 1) for i in range(n)])  85.6 us
    pallas_call x5, Pallas kernels, call(): pl.pallas_call(kernel, out_shape=[jax.ShapeDtypeStruct(shape, dtype) for...  48.5 us
    ppermute x12, waiting for transfers between devices, ring(): return lax.ppermute(x, 'batch', [(i, (i + s) % n) for i in range(n)])  32.2 us
    ppermute x38, starting transfers between devices, hop(): return lax.ppermute(x, 'gran', [(i, i ^ r) for i in range(g)])  31.1 us
    dot_general x8, matrix products, contract_rows(): lax.dot_general(left, right, (((0,), (0,)), ((), ())), preferred_element_...  26.4 us
    ppermute x19, starting transfers between devices, core(): return lax.ppermute(x, 'ffn', [(0, 1), (1, 0)])  23.6 us
    unnamed x100, local copies, waits for them, and re-layouts  19.6 us
  transfers between devices with their start and end apart: 75, of which 35 were waited for; matrix products, arithmetic and copies ran while one was open for 20% of the time, Pallas kernels for 7%

profile of v2, /device:TPU:27, one launch (start us, length us, event | category | flops | bytes accessed | tf_op | source)
XLA Modules:
  0.0 613.7 jit_solution(2953052357891324219)
XLA Ops:
  9.5 10.9 %collective-permute-done.40 = bf16[144,1536]{1,0:T(8,128)(2,1)S(1)} collective-permute-done((bf16[144,1536]{1,0:T(8,128)(2,1)S(1)}, bf16[144,1536]{1,0:T(8,128)(2,1)S(1)}, u32[]{:S(2)}, u32[]{:S(2)}) %collective-permute-start.40) | collective-permute-done | bytes 442400 | tf_op jit(solution)/shard_map/ppermute | solution.py:478
  44.9 32.2 %collective-permute-done.34 = bf16[784,384]{1,0:T(8,128)(2,1)} collective-permute-done((bf16[784,384]{1,0:T(8,128)(2,1)S(1)}, bf16[784,384]{1,0:T(8,128)(2,1)}, u32[]{:S(2)}, u32[]{:S(2)}) %collective-permute-start.34) | collective-permute-done | bytes 602144 | tf_op jit(solution)/shard_map/ppermute | solution.py:484
  83.2 8.9 %collective-permute-done.37 = bf16[144,1536]{1,0:T(8,128)(2,1)S(1)} collective-permute-done((bf16[144,1536]{1,0:T(8,128)(2,1)S(1)}, bf16[144,1536]{1,0:T(8,128)(2,1)S(1)}, u32[]{:S(2)}, u32[]{:S(2)}) %collective-permute-start.37) | collective-permute-done | bytes 442400 | tf_op jit(solution)/shard_map/ppermute | solution.py:475
  98.1 97.0 %conditional.3 = (bf16[512,1536]{1,0:T(8,128)(2,1)}, bf16[1536,1152]{1,0:T(8,128)(2,1)S(1)}, bf16[384,1536]{1,0:T(8,128)(2,1)}, bf16[512,384]{1,0:T(8,128)(2,1)}...) conditional(s32[]{:T(128)} %bitcast.18, () %tuple.47, ...), branch_computations={%region_0.1_spmd, %region_1.3_spmd} | conditional | flops 8651266 | bytes 90142688 | solution.py:539
  114.6 5.9 collective-permute-done.5.refs_2_
  122.6 10.3 %branch_1_fun.5 = (bf16[512,1536]{1,0:T(8,128)(2,1)}, bf16[1536,1152]{1,0:T(8,128)(2,1)S(1)}, bf16[512,384]{1,0:T(8,128)(2,1)}, bf16[512,384]{1,0:T(8,128)(2,1)}...) custom-call(s32[3]{0:T(128)S(1)} %get-tuple-element.100.place, ...), custom_call_target="tpu_custom_call" | custom-call | flops 1 | bytes 1 | tf_op jit(solution)/shard_map/cond/branch_1_fun/pallas_call | solution.py:69
  141.9 8.0 %collective-permute-done.7 = bf16[128,1536]{1,0:T(8,128)(2,1)S(1)} collective-permute-done((bf16[128,1536]{1,0:T(8,128)(2,1)}, bf16[128,1536]{1,0:T(8,128)(2,1)S(1)}, u32[]{:S(2)}, u32[]{:S(2)}) %collective-permute-start.7) | collective-permute-done | bytes 393248 | tf_op jit(solution)/shard_map/cond/branch_1_fun/ppermute | solution.py:475
  162.0 7.1 %collective-permute-done.11 = bf16[128,1536]{1,0:T(8,128)(2,1)S(1)} collective-permute-done((bf16[128,1536]{1,0:T(8,128)(2,1)S(1)}, bf16[128,1536]{1,0:T(8,128)(2,1)S(1)}, u32[]{:S(2)}, u32[]{:S(2)}) %collective-permute-start.11) | collective-permute-done | bytes 393248 | tf_op jit(solution)/shard_map/cond/branch_1_fun/ppermute | solution.py:478
  171.3 12.6 %collective-permute-done.12 = bf16[256,1536]{1,0:T(8,128)(2,1)S(1)} collective-permute-done((bf16[256,1536]{1,0:T(8,128)(2,1)S(1)}, bf16[256,1536]{1,0:T(8,128)(2,1)S(1)}, u32[]{:S(2)}, u32[]{:S(2)}) %collective-permute-start.12) | collective-permute-done | bytes 786464 | tf_op jit(solution)/shard_map/cond/branch_1_fun/ppermute | solution.py:475
  195.1 6.3 %collective-permute-start.44 = (bf16[1152,384]{1,0:T(8,128)(2,1)}, bf16[1152,384]{1,0:T(8,128)(2,1)S(1)}, u32[]{:S(2)}, u32[]{:S(2)}) collective-permute-start(bf16[1152,384]{1,0:T(8,128)(2,1)} %slice_dynamic-update-slice_fusion.4.refs_0_), channel_id=1, source_target_pairs={{0,1},{1,0},{2,3},{3,2},{4,5},{5,4},{6,7},{7,6},{8,9},{9,8},{10,11... | collective-permute-start | bytes 2654216 | tf_op jit(solution)/shard_map/ppermute | solution.py:481
  207.7 6.9 %shard_map.179 = (bf16[1536,768]{1,0:T(8,128)(2,1)}, bf16[1536,768]{1,0:T(8,128)(2,1)}, bf16[768,1536]{1,0:T(8,128)(2,1)}) custom-call(s32[3]{0:T(128)S(1)} %pad_add_fusion.place, bf16[1152,384]{1,0:T(8,128)(2,1)} %slice_dynamic-update-slice_fusion.4.refs_0_, bf16[1152,384]{1,0:T(8,128)(2,1)} %collective-permute-done.41.refs_1_, ...), custom_call_target="tpu_custom_call" | custom-call | flops 1 | bytes 1 | tf_op jit(solution)/shard_map/pallas_call | solution.py:437
  281.9 96.8 %conditional.4 = (f32[128,1536]{1,0:T(8,128)}, bf16[512,1536]{1,0:T(8,128)(2,1)}, bf16[512,1152]{1,0:T(8,128)(2,1)}, bf16[128,1536]{1,0:T(8,128)(2,1)}, bf16[128...) conditional(s32[]{:T(128)} %bitcast.18, () %tuple.46, ...), branch_computations={%region_5.6_spmd, %region_6.8_spmd} | conditional | flops 9437185 | bytes 43306044 | solution.py:539
  288.1 8.3 %collective-permute-done.16 = bf16[128,1536]{1,0:T(8,128)(2,1)S(1)} collective-permute-done((bf16[128,1536]{1,0:T(8,128)(2,1)S(1)}, bf16[128,1536]{1,0:T(8,128)(2,1)S(1)}, u32[]{:S(2)}, u32[]{:S(2)}) %collective-permute-start.16) | collective-permute-done | bytes 393248 | tf_op jit(solution)/shard_map/cond/branch_1_fun/ppermute | solution.py:475
  308.6 37.1 %collective-permute-done.18 = bf16[128,1536]{1,0:T(8,128)(2,1)} collective-permute-done((bf16[128,1536]{1,0:T(8,128)(2,1)}, bf16[128,1536]{1,0:T(8,128)(2,1)}, u32[]{:S(2)}, u32[]{:S(2)}) %collective-permute-start.18) | collective-permute-done | bytes 393248 | tf_op jit(solution)/shard_map/cond/branch_1_fun/ppermute | solution.py:478
  352.4 6.9 %collective-permute-done.19.refs_1_ = bf16[128,1536]{1,0:T(8,128)(2,1)S(1)} collective-permute-done((bf16[128,1536]{1,0:T(8,128)(2,1)S(1)}, bf16[128,1536]{1,0:T(8,128)(2,1)S(1)}, u32[]{:S(2)}, u32[]{:S(2)}) %collective-permute-start.19) | collective-permute-done | bytes 393248 | tf_op jit(solution)/shard_map/cond/branch_1_fun/ppermute | solution.py:475
  366.3 12.3 %branch_1_fun.8 = (bf16[512,1536]{1,0:T(8,128)(2,1)}, bf16[512,1152]{1,0:T(8,128)(2,1)}, bf16[128,1536]{1,0:T(8,128)(2,1)}, bf16[128,1536]{1,0:T(8,128)(2,1)}, f...) custom-call(bf16[128,1536]{1,0:T(8,128)(2,1)} %copy-done.22, bf16[128,1536]{1,0:T(8,128)(2,1)} %copy-done.42, ...), custom_call_target="tpu_custom_call" | custom-call | flops 1 | bytes 1 | tf_op jit(solution)/shard_map/cond/branch_1_fun/pallas_call | solution.py:69
  408.1 6.3 %collective-permute-done.59 = bf16[1,48,1536]{2,1,0:T(8,128)(2,1)S(1)} collective-permute-done((bf16[1,48,1536]{2,1,0:T(8,128)(2,1)S(1)}, bf16[1,48,1536]{2,1,0:T(8,128)(2,1)S(1)}, u32[]{:S(2)}, u32[]{:S(2)}) %collective-permute-start.59) | collective-permute-done | bytes 147488 | tf_op jit(solution)/shard_map/ppermute | solution.py:475
  426.1 137.5 %conditional.5 = (bf16[128,1536]{1,0:T(8,128)(2,1)S(1)}, bf16[128,1536]{1,0:T(8,128)(2,1)}, f32[384]{0:T(512)S(1)}, f32[384,1,3072]{2,1,0:T(1,128)}, f32[384,1,3072]{2,1,0:T(1,128)}, /*index=5*/f32[768,1,1536]{2,1,0:T(1,128)}) conditional(s32[]{:T(128)} %bitcast.18, () %tuple.45, (bf16[256,1536]{1,0:T(8,128)(2,1)}, bf16[128,1536]{1,0:T(8,128)(2,1)}, ...), branch_computations={%region_9.10_spmd, %region_10.13_spmd} | conditional | flops 9831681 | bytes 97168888 | solution.py:539
  453.9 30.4 %collective-permute-done.27 = bf16[128,1536]{1,0:T(8,128)(2,1)S(1)} collective-permute-done((bf16[128,1536]{1,0:T(8,128)(2,1)S(1)}, bf16[128,1536]{1,0:T(8,128)(2,1)S(1)}, u32[]{:S(2)}, u32[]{:S(2)}) %collective-permute-start.27) | collective-permute-done | bytes 393248 | tf_op jit(solution)/shard_map/cond/branch_1_fun/ppermute | solution.py:478
  485.5 38.6 %collective-permute-done.28.refs_1_ = bf16[2304,384]{1,0:T(8,128)(2,1)S(1)} collective-permute-done((bf16[2304,384]{1,0:T(8,128)(2,1)S(1)}, bf16[2304,384]{1,0:T(8,128)(2,1)S(1)}, u32[]{:S(2)}, u32[]{:S(2)}) %collective-permute-start.28) | collective-permute-done | bytes 1769504 | tf_op jit(solution)/shard_map/cond/branch_1_fun/ppermute | solution.py:475
  528.9 15.2 %collective-permute-done.30.refs_3_ = bf16[1152,384]{1,0:T(8,128)(2,1)S(1)} collective-permute-done((bf16[1152,384]{1,0:T(8,128)(2,1)S(1)}, bf16[1152,384]{1,0:T(8,128)(2,1)S(1)}, u32[]{:S(2)}, u32[]{:S(2)}) %collective-permute-start.30) | collective-permute-done | bytes 884768 | tf_op jit(solution)/shard_map/cond/branch_1_fun/ppermute | solution.py:475
  546.3 12.6 %branch_1_fun.9 = (f32[9216,128]{1,0:T(8,128)}, f32[9216,128]{1,0:T(8,128)}, f32[9216,128]{1,0:T(8,128)}, f32[384,1]{1,0:T(8,128)}) custom-call(s32[3]{0:T(128)S(1)} %get-tuple-element.166.place, bf16[2304,384]{1,0:T(8,128)(2,1)} %copy-done.6, bf16[2304,384]{1,0:T(8,128)(2,1)} %copy-done.7, bf16[2304,384]{1,0:T(8,128)(2,1)} %copy-done.8, ...), custom_call_target="tpu_custom_call" | custom-call | flops 1 | bytes 1 | tf_op jit(solution)/shard_map/cond/branch_1_fun/pallas_call | solution.py:69
  568.6 12.7 %collective-permute-done.64.refs_1_ = bf16[768,384]{1,0:T(8,128)(2,1)S(1)} collective-permute-done((bf16[768,384]{1,0:T(8,128)(2,1)S(1)}, bf16[768,384]{1,0:T(8,128)(2,1)S(1)}, u32[]{:S(2)}, u32[]{:S(2)}) %collective-permute-start.64) | collective-permute-done | bytes 589856 | tf_op jit(solution)/shard_map/ppermute | solution.py:475
  595.4 9.7 %shard_map.180 = (f32[384,4608]{1,0:T(8,128)}, f32[384,1536]{1,0:T(8,128)}, f32[384,1]{1,0:T(8,128)}) custom-call(s32[3]{0:T(128)S(1)} %pad_add_fusion.place, bf16[768,384]{1,0:T(8,128)(2,1)} %copy-done.19, bf16[768,384]{1,0:T(8,128)(2,1)} %copy-done.23, bf16[768,384]{1,0:T(8,128)(2,1)} %copy-done.24, bf16[384,384]{1,0:T(8,128)(2,1)} %copy-done.55, ...), custom_call_target="tpu_custom_call" | custom-call | flops 1 | bytes 1 | tf_op jit(solution)/shard_map/pallas_call | solution.py:69
  (459 shorter events, 290.2 us)
Async XLA Ops:
  7.2 187.9 %all-gather.3.cloned.1.call-start = ((), (), s32[]{:S(2)}) async-start(), calls=%async_computation.2 | async-start | bytes 4423680 | tf_op jit(solution)/shard_map/all_gather | solution.py:576
  22.3 398.4 %reduce-scatter.2.cloned.1.call-start = ((), (), s32[]{:S(2)}) async-start(), calls=%async_computation.1 | async-start | bytes 3932160 | tf_op jit(solution)/shard_map/reduce_scatter | solution.py:792
  24.8 20.1 %collective-permute-start.33 = (bf16[784,384]{1,0:T(8,128)(2,1)S(1)}, bf16[784,384]{1,0:T(8,128)(2,1)}, u32[]{:S(2)}, u32[]{:S(2)}) collective-permute-start(bf16[784,384]{1,0:T(8,128)(2,1)S(1)} %shard_map.178), channel_id=1, source_target_pairs={{0,8},{8,16},{16,24},{24,0},{1,9},{9,17},{17,25},{25,1},{2,10},{10... | collective-permute-start | bytes 1806344 | tf_op jit(solution)/shard_map/ppermute | solution.py:484
  24.9 52.2 %collective-permute-start.34 = (bf16[784,384]{1,0:T(8,128)(2,1)S(1)}, bf16[784,384]{1,0:T(8,128)(2,1)}, u32[]{:S(2)}, u32[]{:S(2)}) collective-permute-start(bf16[784,384]{1,0:T(8,128)(2,1)S(1)} %shard_map.178), channel_id=1, source_target_pairs={{0,16},{8,24},{16,0},{24,8},{1,17},{9,25},{17,1},{25,9},{2,18},{10... | collective-permute-start | bytes 1806344 | tf_op jit(solution)/shard_map/ppermute | solution.py:484
  26.2 50.9 %collective-permute-start.35 = (bf16[784,384]{1,0:T(8,128)(2,1)S(1)}, bf16[784,384]{1,0:T(8,128)(2,1)}, u32[]{:S(2)}, u32[]{:S(2)}) collective-permute-start(bf16[784,384]{1,0:T(8,128)(2,1)S(1)} %shard_map.178), channel_id=1, source_target_pairs={{0,24},{8,0},{16,8},{24,16},{1,25},{9,1},{17,9},{25,17},{2,26},{10... | collective-permute-start | bytes 1806344 | tf_op jit(solution)/shard_map/ppermute | solution.py:484
  77.1 118.0 %collective-permute-start.41 = (bf16[1152,384]{1,0:T(8,128)(2,1)}, bf16[1152,384]{1,0:T(8,128)(2,1)}, u32[]{:S(2)}, u32[]{:S(2)}) collective-permute-start(bf16[1152,384]{1,0:T(8,128)(2,1)} %slice_dynamic-update-slice_fusion), channel_id=1, source_target_pairs={{0,8},{8,16},{16,24},{24,0},{1,9},{9,17},{17,25},{25,1},{2,10},{10... | collective-permute-start | bytes 2654216 | tf_op jit(solution)/shard_map/ppermute | solution.py:484
  77.1 118.0 %collective-permute-start.43 = (bf16[1152,384]{1,0:T(8,128)(2,1)}, bf16[1152,384]{1,0:T(8,128)(2,1)}, u32[]{:S(2)}, u32[]{:S(2)}) collective-permute-start(bf16[1152,384]{1,0:T(8,128)(2,1)} %slice_dynamic-update-slice_fusion), channel_id=1, source_target_pairs={{0,24},{8,0},{16,8},{24,16},{1,25},{9,1},{17,9},{25,17},{2,26},{10... | collective-permute-start | bytes 2654216 | tf_op jit(solution)/shard_map/ppermute | solution.py:484
  78.6 116.5 %collective-permute-start.42 = (bf16[1152,384]{1,0:T(8,128)(2,1)}, bf16[1152,384]{1,0:T(8,128)(2,1)}, u32[]{:S(2)}, u32[]{:S(2)}) collective-permute-start(bf16[1152,384]{1,0:T(8,128)(2,1)} %slice_dynamic-update-slice_fusion.4.refs_0_), channel_id=1, source_target_pairs={{0,16},{8,24},{16,0},{24,8},{1,17},{9,25},{17,1},{25,9},{2,18},{10... | collective-permute-start | bytes 2654216 | tf_op jit(solution)/shard_map/ppermute | solution.py:484
  245.2 22.4 %collective-permute-start.52 = (bf16[384,1536]{1,0:T(8,128)(2,1)S(1)}, bf16[384,1536]{1,0:T(8,128)(2,1)S(1)}, u32[]{:S(2)}, u32[]{:S(2)}) collective-permute-start(bf16[384,1536]{1,0:T(8,128)(2,1)S(1)} %convolution_convert_fusion.3), channel_id=1, source_target_pairs={{0,1},{1,0},{2,3},{3,2},{4,5},{5,4},{6,7},{7,6},{8,9},{9,8},{10,11... | collective-permute-start | bytes 3538952 | tf_op jit(solution)/shard_map/ppermute | solution.py:481
  251.8 27.5 %collective-permute-start.49 = (bf16[256,1536]{1,0:T(8,128)(2,1)}, bf16[256,1536]{1,0:T(8,128)(2,1)}, u32[]{:S(2)}, u32[]{:S(2)}) collective-permute-start(bf16[256,1536]{1,0:T(8,128)(2,1)} %pad_maximum_fusion.12), channel_id=1, source_target_pairs={{0,4},{2,6},{4,0},{6,2},{1,5},{3,7},{5,1},{7,3},{8,12},{10,14},{12... | collective-permute-start | bytes 2359304 | tf_op jit(solution)/shard_map/ppermute | solution.py:475
  253.8 25.5 %collective-permute-start.48 = (bf16[256,1536]{1,0:T(8,128)(2,1)}, bf16[256,1536]{1,0:T(8,128)(2,1)}, u32[]{:S(2)}, u32[]{:S(2)}) collective-permute-start(bf16[256,1536]{1,0:T(8,128)(2,1)} %pad_maximum_fusion.11), channel_id=1, source_target_pairs={{0,2},{2,0},{4,6},{6,4},{1,3},{3,1},{5,7},{7,5},{8,10},{10,8},{12,... | collective-permute-start | bytes 2359304 | tf_op jit(solution)/shard_map/ppermute | solution.py:475
  279.3 99.4 %collective-permute-start.53 = (bf16[1152,384]{1,0:T(8,128)(2,1)}, bf16[1152,384]{1,0:T(8,128)(2,1)}, u32[]{:S(2)}, u32[]{:S(2)}) collective-permute-start(bf16[1152,384]{1,0:T(8,128)(2,1)} %pad_maximum_fusion.8), channel_id=1, source_target_pairs={{0,8},{8,16},{16,24},{24,0},{1,9},{9,17},{17,25},{25,1},{2,10},{10... | collective-permute-start | bytes 2654216 | tf_op jit(solution)/shard_map/ppermute | solution.py:484
  280.4 98.4 %collective-permute-start.54 = (bf16[1152,384]{1,0:T(8,128)(2,1)}, bf16[1152,384]{1,0:T(8,128)(2,1)}, u32[]{:S(2)}, u32[]{:S(2)}) collective-permute-start(bf16[1152,384]{1,0:T(8,128)(2,1)} %pad_maximum_fusion.9), channel_id=1, source_target_pairs={{0,16},{8,24},{16,0},{24,8},{1,17},{9,25},{17,1},{25,9},{2,18},{10... | collective-permute-start | bytes 2654216 | tf_op jit(solution)/shard_map/ppermute | solution.py:484
  280.6 98.2 %collective-permute-start.55 = (bf16[1152,384]{1,0:T(8,128)(2,1)}, bf16[1152,384]{1,0:T(8,128)(2,1)}, u32[]{:S(2)}, u32[]{:S(2)}) collective-permute-start(bf16[1152,384]{1,0:T(8,128)(2,1)} %pad_maximum_fusion.10), channel_id=1, source_target_pairs={{0,24},{8,0},{16,8},{24,16},{1,25},{9,1},{17,9},{25,17},{2,26},{10... | collective-permute-start | bytes 2654216 | tf_op jit(solution)/shard_map/ppermute | solution.py:484
  303.5 42.2 %collective-permute-start.18 = (bf16[128,1536]{1,0:T(8,128)(2,1)}, bf16[128,1536]{1,0:T(8,128)(2,1)}, u32[]{:S(2)}, u32[]{:S(2)}) collective-permute-start(bf16[128,1536]{1,0:T(8,128)(2,1)} %slice.366), channel_id=1, source_target_pairs={{0,8},{8,0},{16,24},{24,16},{1,9},{9,1},{17,25},{25,17},{2,10},{10... | collective-permute-start | bytes 1179656 | tf_op jit(solution)/shard_map/cond/branch_1_fun/ppermute | solution.py:478
  420.7 142.9 %collective-permute-start.61 = (bf16[768,384]{1,0:T(8,128)(2,1)}, bf16[768,384]{1,0:T(8,128)(2,1)}, u32[]{:S(2)}, u32[]{:S(2)}) collective-permute-start(bf16[768,384]{1,0:T(8,128)(2,1)} %get-tuple-element.322), channel_id=1, source_target_pairs={{0,8},{8,16},{16,24},{24,0},{1,9},{9,17},{17,25},{25,1},{2,10},{10... | collective-permute-start | bytes 1769480 | tf_op jit(solution)/shard_map/ppermute | solution.py:484
  425.7 137.9 %collective-permute-start.62 = (bf16[768,384]{1,0:T(8,128)(2,1)}, bf16[768,384]{1,0:T(8,128)(2,1)}, u32[]{:S(2)}, u32[]{:S(2)}) collective-permute-start(bf16[768,384]{1,0:T(8,128)(2,1)} %get-tuple-element.323), channel_id=1, source_target_pairs={{0,16},{8,24},{16,0},{24,8},{1,17},{9,25},{17,1},{25,9},{2,18},{10... | collective-permute-start | bytes 1769480 | tf_op jit(solution)/shard_map/ppermute | solution.py:484
  425.8 137.9 %collective-permute-start.63 = (bf16[768,384]{1,0:T(8,128)(2,1)}, bf16[768,384]{1,0:T(8,128)(2,1)}, u32[]{:S(2)}, u32[]{:S(2)}) collective-permute-start(bf16[768,384]{1,0:T(8,128)(2,1)} %get-tuple-element.324), channel_id=1, source_target_pairs={{0,24},{8,0},{16,8},{24,16},{1,25},{9,1},{17,9},{25,17},{2,26},{10... | collective-permute-start | bytes 1769480 | tf_op jit(solution)/shard_map/ppermute | solution.py:484
  451.5 32.9 %collective-permute-start.27 = (bf16[128,1536]{1,0:T(8,128)(2,1)S(1)}, bf16[128,1536]{1,0:T(8,128)(2,1)S(1)}, u32[]{:S(2)}, u32[]{:S(2)}) collective-permute-start(bf16[128,1536]{1,0:T(8,128)(2,1)S(1)} %copy-done.52), channel_id=1, source_target_pairs={{0,8},{8,0},{16,24},{24,16},{1,9},{9,1},{17,25},{25,17},{2,10},{10... | collective-permute-start | bytes 1179656 | tf_op jit(solution)/shard_map/cond/branch_1_fun/ppermute | solution.py:478
  484.4 39.7 %collective-permute-start.28 = (bf16[2304,384]{1,0:T(8,128)(2,1)S(1)}, bf16[2304,384]{1,0:T(8,128)(2,1)S(1)}, u32[]{:S(2)}, u32[]{:S(2)}) collective-permute-start(bf16[2304,384]{1,0:T(8,128)(2,1)S(1)} %pad_maximum_fusion.4.refs_0_), channel_id=1, source_target_pairs={{0,2},{2,0},{4,6},{6,4},{1,3},{3,1},{5,7},{7,5},{8,10},{10,8},{12,... | collective-permute-start | bytes 5308424 | tf_op jit(solution)/shard_map/cond/branch_1_fun/ppermute | solution.py:475
  484.5 39.7 %collective-permute-start.29 = (bf16[2304,384]{1,0:T(8,128)(2,1)S(1)}, bf16[2304,384]{1,0:T(8,128)(2,1)S(1)}, u32[]{:S(2)}, u32[]{:S(2)}) collective-permute-start(bf16[2304,384]{1,0:T(8,128)(2,1)S(1)} %pad_maximum_fusion.4.refs_0_), channel_id=1, source_target_pairs={{0,4},{2,6},{4,0},{6,2},{1,5},{3,7},{5,1},{7,3},{8,12},{10,14},{12... | collective-permute-start | bytes 5308424 | tf_op jit(solution)/shard_map/cond/branch_1_fun/ppermute | solution.py:475
  524.1 19.9 %collective-permute-start.30 = (bf16[1152,384]{1,0:T(8,128)(2,1)S(1)}, bf16[1152,384]{1,0:T(8,128)(2,1)S(1)}, u32[]{:S(2)}, u32[]{:S(2)}) collective-permute-start(bf16[1152,384]{1,0:T(8,128)(2,1)S(1)} %slice.269), channel_id=1, source_target_pairs={{0,4},{2,6},{4,0},{6,2},{1,5},{3,7},{5,1},{7,3},{8,12},{10,14},{12... | collective-permute-start | bytes 2654216 | tf_op jit(solution)/shard_map/cond/branch_1_fun/ppermute | solution.py:475
  525.6 19.9 %collective-permute-start.31 = (bf16[1152,384]{1,0:T(8,128)(2,1)S(1)}, bf16[1152,384]{1,0:T(8,128)(2,1)S(1)}, u32[]{:S(2)}, u32[]{:S(2)}) collective-permute-start(bf16[1152,384]{1,0:T(8,128)(2,1)S(1)} %slice.270), channel_id=1, source_target_pairs={{0,2},{2,0},{4,6},{6,4},{1,3},{3,1},{5,7},{7,5},{8,10},{10,8},{12,... | collective-permute-start | bytes 2654216 | tf_op jit(solution)/shard_map/cond/branch_1_fun/ppermute | solution.py:475
  568.0 24.4 %collective-permute-start.68 = (bf16[768,384]{1,0:T(8,128)(2,1)S(1)}, bf16[768,384]{1,0:T(8,128)(2,1)S(1)}, u32[]{:S(2)}, u32[]{:S(2)}) collective-permute-start(bf16[768,384]{1,0:T(8,128)(2,1)S(1)} %add_convert_fusion.10.refs_0_), channel_id=1, source_target_pairs={{0,1},{1,0},{2,3},{3,2},{4,5},{5,4},{6,7},{7,6},{8,9},{9,8},{10,11... | collective-permute-start | bytes 1769480 | tf_op jit(solution)/shard_map/ppermute | solution.py:481
  (133 other events, 1139.7 us)
Sparse Core Ops, SparseCore 0:
  22.4 49.0 all-gather.2
  279.5 51.5 reduce-scatter.1

commit v3 on v2

--- a/solution.py
+++ b/solution.py
@@ -57,10 +57,11 @@
     return pl.CostEstimate(flops=1, bytes_accessed=1, transcendentals=0)
 
 
-VMEM_LIMIT = 56 * 1024 * 1024
-
-
-def call(kernel, outs, scratch=(), ins=(), operands=()):
+def call(kernel, outs, scratch=(), ins=(), operands=(), out="v", spare=8):
+    held = [v for k, v in zip(ins, operands) if k == "v"]
+    held += [jax.ShapeDtypeStruct(*v) for v in outs if out == "v"]
+    held += [v for v in scratch if v.dtype in (BF, F32)]
+    limit = sum(math.prod(v.shape) * v.dtype.itemsize for v in held) + spare * 2**20
     kinds = {
         "v": pl.BlockSpec(memory_space=pltpu.VMEM),
         "h": pl.BlockSpec(memory_space=pl.ANY),
@@ -70,9 +71,9 @@
         kernel,
         out_shape=[jax.ShapeDtypeStruct(shape, dtype) for shape, dtype in outs],
         in_specs=[kinds[k] for k in ins],
-        out_specs=[kinds["v"]] * len(outs),
+        out_specs=[kinds[out]] * len(outs),
         scratch_shapes=list(scratch),
-        compiler_params=pltpu.CompilerParams(vmem_limit_bytes=VMEM_LIMIT),
+        compiler_params=pltpu.CompilerParams(vmem_limit_bytes=limit),
         cost_estimate=small_cost(),
     )(*operands)
 
@@ -268,35 +269,6 @@
                             sems.at[len(copies)],
                         )
                     )
-    for copy in copies:
-        copy.start()
-    for copy in copies:
-        copy.wait()
-
-
-def unit_weights_kernel(n, depth, strip, place, *refs):
-    here, there = refs[:n], refs[n : 2 * n]
-    gate, up, down, sems = refs[2 * n :]
-    z = place[0]
-    span = n * strip
-    copies = []
-
-    def add(source, target):
-        copies.append(pltpu.make_async_copy(source, target, sems.at[len(copies)]))
-
-    for s in range(n):
-        plane = lax.rem(z - s + n, n)
-        top = pl.multiple_of(plane * depth, 8)
-        for half, pieces in enumerate((here, there)):
-            columns = pl.ds(half * span, span)
-            add(pieces[s].at[pl.ds(0, depth), :], gate.at[pl.ds(top, depth), columns])
-            add(pieces[s].at[pl.ds(depth, depth), :], up.at[pl.ds(top, depth), columns])
-            start = pl.multiple_of(half * span + plane * strip, 8)
-            for k in range(down.shape[1] // span):
-                add(
-                    pieces[s].at[pl.ds(2 * depth + k * strip, strip), :],
-                    down.at[pl.ds(start, strip), pl.ds(k * span, span)],
-                )
     for copy in copies:
         copy.start()
     for copy in copies:
@@ -432,6 +404,152 @@
     out[...] = held_out[...].astype(F32)
 
 
+def out_sums_kernel(members, hs, mine, place, attended, branch, mine_out, theirs_out, held):
+    c = place[2]
+    for k in range(branch.shape[1] // mine):
+        cols = slice(k * mine, (k + 1) * mine)
+        held[...] = contract_rows(attended[...], branch[:, cols])
+        for out, half in ((mine_out, c), (theirs_out, 1 - c)):
+            for quarter in range(members):
+                start = pl.multiple_of((quarter * 2 + half) * hs, 8)
+                value = held[pl.ds(start, hs), :]
+                out[quarter, k * hs : (k + 1) * hs, :] = value.astype(BF)
+
+
+def weight_sums_kernel(members, depth, mine, place, normed, packed, mine_out, theirs_out, held):
+    c = place[2]
+    hd = depth // 2
+    for plane in range(members):
+        block = slice(plane * depth, (plane + 1) * depth)
+        held[...] = contract_rows(normed[:, block], packed[...])
+        for out, half in ((mine_out, c), (theirs_out, 1 - c)):
+            start = pl.multiple_of(half * hd, 8)
+            for k in range(3):
+                value = held[pl.ds(start, hd), k * mine : (k + 1) * mine]
+                out[plane, k * hd : (k + 1) * hd, :] = value.astype(BF)
+
+
+def last_parts_kernel(members, low, place, *refs):
+    sums, quarters, outs, held = refs[0], refs[1 : members + 1], refs[members + 1 : -1], refs[-1]
+    z, p = place[0], place[1]
+    for r in range(members):
+        held[r] = quarters[r][...]
+    for k in range(members):
+        plane = lax.rem(z + k, members)
+        outs[k][:low] = sums[plane]
+        outs[k][low:] = held[p ^ plane]
+
+
+def feed_forward_kernel(n, members, depth, strip, rows, place, unit_index, *refs):
+    pieces, grad_all, refs = refs[:5], refs[5], refs[6:]
+    here, there, refs = refs[:n], refs[n : 2 * n], refs[2 * n :]
+    outs, scratch = refs[:15], refs[15:]
+    x, cot, hidden, grad_gate, grad_lifted, *splits = scratch[:15]
+    gate, up, down, codes, in_sems, out_sems = scratch[15:]
+    z, p = place[0], place[1]
+    span = n * strip
+    units = span * 2 * members
+    size = 2 * rows
+    started, finishing = [], []
+
+    def fetch(source, target):
+        copy = pltpu.make_async_copy(source, target, in_sems.at[len(started)])
+        copy.start()
+        started.append(copy)
+
+    def flush(index, low, count):
+        copy = pltpu.make_async_copy(
+            scratch[index].at[pl.ds(low, count), :],
+            outs[index].at[pl.ds(low, count), :],
+            out_sems.at[len(finishing)],
+        )
+        copy.start()
+        finishing.append(copy)
+
+    at = 0
+    for ref in pieces:
+        fetch(ref, x.at[pl.ds(at, ref.shape[0]), :])
+        at += ref.shape[0]
+    for s in range(n):
+        plane = lax.rem(z - s + n, n)
+        top = pl.multiple_of(plane * depth, 8)
+        for half, parts in enumerate((here, there)):
+            columns = pl.ds(half * span, span)
+            fetch(parts[s].at[pl.ds(0, depth), :], gate.at[pl.ds(top, depth), columns])
+            fetch(parts[s].at[pl.ds(depth, depth), :], up.at[pl.ds(top, depth), columns])
+    first = len(started)
+    for r in range(members):
+        for e in range(2):
+            block = 2 * r + e
+            low = e * (rows + 16)
+            fetch(grad_all.at[p ^ r, pl.ds(low, rows), :], cot.at[pl.ds(block * rows, rows), :])
+            fetch(grad_all.at[p ^ r, pl.ds(low + rows, 16), pl.ds(0, rows)], codes.at[block])
+    for s in range(n):
+        plane = lax.rem(z - s + n, n)
+        for half, parts in enumerate((here, there)):
+            start = pl.multiple_of(half * span + plane * strip, 8)
+            for j in range(down.shape[1] // span):
+                fetch(
+                    parts[s].at[pl.ds(2 * depth + j * strip, strip), :],
+                    down.at[pl.ds(start, strip), pl.ds(j * span, span)],
+                )
+    for copy in started[:first]:
+        copy.wait()
+    flush(0, 0, x.shape[0])
+    row = lax.broadcasted_iota(jnp.int32, (rows, rows), 0)
+    col = lax.broadcasted_iota(jnp.int32, (rows, rows), 1)
+
+    def store(value, r, parts):
+        to_one, to_two, own, two_low, one_high = parts
+        low, high = value[:rows].astype(BF), value[rows:].astype(BF)
+        if r == 0:
+            own[...] = value
+        elif r == 1:
+            to_one[:rows], one_high[...] = low, high
+        elif r == 2:
+            two_low[...], to_two[:rows] = low, high
+        else:
+            to_one[rows:], to_two[rows:] = low, high
+
+    for chunk in range(2):
+        block = slice(chunk * 2 * size, (chunk + 1) * 2 * size)
+        gate_pre = dot(x[block], gate[...])
+        lifted = dot(x[block], up[...])
+        sigmoid = jax.nn.sigmoid(gate_pre)
+        activated = gate_pre * sigmoid
+        if chunk == 0:
+            for copy in started[first:]:
+                copy.wait()
+            flush(1, 0, cot.shape[0])
+        limits = []
+        for b in range(4 * chunk, 4 * chunk + 4):
+            line = jnp.broadcast_to(codes[b].astype(F32)[:1], (rows, rows))
+            code = jnp.sum(jnp.where(row == col, line, 0.0), axis=1, keepdims=True)
+            limits.append(
+                sum(jnp.where(code == k, float(units >> (members - 1 - k)), 0.0) for k in range(members))
+            )
+        live = unit_index[:1, :] < jnp.concatenate(limits, axis=0)
+        hidden[block] = jnp.where(live, activated * lifted, 0.0).astype(BF)
+        grad_hidden = jnp.where(live, contract_cols(cot[block], down[...]), 0.0)
+        grad_gate[block] = (
+            grad_hidden * lifted * sigmoid * (1.0 + gate_pre * (1.0 - sigmoid))
+        ).astype(BF)
+        grad_lifted[block] = (grad_hidden * activated).astype(BF)
+        for index in (2, 3, 4):
+            flush(index, chunk * 2 * size, 2 * size)
+        grads = contract_cols(grad_gate[block], gate[...])
+        grads += contract_cols(grad_lifted[block], up[...])
+        for i in range(2):
+            store(grads[i * size : (i + 1) * size], 2 * chunk + i, splits[:5])
+        value = dot(hidden[block], down[...])
+        for i in range(2):
+            store(value[i * size : (i + 1) * size], 2 * chunk + i, splits[5:])
+    for index in range(5, 15):
+        flush(index, 0, scratch[index].shape[0])
+    for copy in finishing:
+        copy.wait()
+
+
 def move(kernel, outs, copies, operands, ins):
     kinds = {"h": pl.BlockSpec(memory_space=pl.ANY), "s": pl.BlockSpec(memory_space=pltpu.SMEM)}
     return pl.pallas_call(
@@ -440,7 +558,7 @@
         in_specs=[kinds[k] for k in ins],
         out_specs=[pl.BlockSpec(memory_space=pltpu.VMEM)] * len(outs),
         scratch_shapes=[pltpu.SemaphoreType.DMA((copies,))],
-        compiler_params=pltpu.CompilerParams(vmem_limit_bytes=VMEM_LIMIT),
+        compiler_params=pltpu.CompilerParams(vmem_limit_bytes=16 * 2**20),
         cost_estimate=small_cost(),
     )(*operands)
 
@@ -571,12 +689,6 @@
             + [gain_part],
             axis=0,
         )
-    first_pieces = [first_part] + [ring(first_part, s) for s in range(1, n)]
-    token_pieces = plane_gather(token_part)
-    grad_all = lax.all_gather(
-        jnp.concatenate([grad_part, pair(grad_part)], axis=0), "gran", axis=0
-    )
-
     shares = 2 * g
     strip = units // n // shares
     share = p * 2 + z % 2
@@ -598,7 +710,22 @@
             axis=0,
         )
 
-    even_part, odd_part, *first_pieces = cut(second_part(0), second_part(1), *first_pieces)
+    first_moved = [ring(first_part, k) for k in range(1, n)]
+
+    def rows_out(first_part, token_part, grad_part):
+        token_pieces = plane_gather(token_part)
+        first_part, grad_part, *token_pieces = cut(first_part, grad_part, *token_pieces)
+        grad_both = jnp.concatenate([grad_part, pair(grad_part)], axis=0)
+        return token_pieces, core(first_part), grad_both, second_part(0), second_part(1)
+
+    token_pieces, own_far, grad_both, even_part, odd_part = together(
+        rows_out, first_part, token_part, grad_part
+    )
+    even_part, odd_part, own_far, grad_both, *first_moved = cut(
+        even_part, odd_part, own_far, grad_both, *first_moved
+    )
+    grad_all = lax.all_gather(grad_both, "gran", axis=0)
+    first_pieces = [first_part, *first_moved]
     second_here = [even_part] + [
         ring(odd_part if k % 2 else even_part, k) for k in range(1, n)
     ]
@@ -609,9 +736,9 @@
         inverse = lax.rsqrt(jnp.mean(values * values, axis=-1, keepdims=True) + EPSILON)
         return values * inverse, inverse
 
-    def attention(token_pieces, first_pieces):
-        first_far = [core(v) for v in first_pieces[:2]]
-        first_far += [core(v) for v in cut(*first_pieces[2:], *first_far)[: n - 2]]
+    def attention(token_pieces, first_pieces, own_far):
+        first_far = [own_far, *(core(v) for v in first_pieces[1:3])]
+        first_far += [core(v) for v in cut(*first_pieces[3:], *first_far)[: n - 3]]
         frequencies = ROPE_BASE ** (-(2.0 * jnp.arange(head // 2, dtype=F32)) / head)
         frequencies = jnp.broadcast_to(jnp.concatenate([frequencies, frequencies]), (8, head))
         all_normed, my_qkv, queries, keys, values, attended, cosines, sines, bias, gains = call(
@@ -649,7 +776,7 @@
             return jnp.stack(picked)
 
         out_pieces = [out_part_for(0)] + [hop(out_part_for(r), r) for r in (1, 2)]
-        out_pieces.append(hop(after(out_part_for(3), *out_pieces), 3))
+        out_pieces.append(hop(after(out_part_for(3), attended, *out_pieces), 3))
         if hs % 8 == 0:
             [my_out] = move(
                 functools.partial(out_weight_kernel, n, g, hs, mine),
@@ -672,29 +799,52 @@
         middle = tokens.astype(F32) + plane_reduce(*attn_parts)
         unit_second, inverse_second = unit(middle)
         normed_ffn = (unit_second * gains[8:9]).astype(BF)
-        both_rows = plane_gather(jnp.concatenate([normed_ffn, pair(normed_ffn)], axis=0))
-        group_rows = jnp.concatenate(both_rows, axis=0)
+        both_rows = jnp.concatenate([normed_ffn, pair(normed_ffn)], axis=0)
         kept = (all_normed, my_qkv, my_out, queries, keys, values, attended, cosines, sines, bias)
-        return kept, gains, middle, unit_second, inverse_second, group_rows
-
-    kept, gains, middle, unit_second, inverse_second, group_rows = together(
-        attention, token_pieces, first_pieces
+        return kept, gains, middle, unit_second, inverse_second, both_rows
+
+    kept, gains, middle, unit_second, inverse_second, both_rows = together(
+        attention, token_pieces, first_pieces, own_far
     )
     all_normed, my_qkv, my_out, queries, keys, values, attended, cosines, sines, bias = kept
     gain_first, gain_second = gains[0:1], gains[8:9]
     residual = tokens.astype(F32)
-    group_rows, grad_all, *second_here = cut(group_rows, grad_all, *second_here)
+    both_rows, grad_all, *second_here = cut(both_rows, grad_all, *second_here)
+    row_pieces = plane_gather(both_rows)
     second_far = [core(v) for v in second_here]
 
-    if strip % 8 == 0:
-        gate_matrix, up_matrix, down_matrix = move(
-            functools.partial(unit_weights_kernel, n, depth, strip),
-            [(width, 2 * span), (width, 2 * span), (2 * span, width)],
-            2 * n * (2 + cuts),
-            (place, *second_here, *second_far),
-            "s" + "h" * (2 * n),
-        )
+    index = jnp.arange(2 * span, dtype=jnp.int32) % span
+    unit_index = (index // strip) * (strip * shares) + share * strip + index % strip
+    pair_rows = 2 * all_rows
+    if strip % 16 == 0:
+        shapes = [((pair_rows, width), BF)] * 2 + [((pair_rows, 2 * span), BF)] * 3
+        shapes += split_shapes(2 * rows, width) * 2
+        group_rows, group_grads, hidden, grad_gate, grad_lifted, *parts = call(
+            functools.partial(feed_forward_kernel, n, g, depth, strip, rows),
+            shapes,
+            [pltpu.VMEM(*v) for v in shapes]
+            + [
+                pltpu.VMEM((width, 2 * span), BF),
+                pltpu.VMEM((width, 2 * span), BF),
+                pltpu.VMEM((2 * span, width), BF),
+                pltpu.VMEM((2 * g, 16, rows), BF),
+                pltpu.SemaphoreType.DMA((5 + 2 * n * (2 + cuts) + 4 * g,)),
+                pltpu.SemaphoreType.DMA((18,)),
+            ],
+            "sv" + "h" * (6 + 2 * n),
+            (
+                place,
+                jnp.broadcast_to(unit_index.astype(F32), (8, 2 * span)),
+                *row_pieces,
+                grad_all,
+                *second_here,
+                *second_far,
+            ),
+            out="h",
+        )
+        input_parts, partial_ffn = parts[:5], parts[5:]
     else:
+        group_rows = jnp.concatenate(row_pieces, axis=0)
         stacks = []
         for pieces in (second_here, second_far):
             out = jnp.zeros((n, *pieces[0].shape), BF)
@@ -711,42 +861,49 @@
             [v[:, 2 * depth :].reshape(n, cuts, strip, span).transpose(0, 2, 1, 3) for v in stacks],
             axis=0,
         ).reshape(2 * span, width)
-    grad_got = jnp.stack(
-        [lax.dynamic_index_in_dim(grad_all, p ^ r, 0, keepdims=False) for r in range(g)]
-    ).reshape(g, 2, rows + 16, width)
-    group_grads = grad_got[:, :, :rows].reshape(2 * g * rows, width)
-    group_codes = grad_got[:, :, rows, :rows].reshape(2 * g * rows, 1).astype(jnp.int32)
-    group_limits = jnp.where(
-        group_codes < 0, 0, jnp.right_shift(jnp.int32(units), jnp.minimum(3 - group_codes, 3))
+        grad_got = jnp.stack(
+            [lax.dynamic_index_in_dim(grad_all, p ^ r, 0, keepdims=False) for r in range(g)]
+        ).reshape(g, 2, rows + 16, width)
+        group_grads = grad_got[:, :, :rows].reshape(2 * g * rows, width)
+        group_codes = grad_got[:, :, rows, :rows].reshape(2 * g * rows, 1).astype(jnp.int32)
+        group_limits = jnp.where(
+            group_codes < 0, 0, jnp.right_shift(jnp.int32(units), jnp.minimum(3 - group_codes, 3))
+        )
+        live = unit_index[None, :] < group_limits
+        gate_pre = dot(group_rows, gate_matrix)
+        lifted = dot(group_rows, up_matrix)
+        sigmoid_gate = jax.nn.sigmoid(gate_pre)
+        activated = gate_pre * sigmoid_gate
+        hidden = jnp.where(live, (activated * lifted).astype(BF), jnp.zeros((), BF))
+        grad_hidden = jnp.where(live, contract_cols(group_grads, down_matrix), 0.0)
+        grad_gate = (
+            grad_hidden * lifted * sigmoid_gate * (1.0 + gate_pre * (1.0 - sigmoid_gate))
+        ).astype(BF)
+        grad_lifted = (grad_hidden * activated).astype(BF)
+        partial_input = (
+            contract_cols(grad_gate, gate_matrix) + contract_cols(grad_lifted, up_matrix)
+        ).astype(BF)
+        input_parts = split_rows(partial_input.reshape(g, 2 * rows, width))
+        partial_ffn = split_rows(dot(hidden, down_matrix).astype(BF).reshape(g, 2 * rows, width))
+
+    def unit_grads(half):
+        low = slice(half * span, (half + 1) * span)
+        return (
+            contract_rows(group_rows, grad_gate[:, low]),
+            contract_rows(group_rows, grad_lifted[:, low]),
+            contract_rows(hidden[:, low], group_grads),
+        )
+
+    to_one, to_two, *waiting = input_parts
+    got = cut(hop(to_one, 1), hop(to_two, 2), *(v.astype(BF) for v in unit_grads(1)))
+    reduced = plane_reduce_rest(*got[:2], *waiting)
+    gate_sum, up_sum, down_sum = (
+        (v + core(w).astype(F32)).astype(BF) for v, w in zip(unit_grads(0), got[2:])
     )
-    index = jnp.arange(2 * span, dtype=jnp.int32) % span
-    unit_index = (index // strip) * (strip * shares) + share * strip + index % strip
-    live = unit_index[None, :] < group_limits
-    gate_pre = dot(group_rows, gate_matrix)
-    lifted = dot(group_rows, up_matrix)
-    sigmoid_gate = jax.nn.sigmoid(gate_pre)
-    activated = gate_pre * sigmoid_gate
-    hidden = jnp.where(live, (activated * lifted).astype(BF), jnp.zeros((), BF))
-    grad_hidden = jnp.where(live, contract_cols(group_grads, down_matrix), 0.0)
-    grad_gate = (
-        grad_hidden * lifted * sigmoid_gate * (1.0 + gate_pre * (1.0 - sigmoid_gate))
-    ).astype(BF)
-    grad_lifted = (grad_hidden * activated).astype(BF)
-    partial_input = (
-        contract_cols(grad_gate, gate_matrix) + contract_cols(grad_lifted, up_matrix)
-    ).astype(BF)
-    input_parts = split_rows(partial_input.reshape(g, 2 * rows, width))
-
-    def core_sum(left, right, split_left):
-        if split_left:
-            theirs = contract_rows(left[:, span:], right).astype(BF)
-            return (contract_rows(left[:, :span], right) + core(theirs).astype(F32)).astype(BF)
-        theirs = contract_rows(left, right[:, span:]).astype(BF)
-        return (contract_rows(left, right[:, :span]) + core(theirs).astype(F32)).astype(BF)
-
-    gate_sum = core_sum(group_rows, grad_gate, False).reshape(n, depth, span)
-    up_sum = core_sum(group_rows, grad_lifted, False).reshape(n, depth, span)
-    down_sum = core_sum(hidden, group_grads, True).reshape(n, strip, cuts, span)
+    halves, gate_sum, up_sum, down_sum = cut(reduced, gate_sum, up_sum, down_sum)
+    gate_sum = gate_sum.reshape(n, depth, span)
+    up_sum = up_sum.reshape(n, depth, span)
+    down_sum = down_sum.reshape(n, strip, cuts, span)
 
     def unit_sums(k):
         own = lax.dynamic_index_in_dim(down_sum, k, 0, keepdims=False).transpose(1, 0, 2)
@@ -756,147 +913,168 @@
             axis=0,
         )
 
-    to_one, to_two, *waiting = input_parts
-    got_one, got_two = hop(to_one, 1), hop(to_two, 2)
+    own_half, far_half = halves[:rows], pair(halves[rows:].astype(BF))
+    to_one, to_two, *branch_waiting = partial_ffn
+    to_one, to_two = cut(to_one, to_two, halves)[:2]
+    branch_got = hop(to_one, 1), hop(to_two, 2)
     messages = [unit_sums((z + k) % n) for k in range(n)]
-    got_one, got_two, *messages = cut(got_one, got_two, *messages)
+    far_half, branch_got, *messages = cut(far_half, branch_got, *messages)
     sums = [messages[0].astype(F32), 0.0]
     moved = [ring(messages[k], k) for k in range(1, n)]
 
-    def attention_back(got_one, got_two, waiting):
-        halves = plane_reduce_rest(got_one, got_two, *waiting)
-        grad_normed_ffn = halves[:rows] + pair(halves[rows:].astype(BF)).astype(F32)
-        grad_normed_ffn = grad_normed_ffn.astype(BF).astype(F32)
+    def my_half(x, which, axis):
+        return lax.dynamic_index_in_dim(x, which, axis, keepdims=False)
+
+    def for_member(stacked, r, axis):
+        return lax.dynamic_index_in_dim(stacked, p ^ r, axis, keepdims=False)
+
+    def attention_back(own_half, far_half, branch_got):
+        grad_normed_ffn = (own_half + far_half.astype(F32)).astype(BF).astype(F32)
         grad_middle = out_cotangent.astype(F32) + norm_back(
             grad_normed_ffn, unit_second, inverse_second, gain_second
         )
         branch_pieces = plane_gather(grad_middle.astype(BF))
-        return grad_middle, call(
+        fast = n == g and hs % 16 == 0
+        if fast:
+            branch_rows = jnp.concatenate(branch_pieces, axis=0)
+            out_here, out_there = call(
+                functools.partial(out_sums_kernel, g, hs, mine),
+                [((g, blocks * hs, mine), BF)] * 2,
+                [pltpu.VMEM((mine, mine), F32)],
+                "svv",
+                (place, attended, branch_rows),
+            )
+            out_there, *branch_pieces = cut(core(out_there), *branch_pieces)
+            out_sum = (out_here.astype(F32) + out_there.astype(F32)).astype(BF)
+        got_one, got_two, *branch_pieces = cut(*branch_got, *branch_pieces)
+        branch_sum = plane_reduce_rest(got_one, got_two, *branch_waiting)
+        grad_branch, grad_packed, *normed_parts = call(
             functools.partial(attend_back_kernel, rows, mine, head),
             [((all_rows, width), BF), ((all_rows, 3 * mine), BF), *split_shapes(rows, width)],
             [pltpu.VMEM((all_rows, mine), BF)],
             "v" * 13,
             (*branch_pieces, my_out, my_qkv, queries, keys, values, cosines, sines, bias),
         )
-
-    grad_middle, (grad_branch, grad_packed, *normed_parts) = together(
-        attention_back, got_one, got_two, waiting
+        branch_sum, grad_packed = cut(branch_sum, grad_packed)
+        if fast:
+            quarters = [hop(for_member(after(out_sum, grad_packed), r, 0), r) for r in (1, 2)]
+            sum_here, sum_there = call(
+                functools.partial(weight_sums_kernel, g, depth, mine),
+                [((g, 3 * hd, mine), BF)] * 2,
+                [pltpu.VMEM((depth, 3 * mine), F32)],
+                "svv",
+                (place, all_normed, grad_packed),
+            )
+            sum_there, out_sum, *quarters = cut(sum_there, out_sum, *quarters)
+            quarters.append(hop(for_member(out_sum, 3, 0), 3))
+            weight_sum = (sum_here.astype(F32) + core(sum_there).astype(F32)).astype(BF)
+            last_parts = call(
+                functools.partial(last_parts_kernel, g, 3 * hd),
+                [((3 * hd + blocks * hs, mine), BF)] * g,
+                [pltpu.VMEM((g, blocks * hs, mine), BF)],
+                "s" + "v" * (g + 1),
+                (place, weight_sum, for_member(out_sum, 0, 0), *quarters),
+            )
+        else:
+            out_grad = contract_rows(attended, grad_branch).astype(BF)
+            out_grad = out_grad.reshape(n // g, g, 2, hs, width)
+            out_sum = my_half(out_grad, c, 2).astype(F32)
+            out_sum = (out_sum + core(my_half(out_grad, 1 - c, 2)).astype(F32)).astype(BF)
+            out_sum = by_member(
+                [for_member(out_sum, 0, 1)]
+                + [hop(for_member(out_sum, r, 1), r) for r in range(1, g)]
+            ).reshape(n, hs, blocks, mine)
+            qkv_grad = contract_rows(all_normed, grad_packed).astype(BF).reshape(n, 2, hd, 3, mine)
+            qkv_sum = my_half(qkv_grad, c, 1).astype(F32)
+            qkv_sum += core(my_half(qkv_grad, 1 - c, 1)).astype(F32)
+            last_part = jnp.concatenate(
+                [
+                    qkv_sum.astype(BF).transpose(0, 2, 1, 3).reshape(n, 3 * hd, mine),
+                    out_sum.transpose(0, 2, 1, 3).reshape(n, blocks * hs, mine),
+                ],
+                axis=1,
+            )
+            last_parts = [
+                lax.dynamic_index_in_dim(last_part, (z + k) % n, 0, keepdims=False) for k in range(n)
+            ]
+        return grad_middle, normed_parts, last_parts, branch_sum
+
+    grad_middle, normed_parts, last_parts, branch_sum = together(
+        attention_back, own_half, far_half, branch_got
     )
-    grad_branch, grad_packed, *moved = cut(grad_branch, grad_packed, *moved)
+    cut_values = cut(*moved, *last_parts)
+    moved, last_parts = cut_values[: n - 1], cut_values[n - 1 :]
     for k in range(1, n):
         sums[k % 2] += moved[k - 1].astype(F32)
     even_sum, odd_sum = (v.astype(BF) for v in sums)
-
-    partial_ffn = dot(hidden, down_matrix).astype(BF).reshape(g, 2 * rows, width)
-    partial_ffn = by_member([partial_ffn[r] for r in range(g)]).reshape(-1, width)
-    branch_sum = lax.psum_scatter(
-        after(partial_ffn, got_one), "gran", scatter_dimension=0, tiled=True
-    )
-
-    def my_half(x, which, axis):
-        return lax.dynamic_index_in_dim(x, which, axis, keepdims=False)
-
-    def for_member(stacked, r, axis):
-        return lax.dynamic_index_in_dim(stacked, p ^ r, axis, keepdims=False)
-
-    out_grad = contract_rows(attended, grad_branch).astype(BF).reshape(n // g, g, 2, hs, width)
-    out_sum = my_half(out_grad, c, 2).astype(F32) + core(my_half(out_grad, 1 - c, 2)).astype(F32)
-    out_sum = out_sum.astype(BF)
-    out_sum = by_member(
-        [for_member(out_sum, 0, 1)]
-        + [hop(for_member(out_sum, r, 1), r) for r in range(1, g)]
-    ).reshape(n, hs, blocks, mine)
-    qkv_grad = contract_rows(all_normed, grad_packed).astype(BF).reshape(n, 2, hd, 3, mine)
-    qkv_sum = my_half(qkv_grad, c, 1).astype(F32) + core(my_half(qkv_grad, 1 - c, 1)).astype(F32)
-    last_part = jnp.concatenate(
-        [
-            qkv_sum.astype(BF).transpose(0, 2, 1, 3).reshape(n, 3 * hd, mine),
-            out_sum.transpose(0, 2, 1, 3).reshape(n, blocks * hs, mine),
-        ],
-        axis=1,
-    )
-    last_parts = [
-        lax.dynamic_index_in_dim(last_part, (z + k) % n, 0, keepdims=False) for k in range(n)
-    ]
-    normed_parts, branch_sum, even_sum, odd_sum, *last_parts = cut(
-        normed_parts, branch_sum, even_sum, odd_sum, *last_parts
-    )
     last_moved = [ring(last_parts[k], k) for k in range(1, n)]
 
-    def results(normed_parts, branch_sum, even_sum, odd_sum):
+    def units_out(even_sum, odd_sum, normed_parts):
+        unit_pieces = plane_gather(jnp.concatenate([even_sum, odd_sum], axis=0))
+        normed_parts = cut(*normed_parts, *unit_pieces)[:5]
         grad_normed = plane_reduce(*normed_parts)
         unit_first, inverse_first = unit(residual)
         input_grad = (
             grad_middle + norm_back(grad_normed, unit_first, inverse_first, gain_first)
         ).astype(BF)
-        branch_far = pair(after(branch_sum[rows:], grad_normed))
-        branch_ffn = branch_sum[:rows].astype(F32) + branch_far.astype(F32)
-        outputs = (middle + branch_ffn).astype(BF)
-        unit_pieces = plane_gather(
-            after(jnp.concatenate([even_sum, odd_sum], axis=0), branch_far)
-        )
-        if strip % 32 == 0:
-            share_gate, share_up, share_down, ffn_part = call(
-                functools.partial(unit_results_kernel, n, g, depth, strip),
-                [
-                    ((depth * units // 128, 128), F32),
-                    ((depth * units // 128, 128), F32),
-                    ((units // n * width // 128, 128), F32),
-                    ((depth, 1), F32),
-                ],
-                [
-                    pltpu.VMEM((shares, 2 * depth + cuts * strip, span), BF),
-                    pltpu.SemaphoreType.DMA((3, shares)),
-                ],
-                "s" + "h" * 5 + "vv",
-                (place, *unit_pieces, w_gate[:, 0], w_up[:, 0]),
-            )
-            ffn_part = ffn_part[:, 0]
-        else:
-            got = as_members(unit_pieces).reshape(g, 2, -1, span)
-            all_units = jnp.zeros((shares, *got.shape[2:]), BF)
-            for r in range(g):
-                for odd in (0, 1):
-                    all_units = lax.dynamic_update_index_in_dim(
-                        all_units, got[r, odd], (p ^ r) * 2 + (z % 2) ^ odd, 0
-                    )
-
-            def columns_back(pieces):
-                return (
-                    pieces.reshape(shares, depth, n, strip)
-                    .transpose(1, 2, 0, 3)
-                    .reshape(depth, units)
-                    .astype(F32)
+        return list(unit_pieces), input_grad
+
+    unit_pieces, input_grad = together(units_out, even_sum, odd_sum, normed_parts)
+    got = cut(*unit_pieces, *last_moved)
+    unit_pieces, last_moved = got[:5], got[5:]
+    last_sum = last_parts[0].astype(F32) + sum(v.astype(F32) for v in last_moved)
+    last_one = gather_first(last_sum.astype(BF))
+    if strip % 32 == 0:
+        share_gate, share_up, share_down, ffn_part = call(
+            functools.partial(unit_results_kernel, n, g, depth, strip),
+            [
+                ((depth * units // 128, 128), F32),
+                ((depth * units // 128, 128), F32),
+                ((units // n * width // 128, 128), F32),
+                ((depth, 1), F32),
+            ],
+            [
+                pltpu.VMEM((shares, 2 * depth + cuts * strip, span), BF),
+                pltpu.SemaphoreType.DMA((3, shares)),
+            ],
+            "s" + "h" * 5 + "vv",
+            (place, *unit_pieces, w_gate[:, 0], w_up[:, 0]),
+        )
+        ffn_part = ffn_part[:, 0]
+    else:
+        got = as_members(unit_pieces).reshape(g, 2, -1, span)
+        all_units = jnp.zeros((shares, *got.shape[2:]), BF)
+        for r in range(g):
+            for odd in (0, 1):
+                all_units = lax.dynamic_update_index_in_dim(
+                    all_units, got[r, odd], (p ^ r) * 2 + (z % 2) ^ odd, 0
                 )
 
-            share_gate = columns_back(all_units[:, :depth])
-            share_up = columns_back(all_units[:, depth : 2 * depth])
-            share_down = (
-                all_units[:, 2 * depth :]
-                .reshape(shares, cuts, strip, span)
-                .transpose(0, 2, 1, 3)
-                .reshape(units // n, width)
+        def columns_back(pieces):
+            return (
+                pieces.reshape(shares, depth, n, strip)
+                .transpose(1, 2, 0, 3)
+                .reshape(depth, units)
                 .astype(F32)
             )
-            ffn_part = jnp.sum(
-                share_gate * w_gate[:, 0].astype(F32) + share_up * w_up[:, 0].astype(F32), axis=1
-            )
-        share_gain_ffn = (ffn_part + core(ffn_part)) / gain_ffn.astype(F32)
-        return (
-            outputs,
-            input_grad,
-            share_gain_ffn,
-            share_gate.reshape(depth, 1, units),
-            share_up.reshape(depth, 1, units),
-            share_down.reshape(units // n, 1, width),
-        )
-
-    outputs, input_grad, share_gain_ffn, share_gate, share_up, share_down = together(
-        results, normed_parts, branch_sum, even_sum, odd_sum
-    )
-    outputs, *last_moved = cut(outputs, *last_moved)
-    last_sum = last_parts[0].astype(F32) + sum(v.astype(F32) for v in last_moved)
-    last_pieces = plane_gather(last_sum.astype(BF))
+
+        share_gate = columns_back(all_units[:, :depth])
+        share_up = columns_back(all_units[:, depth : 2 * depth])
+        share_down = (
+            all_units[:, 2 * depth :]
+            .reshape(shares, cuts, strip, span)
+            .transpose(0, 2, 1, 3)
+            .reshape(units // n, width)
+            .astype(F32)
+        )
+        ffn_part = jnp.sum(
+            share_gate * w_gate[:, 0].astype(F32) + share_up * w_up[:, 0].astype(F32), axis=1
+        )
+    *last_one, ffn_part = cut(*last_one, ffn_part)
+    last_pieces = gather_rest(last_one)
+    share_gain_ffn = (ffn_part + core(ffn_part)) / gain_ffn.astype(F32)
+    branch_ffn = branch_sum[:rows] + pair(branch_sum[rows:].astype(BF)).astype(F32)
+    outputs = (middle + branch_ffn.astype(BF).astype(F32)).astype(BF)
     if hs % 16 == 0:
         share_qkv, share_out, attn_part = call(
             functools.partial(attention_results_kernel, g, depth, mine),
@@ -937,9 +1115,9 @@
         share_out,
         share_gain_attn,
         share_gain_ffn,
-        share_gate,
-        share_up,
-        share_down,
+        share_gate.reshape(depth, 1, units),
+        share_up.reshape(depth, 1, units),
+        share_down.reshape(units // n, 1, width),
     )
 
 

time: 619 us -> 532 us (0.86)
  the two profiles are of different devices: /device:TPU:27 before, /device:TPU:0 now
where the time goes in v3:
time: 532 us; the launch traced here: 526 us
  waiting for transfers between devices  208 us (39%)
  starting transfers between devices  104 us (20%)
  Pallas kernels  80.4 us (15%)
  local copies, waits for them, and re-layouts  55.2 us (10%)
  other arithmetic  41 us (8%)
  matrix products  21.8 us (4%)
  between operations  15.3 us (3%)
    ppermute x42, waiting for transfers between devices, hop(): return lax.ppermute(x, 'gran', [(i, i ^ r) for i in range(g)])  180 us
    pallas_call x9, Pallas kernels, call(): pl.pallas_call(kernel, out_shape=[jax.ShapeDtypeStruct(shape, dtype) for...  76.8 us
    ppermute x12, starting transfers between devices, ring(): return lax.ppermute(x, 'batch', [(i, (i + s) % n) for i in range(n)])  48.5 us
    ppermute x42, starting transfers between devices, hop(): return lax.ppermute(x, 'gran', [(i, i ^ r) for i in range(g)])  48.4 us
    dot_general x6, matrix products, contract_rows(): lax.dot_general(left, right, (((0,), (0,)), ((), ())), preferred_element_...  21.8 us
    ppermute x4, waiting for transfers between devices, pair(): return lax.ppermute(x, 'batch', [(i, i ^ 1) for i in range(n)])  21 us
    unnamed x94, local copies, waits for them, and re-layouts  12.7 us
  transfers between devices with their start and end apart: 78, of which 39 were waited for; matrix products, arithmetic and copies ran while one was open for 18% of the time, Pallas kernels for 9%

profile of v3, /device:TPU:0, one launch (start us, length us, event | category | flops | bytes accessed | tf_op | source)
XLA Modules:
  0.0 526.2 jit_solution(1157643803812239295)
XLA Ops:
  21.9 48.1 %conditional.4 = (bf16[144,1536]{1,0:T(8,128)(2,1)}, bf16[144,1536]{1,0:T(8,128)(2,1)}, bf16[144,1536]{1,0:T(8,128)(2,1)}, bf16[64,1536]{1,0:T(8,128)(2,1)}, bf1...) conditional(s32[]{:T(128)} %bitcast.27, () %tuple.61, ...), branch_computations={%region_2.3_spmd, %region_3.4_spmd} | conditional | flops 1769479 | bytes 35045864 | solution.py:657
  24.9 8.4 %collective-permute-done.31 = bf16[144,1536]{1,0:T(8,128)(2,1)} collective-permute-done((bf16[144,1536]{1,0:T(8,128)(2,1)}, bf16[144,1536]{1,0:T(8,128)(2,1)}, u32[]{:S(2)}, u32[]{:S(2)}) %collective-permute-start.31) | collective-permute-done | bytes 442400 | tf_op jit(solution)/shard_map/cond/branch_1_fun/ppermute | solution.py:593
  57.3 10.5 %collective-permute-done.35 = bf16[144,1536]{1,0:T(8,128)(2,1)} collective-permute-done((bf16[144,1536]{1,0:T(8,128)(2,1)}, bf16[144,1536]{1,0:T(8,128)(2,1)}, u32[]{:S(2)}, u32[]{:S(2)}) %collective-permute-start.35) | collective-permute-done | bytes 442400 | tf_op jit(solution)/shard_map/cond/branch_1_fun/ppermute | solution.py:596
  75.5 8.6 %collective-permute-start.40 = (bf16[1152,384]{1,0:T(8,128)(2,1)}, bf16[1152,384]{1,0:T(8,128)(2,1)}, u32[]{:S(2)}, u32[]{:S(2)}) collective-permute-start(bf16[1152,384]{1,0:T(8,128)(2,1)} %copy.89), channel_id=1, source_target_pairs={{0,16},{8,24},{16,0},{24,8},{1,17},{9,25},{17,1},{25,9},{2,18},{10... | collective-permute-start | bytes 2654216 | tf_op jit(solution)/shard_map/ppermute | solution.py:602
  84.5 74.6 %conditional.5 = (bf16[512,1536]{1,0:T(8,128)(2,1)S(1)}, bf16[1536,1152]{1,0:T(8,128)(2,1)S(1)}, bf16[384,1536]{1,0:T(8,128)(2,1)}, bf16[512,384]{1,0:T(8,128)(2...) conditional(s32[]{:T(128)} %bitcast.27, () %tuple.60, ...), branch_computations={%region_4.5_spmd, %region_5.7_spmd} | conditional | flops 8651267 | bytes 44823876 | solution.py:657
  93.9 10.3 %branch_1_fun.7 = (bf16[512,1536]{1,0:T(8,128)(2,1)}, bf16[1536,1152]{1,0:T(8,128)(2,1)S(1)}, bf16[512,384]{1,0:T(8,128)(2,1)}, bf16[512,384]{1,0:T(8,128)(2,1)}...) custom-call(s32[3]{0:T(128)S(1)} %get-tuple-element.127.place, ...), custom_call_target="tpu_custom_call" | custom-call | flops 1 | bytes 1 | tf_op jit(solution)/shard_map/cond/branch_1_fun/pallas_call | solution.py:70
  105.8 12.2 %collective-permute-done.13.refs_3_ = bf16[1,2,192,384]{3,2,1,0:T(8,128)(2,1)S(1)} collective-permute-done((bf16[1,2,192,384]{3,2,1,0:T(8,128)(2,1)S(1)}, bf16[1,2,192,384]{3,2,1,0:T(8,128)(2,1)S(1)}, u32[]{:S(2)}, u32[]{:S(2)}) %collective-permute-start.13) | collective-permute-done | bytes 294944 | tf_op jit(solution)/shard_map/cond/branch_1_fun/ppermute | solution.py:593
  125.6 14.8 %collective-permute-done.14 = bf16[128,1536]{1,0:T(8,128)(2,1)S(1)} collective-permute-done((bf16[128,1536]{1,0:T(8,128)(2,1)S(1)}, bf16[128,1536]{1,0:T(8,128)(2,1)S(1)}, u32[]{:S(2)}, u32[]{:S(2)}) %collective-permute-start.14) | collective-permute-done | bytes 393248 | tf_op jit(solution)/shard_map/cond/branch_1_fun/ppermute | solution.py:593
  152.4 6.2 %collective-permute-done.18 = bf16[128,1536]{1,0:T(8,128)(2,1)S(1)} collective-permute-done((bf16[128,1536]{1,0:T(8,128)(2,1)S(1)}, bf16[128,1536]{1,0:T(8,128)(2,1)S(1)}, u32[]{:S(2)}, u32[]{:S(2)}) %collective-permute-start.18) | collective-permute-done | bytes 393248 | tf_op jit(solution)/shard_map/cond/branch_1_fun/ppermute | solution.py:596
  165.6 9.7 %collective-permute-done.42.refs_1_ = bf16[256,1536]{1,0:T(8,128)(2,1)S(1)} collective-permute-done((bf16[256,1536]{1,0:T(8,128)(2,1)}, bf16[256,1536]{1,0:T(8,128)(2,1)S(1)}, u32[]{:S(2)}, u32[]{:S(2)}) %collective-permute-start.42) | collective-permute-done | bytes 786464 | tf_op jit(solution)/shard_map/ppermute | solution.py:593
  176.1 8.5 %collective-permute-done.43.refs_2_ = bf16[256,1536]{1,0:T(8,128)(2,1)S(1)} collective-permute-done((bf16[256,1536]{1,0:T(8,128)(2,1)}, bf16[256,1536]{1,0:T(8,128)(2,1)S(1)}, u32[]{:S(2)}, u32[]{:S(2)}) %collective-permute-start.43) | collective-permute-done | bytes 786464 | tf_op jit(solution)/shard_map/ppermute | solution.py:593
  188.1 7.5 %collective-permute-done.44.refs_3_ = bf16[128,1536]{1,0:T(8,128)(2,1)} collective-permute-done((bf16[128,1536]{1,0:T(8,128)(2,1)}, bf16[128,1536]{1,0:T(8,128)(2,1)}, u32[]{:S(2)}, u32[]{:S(2)}) %collective-permute-start.44) | collective-permute-done | bytes 393248 | tf_op jit(solution)/shard_map/ppermute | solution.py:593
  198.8 23.2 %shard_map.180 = (bf16[1024,1536]{1,0:T(8,128)(2,1)}, bf16[1024,1536]{1,0:T(8,128)(2,1)}, bf16[1024,768]{1,0:T(8,128)(2,1)S(1)}, bf16[1024,768]{1,0:T(8,128)(2,1...) custom-call(s32[3]{0:T(128)S(1)} %pad_add_fusion.place, ...), custom_call_target="tpu_custom_call" | custom-call | flops 1 | bytes 1 | tf_op jit(solution)/shard_map/pallas_call | solution.py:70
  246.8 6.8 %collective-permute-done.52 = bf16[128,1536]{1,0:T(8,128)(2,1)S(1)} collective-permute-done((bf16[128,1536]{1,0:T(8,128)(2,1)}, bf16[128,1536]{1,0:T(8,128)(2,1)S(1)}, u32[]{:S(2)}, u32[]{:S(2)}) %collective-permute-start.52) | collective-permute-done | bytes 393248 | tf_op jit(solution)/shard_map/ppermute | solution.py:593
  287.0 7.6 %collective-permute-done.58 = bf16[256,1536]{1,0:T(8,128)(2,1)} collective-permute-done((bf16[256,1536]{1,0:T(8,128)(2,1)S(1)}, bf16[256,1536]{1,0:T(8,128)(2,1)}, u32[]{:S(2)}, u32[]{:S(2)}) %collective-permute-start.58) | collective-permute-done | bytes 786464 | tf_op jit(solution)/shard_map/ppermute | solution.py:593
  301.8 65.3 %conditional.6 = (f32[128,1536]{1,0:T(8,128)}, bf16[128,1536]{1,0:T(8,128)(2,1)}, bf16[128,1536]{1,0:T(8,128)(2,1)}, f32[128,1536]{1,0:T(8,128)}, bf16[64,1536]{...) conditional(s32[]{:T(128)} %bitcast.27, () %tuple.65, ...), branch_computations={%region_7.8_spmd, %region_8.10_spmd} | conditional | flops 13762578 | bytes 73362912 | solution.py:657
  332.6 12.7 %branch_1_fun.11 = (bf16[512,1536]{1,0:T(8,128)(2,1)}, bf16[512,1152]{1,0:T(8,128)(2,1)S(1)}, bf16[128,1536]{1,0:T(8,128)(2,1)}, bf16[128,1536]{1,0:T(8,128)(2,1...) custom-call(bf16[128,1536]{1,0:T(8,128)(2,1)S(1)} %get-tuple-element.175.refs_0_, ...), custom_call_target="tpu_custom_call" | custom-call | flops 1 | bytes 1 | tf_op jit(solution)/shard_map/cond/branch_1_fun/pallas_call | solution.py:70
  367.1 22.0 %collective-permute-start.64 = (bf16[768,384]{1,0:T(8,128)(2,1)}, bf16[768,384]{1,0:T(8,128)(2,1)S(1)}, u32[]{:S(2)}, u32[]{:S(2)}) collective-permute-start(bf16[768,384]{1,0:T(8,128)(2,1)} %get-tuple-element.446), channel_id=1, source_target_pairs={{0,8},{8,16},{16,24},{24,0},{1,9},{9,17},{17,25},{25,1},{2,10},{10... | collective-permute-start | bytes 1769480 | tf_op jit(solution)/shard_map/ppermute | solution.py:602
  394.7 87.5 %conditional.7 = (bf16[2304,384]{1,0:T(8,128)(2,1)}, bf16[2304,384]{1,0:T(8,128)(2,1)}, bf16[2304,384]{1,0:T(8,128)(2,1)}, bf16[1152,384]{1,0:T(8,128)(2,1)}, bf...) conditional(s32[]{:T(128)} %bitcast.27, () %tuple.72, (bf16[1152,384]{1,0:T(8,128)(2,1)S(1)}, ...), branch_computations={%region_10.11_spmd, %region_11.14_spmd} | conditional | flops 7274624 | bytes 41710452 | solution.py:657
  399.6 37.3 %collective-permute-done = bf16[2304,384]{1,0:T(8,128)(2,1)} collective-permute-done((bf16[2304,384]{1,0:T(8,128)(2,1)}, bf16[2304,384]{1,0:T(8,128)(2,1)}, u32[]{:S(2)}, u32[]{:S(2)}) %collective-permute-start) | collective-permute-done | bytes 1769504 | tf_op jit(solution)/shard_map/cond/branch_1_fun/ppermute | solution.py:593
  442.6 15.9 %collective-permute-done.2 = bf16[1152,384]{1,0:T(8,128)(2,1)} collective-permute-done((bf16[1152,384]{1,0:T(8,128)(2,1)S(1)}, bf16[1152,384]{1,0:T(8,128)(2,1)}, u32[]{:S(2)}, u32[]{:S(2)}) %collective-permute-start.2) | collective-permute-done | bytes 884768 | tf_op jit(solution)/shard_map/cond/branch_1_fun/ppermute | solution.py:593
  463.2 6.4 %collective-permute-done.4 = bf16[128,1536]{1,0:T(8,128)(2,1)S(1)} collective-permute-done((bf16[128,1536]{1,0:T(8,128)(2,1)}, bf16[128,1536]{1,0:T(8,128)(2,1)S(1)}, u32[]{:S(2)}, u32[]{:S(2)}) %collective-permute-start.4) | collective-permute-done | bytes 393248 | tf_op jit(solution)/shard_map/cond/branch_1_fun/ppermute | solution.py:593
  487.3 13.7 %shard_map.181 = (f32[9216,128]{1,0:T(8,128)}, f32[9216,128]{1,0:T(8,128)}, f32[9216,128]{1,0:T(8,128)}, f32[384,1]{1,0:T(8,128)S(1)}) custom-call(s32[3]{0:T(128)S(1)} %pad_add_fusion.place, bf16[2304,384]{1,0:T(8,128)(2,1)} %get-tuple-element.452.refs_0_, bf16[2304,384]{1,0:T(8,128)(2,1)} %get-tuple-element.453.refs_1_, ...), custom_call_target="tpu_custom_call" | custom-call | flops 1 | bytes 1 | tf_op jit(solution)/shard_map/pallas_call | solution.py:70
  511.5 6.7 %shard_map.182 = (f32[384,4608]{1,0:T(8,128)}, f32[384,1536]{1,0:T(8,128)}, f32[384,1]{1,0:T(8,128)S(1)}) custom-call(s32[3]{0:T(128)S(1)} %pad_add_fusion.place, bf16[768,384]{1,0:T(8,128)(2,1)S(1)} %add_convert_fusion.12.refs_0_, bf16[768,384]{1,0:T(8,128)(2,1)S(1)} %collective-permute-done.67.refs_1_, ...), custom_call_target="tpu_custom_call" | custom-call | flops 1 | bytes 1 | tf_op jit(solution)/shard_map/pallas_call | solution.py:70
  (399 shorter events, 260.6 us)
Async XLA Ops:
  7.2 154.3 %all-gather.3.cloned.1.call-start = ((), (), s32[]{:S(2)}) async-start(), calls=%async_computation | async-start | bytes 4423680 | tf_op jit(solution)/shard_map/all_gather | solution.py:727
  13.5 56.4 %collective-permute-start.36 = (bf16[784,384]{1,0:T(8,128)(2,1)}, bf16[784,384]{1,0:T(8,128)(2,1)}, u32[]{:S(2)}, u32[]{:S(2)}) collective-permute-start(bf16[784,384]{1,0:T(8,128)(2,1)} %shard_map.179), channel_id=1, source_target_pairs={{0,8},{8,16},{16,24},{24,0},{1,9},{9,17},{17,25},{25,1},{2,10},{10... | collective-permute-start | bytes 1806344 | tf_op jit(solution)/shard_map/ppermute | solution.py:602
  16.6 53.4 %collective-permute-start.37 = (bf16[784,384]{1,0:T(8,128)(2,1)}, bf16[784,384]{1,0:T(8,128)(2,1)}, u32[]{:S(2)}, u32[]{:S(2)}) collective-permute-start(bf16[784,384]{1,0:T(8,128)(2,1)} %shard_map.179), channel_id=1, source_target_pairs={{0,16},{8,24},{16,0},{24,8},{1,17},{9,25},{17,1},{25,9},{2,18},{10... | collective-permute-start | bytes 1806344 | tf_op jit(solution)/shard_map/ppermute | solution.py:602
  19.2 50.8 %collective-permute-start.38 = (bf16[784,384]{1,0:T(8,128)(2,1)}, bf16[784,384]{1,0:T(8,128)(2,1)}, u32[]{:S(2)}, u32[]{:S(2)}) collective-permute-start(bf16[784,384]{1,0:T(8,128)(2,1)} %shard_map.179), channel_id=1, source_target_pairs={{0,24},{8,0},{16,8},{24,16},{1,25},{9,1},{17,9},{25,17},{2,26},{10... | collective-permute-start | bytes 1806344 | tf_op jit(solution)/shard_map/ppermute | solution.py:602
  42.6 25.3 %collective-permute-start.35 = (bf16[144,1536]{1,0:T(8,128)(2,1)}, bf16[144,1536]{1,0:T(8,128)(2,1)}, u32[]{:S(2)}, u32[]{:S(2)}) collective-permute-start(bf16[144,1536]{1,0:T(8,128)(2,1)} %get-tuple-element.122), channel_id=1, source_target_pairs={{0,8},{8,0},{16,24},{24,16},{1,9},{9,1},{17,25},{25,17},{2,10},{10... | collective-permute-start | bytes 1327112 | tf_op jit(solution)/shard_map/cond/branch_1_fun/ppermute | solution.py:596
  50.7 19.2 %collective-permute-start.34 = (bf16[784,384]{1,0:T(8,128)(2,1)}, bf16[784,384]{1,0:T(8,128)(2,1)}, u32[]{:S(2)}, u32[]{:S(2)}) collective-permute-start(bf16[784,384]{1,0:T(8,128)(2,1)} %get-tuple-element.121), channel_id=1, source_target_pairs={{0,1},{1,0},{2,3},{3,2},{4,5},{5,4},{6,7},{7,6},{8,9},{9,8},{10,11... | collective-permute-start | bytes 1806344 | tf_op jit(solution)/shard_map/cond/branch_1_fun/ppermute | solution.py:599
  72.5 86.7 %collective-permute-start.39 = (bf16[1152,384]{1,0:T(8,128)(2,1)}, bf16[1152,384]{1,0:T(8,128)(2,1)S(1)}, u32[]{:S(2)}, u32[]{:S(2)}) collective-permute-start(bf16[1152,384]{1,0:T(8,128)(2,1)} %copy.88), channel_id=1, source_target_pairs={{0,8},{8,16},{16,24},{24,0},{1,9},{9,17},{17,25},{25,1},{2,10},{10... | collective-permute-start | bytes 2654216 | tf_op jit(solution)/shard_map/ppermute | solution.py:602
  75.5 85.4 %collective-permute-start.40 = (bf16[1152,384]{1,0:T(8,128)(2,1)}, bf16[1152,384]{1,0:T(8,128)(2,1)}, u32[]{:S(2)}, u32[]{:S(2)}) collective-permute-start(bf16[1152,384]{1,0:T(8,128)(2,1)} %copy.89), channel_id=1, source_target_pairs={{0,16},{8,24},{16,0},{24,8},{1,17},{9,25},{17,1},{25,9},{2,18},{10... | collective-permute-start | bytes 2654216 | tf_op jit(solution)/shard_map/ppermute | solution.py:602
  84.0 77.5 %collective-permute-start.41 = (bf16[1152,384]{1,0:T(8,128)(2,1)}, bf16[1152,384]{1,0:T(8,128)(2,1)}, u32[]{:S(2)}, u32[]{:S(2)}) collective-permute-start(bf16[1152,384]{1,0:T(8,128)(2,1)} %copy.88), channel_id=1, source_target_pairs={{0,24},{8,0},{16,8},{24,16},{1,25},{9,1},{17,9},{25,17},{2,26},{10... | collective-permute-start | bytes 2654216 | tf_op jit(solution)/shard_map/ppermute | solution.py:602
  164.4 21.6 %collective-permute-start.46 = (bf16[1152,384]{1,0:T(8,128)(2,1)S(1)}, bf16[1152,384]{1,0:T(8,128)(2,1)S(1)}, u32[]{:S(2)}, u32[]{:S(2)}) collective-permute-start(bf16[1152,384]{1,0:T(8,128)(2,1)S(1)} %copy.92.refs_6_), channel_id=1, source_target_pairs={{0,1},{1,0},{2,3},{3,2},{4,5},{5,4},{6,7},{7,6},{8,9},{9,8},{10,11... | collective-permute-start | bytes 2654216 | tf_op jit(solution)/shard_map/ppermute | solution.py:599
  164.5 20.2 %collective-permute-start.43 = (bf16[256,1536]{1,0:T(8,128)(2,1)}, bf16[256,1536]{1,0:T(8,128)(2,1)S(1)}, u32[]{:S(2)}, u32[]{:S(2)}) collective-permute-start(bf16[256,1536]{1,0:T(8,128)(2,1)} %copy-done.36), channel_id=1, source_target_pairs={{0,4},{2,6},{4,0},{6,2},{1,5},{3,7},{5,1},{7,3},{8,12},{10,14},{12... | collective-permute-start | bytes 2359304 | tf_op jit(solution)/shard_map/ppermute | solution.py:593
  165.1 23.0 %collective-permute-start.47 = (bf16[1152,384]{1,0:T(8,128)(2,1)S(1)}, bf16[1152,384]{1,0:T(8,128)(2,1)}, u32[]{:S(2)}, u32[]{:S(2)}) collective-permute-start(bf16[1152,384]{1,0:T(8,128)(2,1)S(1)} %collective-permute-done.39.refs_7_), channel_id=1, source_target_pairs={{0,1},{1,0},{2,3},{3,2},{4,5},{5,4},{6,7},{7,6},{8,9},{9,8},{10,11... | collective-permute-start | bytes 2654216 | tf_op jit(solution)/shard_map/ppermute | solution.py:599
  165.3 22.8 %collective-permute-start.48 = (bf16[1152,384]{1,0:T(8,128)(2,1)}, bf16[1152,384]{1,0:T(8,128)(2,1)}, u32[]{:S(2)}, u32[]{:S(2)}) collective-permute-start(bf16[1152,384]{1,0:T(8,128)(2,1)} %collective-permute-done.40.refs_8_), channel_id=1, source_target_pairs={{0,1},{1,0},{2,3},{3,2},{4,5},{5,4},{6,7},{7,6},{8,9},{9,8},{10,11... | collective-permute-start | bytes 2654216 | tf_op jit(solution)/shard_map/ppermute | solution.py:599
  246.2 20.7 %collective-permute-start.54 = (bf16[1536,384]{1,0:T(8,128)(2,1)S(1)}, bf16[1536,384]{1,0:T(8,128)(2,1)S(1)}, u32[]{:S(2)}, u32[]{:S(2)}) collective-permute-start(bf16[1536,384]{1,0:T(8,128)(2,1)S(1)} %copy-done.59), channel_id=1, source_target_pairs={{0,1},{1,0},{2,3},{3,2},{4,5},{5,4},{6,7},{7,6},{8,9},{9,8},{10,11... | collective-permute-start | bytes 3538952 | tf_op jit(solution)/shard_map/ppermute | solution.py:599
  295.3 71.9 %collective-permute-start.61 = (bf16[1152,384]{1,0:T(8,128)(2,1)}, bf16[1152,384]{1,0:T(8,128)(2,1)}, u32[]{:S(2)}, u32[]{:S(2)}) collective-permute-start(bf16[1152,384]{1,0:T(8,128)(2,1)} %pad_maximum_fusion.6), channel_id=1, source_target_pairs={{0,8},{8,16},{16,24},{24,0},{1,9},{9,17},{17,25},{25,1},{2,10},{10... | collective-permute-start | bytes 2654216 | tf_op jit(solution)/shard_map/ppermute | solution.py:602
  296.8 70.3 %collective-permute-start.62 = (bf16[1152,384]{1,0:T(8,128)(2,1)}, bf16[1152,384]{1,0:T(8,128)(2,1)}, u32[]{:S(2)}, u32[]{:S(2)}) collective-permute-start(bf16[1152,384]{1,0:T(8,128)(2,1)} %pad_maximum_fusion.7), channel_id=1, source_target_pairs={{0,16},{8,24},{16,0},{24,8},{1,17},{9,25},{17,1},{25,9},{2,18},{10... | collective-permute-start | bytes 2654216 | tf_op jit(solution)/shard_map/ppermute | solution.py:602
  301.3 65.8 %collective-permute-start.63 = (bf16[1152,384]{1,0:T(8,128)(2,1)}, bf16[1152,384]{1,0:T(8,128)(2,1)}, u32[]{:S(2)}, u32[]{:S(2)}) collective-permute-start(bf16[1152,384]{1,0:T(8,128)(2,1)} %pad_maximum_fusion.8), channel_id=1, source_target_pairs={{0,24},{8,0},{16,8},{24,16},{1,25},{9,1},{17,9},{25,17},{2,26},{10... | collective-permute-start | bytes 2654216 | tf_op jit(solution)/shard_map/ppermute | solution.py:602
  367.1 115.0 %collective-permute-start.64 = (bf16[768,384]{1,0:T(8,128)(2,1)}, bf16[768,384]{1,0:T(8,128)(2,1)S(1)}, u32[]{:S(2)}, u32[]{:S(2)}) collective-permute-start(bf16[768,384]{1,0:T(8,128)(2,1)} %get-tuple-element.446), channel_id=1, source_target_pairs={{0,8},{8,16},{16,24},{24,0},{1,9},{9,17},{17,25},{25,1},{2,10},{10... | collective-permute-start | bytes 1769480 | tf_op jit(solution)/shard_map/ppermute | solution.py:602
  389.2 93.0 %collective-permute-start.65 = (bf16[768,384]{1,0:T(8,128)(2,1)}, bf16[768,384]{1,0:T(8,128)(2,1)}, u32[]{:S(2)}, u32[]{:S(2)}) collective-permute-start(bf16[768,384]{1,0:T(8,128)(2,1)} %get-tuple-element.447), channel_id=1, source_target_pairs={{0,16},{8,24},{16,0},{24,8},{1,17},{9,25},{17,1},{25,9},{2,18},{10... | collective-permute-start | bytes 1769480 | tf_op jit(solution)/shard_map/ppermute | solution.py:602
  389.2 93.0 %collective-permute-start.66 = (bf16[768,384]{1,0:T(8,128)(2,1)}, bf16[768,384]{1,0:T(8,128)(2,1)}, u32[]{:S(2)}, u32[]{:S(2)}) collective-permute-start(bf16[768,384]{1,0:T(8,128)(2,1)} %get-tuple-element.448), channel_id=1, source_target_pairs={{0,24},{8,0},{16,8},{24,16},{1,25},{9,1},{17,9},{25,17},{2,26},{10... | collective-permute-start | bytes 1769480 | tf_op jit(solution)/shard_map/ppermute | solution.py:602
  396.7 40.3 %collective-permute-start = (bf16[2304,384]{1,0:T(8,128)(2,1)}, bf16[2304,384]{1,0:T(8,128)(2,1)}, u32[]{:S(2)}, u32[]{:S(2)}) collective-permute-start(bf16[2304,384]{1,0:T(8,128)(2,1)} %constant_dynamic-update-slice_fusion.5), channel_id=1, source_target_pairs={{0,2},{2,0},{4,6},{6,4},{1,3},{3,1},{5,7},{7,5},{8,10},{10,8},{12,... | collective-permute-start | bytes 5308424 | tf_op jit(solution)/shard_map/cond/branch_1_fun/ppermute | solution.py:593
  398.1 41.7 %collective-permute-start.1 = (bf16[2304,384]{1,0:T(8,128)(2,1)}, bf16[2304,384]{1,0:T(8,128)(2,1)}, u32[]{:S(2)}, u32[]{:S(2)}) collective-permute-start(bf16[2304,384]{1,0:T(8,128)(2,1)} %constant_dynamic-update-slice_fusion.5), channel_id=1, source_target_pairs={{0,4},{2,6},{4,0},{6,2},{1,5},{3,7},{5,1},{7,3},{8,12},{10,14},{12... | collective-permute-start | bytes 5308424 | tf_op jit(solution)/shard_map/cond/branch_1_fun/ppermute | solution.py:593
  438.2 20.3 %collective-permute-start.2 = (bf16[1152,384]{1,0:T(8,128)(2,1)S(1)}, bf16[1152,384]{1,0:T(8,128)(2,1)}, u32[]{:S(2)}, u32[]{:S(2)}) collective-permute-start(bf16[1152,384]{1,0:T(8,128)(2,1)S(1)} %slice.215), channel_id=1, source_target_pairs={{0,4},{2,6},{4,0},{6,2},{1,5},{3,7},{5,1},{7,3},{8,12},{10,14},{12... | collective-permute-start | bytes 2654216 | tf_op jit(solution)/shard_map/cond/branch_1_fun/ppermute | solution.py:593
  441.1 20.0 %collective-permute-start.3 = (bf16[1152,384]{1,0:T(8,128)(2,1)S(1)}, bf16[1152,384]{1,0:T(8,128)(2,1)}, u32[]{:S(2)}, u32[]{:S(2)}) collective-permute-start(bf16[1152,384]{1,0:T(8,128)(2,1)S(1)} %slice.216), channel_id=1, source_target_pairs={{0,2},{2,0},{4,6},{6,4},{1,3},{3,1},{5,7},{7,5},{8,10},{10,8},{12,... | collective-permute-start | bytes 2654216 | tf_op jit(solution)/shard_map/cond/branch_1_fun/ppermute | solution.py:593
  (116 other events, 1041.9 us)
Sparse Core Ops, SparseCore 0:
  70.1 70.3 all-gather.2

commit v4 on v3

--- a/solution.py
+++ b/solution.py
@@ -98,6 +98,14 @@
         ((half, width), BF),
         ((half, width), BF),
     ]
+
+
+def reduce_first_kernel(got_one, got_two, own, two_low, one_high, to_two, to_one, total):
+    half = two_low.shape[0]
+    to_two[...] = (two_low[...].astype(F32) + got_one[half:].astype(F32)).astype(BF)
+    to_one[...] = (one_high[...].astype(F32) + got_two[half:].astype(F32)).astype(BF)
+    total[:half] = own[:half].astype(F32) + got_one[:half].astype(F32)
+    total[half:] = own[half:].astype(F32) + got_two[:half].astype(F32)
 
 
 def attend_kernel(n, rows, depth, mine, head, place, freq, *refs):
@@ -440,16 +448,15 @@
         outs[k][low:] = held[p ^ plane]
 
 
-def feed_forward_kernel(n, members, depth, strip, rows, place, unit_index, *refs):
-    pieces, grad_all, refs = refs[:5], refs[5], refs[6:]
+def feed_forward_kernel(n, members, depth, strip, rows, e, place, unit_index, *refs):
+    pieces, all_grads, refs = refs[:5], refs[5], refs[6:]
     here, there, refs = refs[:n], refs[n : 2 * n], refs[2 * n :]
-    outs, scratch = refs[:15], refs[15:]
-    x, cot, hidden, grad_gate, grad_lifted, *splits = scratch[:15]
-    gate, up, down, codes, in_sems, out_sems = scratch[15:]
+    outs, scratch = refs[:14], refs[14:28]
+    splits, (x, cot, hidden, grads_two) = scratch[:10], scratch[10:]
+    gate, up, down, codes, in_sems, out_sems = refs[28:]
     z, p = place[0], place[1]
     span = n * strip
     units = span * 2 * members
-    size = 2 * rows
     started, finishing = [], []
 
     def fetch(source, target):
@@ -457,12 +464,8 @@
         copy.start()
         started.append(copy)
 
-    def flush(index, low, count):
-        copy = pltpu.make_async_copy(
-            scratch[index].at[pl.ds(low, count), :],
-            outs[index].at[pl.ds(low, count), :],
-            out_sems.at[len(finishing)],
-        )
+    def flush(index):
+        copy = pltpu.make_async_copy(scratch[index], outs[index], out_sems.at[index])
         copy.start()
         finishing.append(copy)
 
@@ -479,11 +482,8 @@
             fetch(parts[s].at[pl.ds(depth, depth), :], up.at[pl.ds(top, depth), columns])
     first = len(started)
     for r in range(members):
-        for e in range(2):
-            block = 2 * r + e
-            low = e * (rows + 16)
-            fetch(grad_all.at[p ^ r, pl.ds(low, rows), :], cot.at[pl.ds(block * rows, rows), :])
-            fetch(grad_all.at[p ^ r, pl.ds(low + rows, 16), pl.ds(0, rows)], codes.at[block])
+        fetch(all_grads.at[p ^ r, e, pl.ds(0, rows), :], cot.at[pl.ds(r * rows, rows), :])
+        fetch(all_grads.at[p ^ r, e, pl.ds(rows, 16), pl.ds(0, rows)], codes.at[r])
     for s in range(n):
         plane = lax.rem(z - s + n, n)
         for half, parts in enumerate((here, there)):
@@ -495,59 +495,65 @@
                 )
     for copy in started[:first]:
         copy.wait()
-    flush(0, 0, x.shape[0])
+    flush(10)
     row = lax.broadcasted_iota(jnp.int32, (rows, rows), 0)
     col = lax.broadcasted_iota(jnp.int32, (rows, rows), 1)
 
-    def store(value, r, parts):
-        to_one, to_two, own, two_low, one_high = parts
-        low, high = value[:rows].astype(BF), value[rows:].astype(BF)
-        if r == 0:
-            own[...] = value
-        elif r == 1:
-            to_one[:rows], one_high[...] = low, high
-        elif r == 2:
-            two_low[...], to_two[:rows] = low, high
-        else:
-            to_one[rows:], to_two[rows:] = low, high
-
-    for chunk in range(2):
-        block = slice(chunk * 2 * size, (chunk + 1) * 2 * size)
-        gate_pre = dot(x[block], gate[...])
-        lifted = dot(x[block], up[...])
-        sigmoid = jax.nn.sigmoid(gate_pre)
-        activated = gate_pre * sigmoid
-        if chunk == 0:
-            for copy in started[first:]:
-                copy.wait()
-            flush(1, 0, cot.shape[0])
-        limits = []
-        for b in range(4 * chunk, 4 * chunk + 4):
-            line = jnp.broadcast_to(codes[b].astype(F32)[:1], (rows, rows))
-            code = jnp.sum(jnp.where(row == col, line, 0.0), axis=1, keepdims=True)
-            limits.append(
-                sum(jnp.where(code == k, float(units >> (members - 1 - k)), 0.0) for k in range(members))
-            )
-        live = unit_index[:1, :] < jnp.concatenate(limits, axis=0)
-        hidden[block] = jnp.where(live, activated * lifted, 0.0).astype(BF)
-        grad_hidden = jnp.where(live, contract_cols(cot[block], down[...]), 0.0)
-        grad_gate[block] = (
-            grad_hidden * lifted * sigmoid * (1.0 + gate_pre * (1.0 - sigmoid))
-        ).astype(BF)
-        grad_lifted[block] = (grad_hidden * activated).astype(BF)
-        for index in (2, 3, 4):
-            flush(index, chunk * 2 * size, 2 * size)
-        grads = contract_cols(grad_gate[block], gate[...])
-        grads += contract_cols(grad_lifted[block], up[...])
-        for i in range(2):
-            store(grads[i * size : (i + 1) * size], 2 * chunk + i, splits[:5])
-        value = dot(hidden[block], down[...])
-        for i in range(2):
-            store(value[i * size : (i + 1) * size], 2 * chunk + i, splits[5:])
-    for index in range(5, 15):
-        flush(index, 0, scratch[index].shape[0])
+    gate_pre = dot(x[...], gate[...])
+    lifted = dot(x[...], up[...])
+    sigmoid = jax.nn.sigmoid(gate_pre)
+    activated = gate_pre * sigmoid
+    for copy in started[first:]:
+        copy.wait()
+    flush(11)
+    limits = []
+    for r in range(members):
+        line = jnp.broadcast_to(codes[r].astype(F32)[:1], (rows, rows))
+        code = jnp.sum(jnp.where(row == col, line, 0.0), axis=1, keepdims=True)
+        limits.append(
+            sum(jnp.where(code == k, float(units >> (members - 1 - k)), 0.0) for k in range(members))
+        )
+    live = unit_index[:1, :] < jnp.concatenate(limits, axis=0)
+    hidden[...] = jnp.where(live, activated * lifted, 0.0).astype(BF)
+    grad_hidden = jnp.where(live, contract_cols(cot[...], down[...]), 0.0)
+    wide = 2 * span
+    grads_two[:, :wide] = (
+        grad_hidden * lifted * sigmoid * (1.0 + gate_pre * (1.0 - sigmoid))
+    ).astype(BF)
+    grads_two[:, wide:] = (grad_hidden * activated).astype(BF)
+    flush(12)
+    flush(13)
+    grads = contract_cols(grads_two[:, :wide], gate[...])
+    grads += contract_cols(grads_two[:, wide:], up[...])
+    split_parts(grads, rows, *splits[:5])
+    for index in range(5):
+        flush(index)
+    split_parts(dot(hidden[...], down[...]), rows, *splits[5:])
+    for index in range(5, 10):
+        flush(index)
     for copy in finishing:
         copy.wait()
+
+
+def unit_sums_kernel(n, depth, strip, *refs):
+    parts, (here, there) = (refs[:4], refs[4:8]), refs[8:]
+    span = n * strip
+    for plane in range(n):
+        block = slice(plane * depth, (plane + 1) * depth)
+        made = sum(contract_rows(x[:, block], grads[...]) for x, _, _, grads in parts)
+        for k in range(2):
+            for half, out in enumerate((here, there)):
+                low = (2 * k + half) * span
+                value = made[:, low : low + span].astype(BF)
+                out[plane, k * depth : (k + 1) * depth, :] = value
+    for j in range(parts[0][1].shape[1] // span):
+        cols = slice(j * span, (j + 1) * span)
+        made = sum(contract_rows(hidden[...], cot[:, cols]) for _, cot, hidden, _ in parts)
+        made = made.astype(BF)
+        for half, out in enumerate((here, there)):
+            for plane in range(n):
+                low, at = half * span + plane * strip, 2 * depth + j * strip
+                out[plane, at : at + strip, :] = made[low : low + strip]
 
 
 def move(kernel, outs, copies, operands, ins):
@@ -558,7 +564,7 @@
         in_specs=[kinds[k] for k in ins],
         out_specs=[pl.BlockSpec(memory_space=pltpu.VMEM)] * len(outs),
         scratch_shapes=[pltpu.SemaphoreType.DMA((copies,))],
-        compiler_params=pltpu.CompilerParams(vmem_limit_bytes=16 * 2**20),
+        compiler_params=pltpu.CompilerParams(vmem_limit_bytes=56 * 2**20),
         cost_estimate=small_cost(),
     )(*operands)
 
@@ -628,15 +634,15 @@
         return plane_reduce_rest(hop(to_one, 1), hop(to_two, 2), own, two_low, one_high)
 
     def plane_reduce_rest(got_one, got_two, own, two_low, one_high):
-        half = two_low.shape[0]
-        two_low = (two_low.astype(F32) + got_one[half:].astype(F32)).astype(BF)
-        one_high = (one_high.astype(F32) + got_two[half:].astype(F32)).astype(BF)
-        low, high = hop(two_low, 2), hop(one_high, 1)
-        got = [
-            jnp.concatenate([v, w], axis=0).astype(F32)
-            for v, w in ((got_one[:half], got_two[:half]), (low, high))
-        ]
-        return own.astype(F32) + got[0] + got[1]
+        half, columns = two_low.shape
+        two_low, one_high, total = call(
+            reduce_first_kernel,
+            [((half, columns), BF), ((half, columns), BF), ((2 * half, columns), F32)],
+            (),
+            "v" * 5,
+            (got_one, got_two, own, two_low, one_high),
+        )
+        return total + jnp.concatenate([hop(two_low, 2), hop(one_high, 1)], axis=0).astype(F32)
 
     def by_member(pieces):
         out = jnp.zeros((g, *pieces[0].shape), pieces[0].dtype)
@@ -715,7 +721,7 @@
     def rows_out(first_part, token_part, grad_part):
         token_pieces = plane_gather(token_part)
         first_part, grad_part, *token_pieces = cut(first_part, grad_part, *token_pieces)
-        grad_both = jnp.concatenate([grad_part, pair(grad_part)], axis=0)
+        grad_both = jnp.stack([grad_part, pair(grad_part)])
         return token_pieces, core(first_part), grad_both, second_part(0), second_part(1)
 
     token_pieces, own_far, grad_both, even_part, odd_part = together(
@@ -724,11 +730,9 @@
     even_part, odd_part, own_far, grad_both, *first_moved = cut(
         even_part, odd_part, own_far, grad_both, *first_moved
     )
-    grad_all = lax.all_gather(grad_both, "gran", axis=0)
+    all_grads = lax.all_gather(grad_both, "gran", axis=0)
     first_pieces = [first_part, *first_moved]
-    second_here = [even_part] + [
-        ring(odd_part if k % 2 else even_part, k) for k in range(1, n)
-    ]
+    second_odd = {k: ring(odd_part, k) for k in range(1, n, 2)}
 
     all_rows = g * rows
 
@@ -737,8 +741,7 @@
         return values * inverse, inverse
 
     def attention(token_pieces, first_pieces, own_far):
-        first_far = [own_far, *(core(v) for v in first_pieces[1:3])]
-        first_far += [core(v) for v in cut(*first_pieces[3:], *first_far)[: n - 3]]
+        first_far = [own_far, *(core(v) for v in first_pieces[1:])]
         frequencies = ROPE_BASE ** (-(2.0 * jnp.arange(head // 2, dtype=F32)) / head)
         frequencies = jnp.broadcast_to(jnp.concatenate([frequencies, frequencies]), (8, head))
         all_normed, my_qkv, queries, keys, values, attended, cosines, sines, bias, gains = call(
@@ -775,8 +778,7 @@
             ]
             return jnp.stack(picked)
 
-        out_pieces = [out_part_for(0)] + [hop(out_part_for(r), r) for r in (1, 2)]
-        out_pieces.append(hop(after(out_part_for(3), attended, *out_pieces), 3))
+        out_pieces = [out_part_for(0)] + [hop(out_part_for(r), r) for r in range(1, g)]
         if hs % 8 == 0:
             [my_out] = move(
                 functools.partial(out_weight_kernel, n, g, hs, mine),
@@ -796,60 +798,82 @@
             (attended, my_out),
         )
 
-        middle = tokens.astype(F32) + plane_reduce(*attn_parts)
+        kept = (all_normed, my_qkv, my_out, queries, keys, values, attended, cosines, sines, bias)
+        return kept, gains, attn_parts
+
+    kept, gains, attn_parts = together(attention, token_pieces, first_pieces, own_far)
+    even_part, *got = cut(even_part, *attn_parts, *second_odd.values())
+    attn_parts, second_odd = got[:5], dict(zip(second_odd, got[5:]))
+    second_even = {k: ring(even_part, k) for k in range(2, n, 2)}
+
+    def attention_end(attn_parts, even_part, odd_parts):
+        to_one, to_two, *waiting = attn_parts
+        got_one, got_two, even_part, *odd_far = cut(
+            hop(to_one, 1), hop(to_two, 2), even_part, *(core(v) for v in odd_parts)
+        )
+        reduced, own_far = cut(plane_reduce_rest(got_one, got_two, *waiting), core(even_part))
+        middle = tokens.astype(F32) + reduced
         unit_second, inverse_second = unit(middle)
         normed_ffn = (unit_second * gains[8:9]).astype(BF)
-        both_rows = jnp.concatenate([normed_ffn, pair(normed_ffn)], axis=0)
-        kept = (all_normed, my_qkv, my_out, queries, keys, values, attended, cosines, sines, bias)
-        return kept, gains, middle, unit_second, inverse_second, both_rows
-
-    kept, gains, middle, unit_second, inverse_second, both_rows = together(
-        attention, token_pieces, first_pieces, own_far
+        far_rows = pair(normed_ffn)
+        own_pieces = plane_gather(normed_ffn)
+        return middle, unit_second, inverse_second, own_pieces, gather_first(far_rows), own_far, odd_far
+
+    middle, unit_second, inverse_second, own_pieces, far_pieces, own_far, odd_far = together(
+        attention_end, attn_parts, even_part, list(second_odd.values())
     )
     all_normed, my_qkv, my_out, queries, keys, values, attended, cosines, sines, bias = kept
     gain_first, gain_second = gains[0:1], gains[8:9]
     residual = tokens.astype(F32)
-    both_rows, grad_all, *second_here = cut(both_rows, grad_all, *second_here)
-    row_pieces = plane_gather(both_rows)
-    second_far = [core(v) for v in second_here]
+    *got, all_grads = cut(*own_pieces, *far_pieces, *second_even.values(), all_grads)
+    own_pieces, far_pieces, second_even = got[:5], got[5:8], dict(zip(second_even, got[8:]))
+    odd_far = dict(zip(second_odd, odd_far))
+    even_far = {k: core(v) for k, v in second_even.items()}
+    second_here = {0: even_part, **second_odd, **second_even}
+    second_far = {0: own_far, **odd_far, **even_far}
+    second_here = [second_here[k] for k in range(n)]
+    second_far = [second_far[k] for k in range(n)]
 
     index = jnp.arange(2 * span, dtype=jnp.int32) % span
     unit_index = (index // strip) * (strip * shares) + share * strip + index % strip
-    pair_rows = 2 * all_rows
-    if strip % 16 == 0:
-        shapes = [((pair_rows, width), BF)] * 2 + [((pair_rows, 2 * span), BF)] * 3
-        shapes += split_shapes(2 * rows, width) * 2
-        group_rows, group_grads, hidden, grad_gate, grad_lifted, *parts = call(
-            functools.partial(feed_forward_kernel, n, g, depth, strip, rows),
-            shapes,
-            [pltpu.VMEM(*v) for v in shapes]
-            + [
-                pltpu.VMEM((width, 2 * span), BF),
-                pltpu.VMEM((width, 2 * span), BF),
-                pltpu.VMEM((2 * span, width), BF),
-                pltpu.VMEM((2 * g, 16, rows), BF),
-                pltpu.SemaphoreType.DMA((5 + 2 * n * (2 + cuts) + 4 * g,)),
-                pltpu.SemaphoreType.DMA((18,)),
-            ],
-            "sv" + "h" * (6 + 2 * n),
-            (
-                place,
-                jnp.broadcast_to(unit_index.astype(F32), (8, 2 * span)),
-                *row_pieces,
-                grad_all,
-                *second_here,
-                *second_far,
-            ),
-            out="h",
-        )
-        input_parts, partial_ffn = parts[:5], parts[5:]
-    else:
+    fast_units = strip % 16 == 0
+
+    def feed_forward(e, row_pieces):
+        if fast_units:
+            shapes = split_shapes(rows, width) * 2
+            shapes += [((all_rows, width), BF)] * 2
+            shapes += [((all_rows, 2 * span), BF), ((all_rows, 4 * span), BF)]
+            got = call(
+                functools.partial(feed_forward_kernel, n, g, depth, strip, rows, e),
+                shapes,
+                [pltpu.VMEM(*v) for v in shapes]
+                + [
+                    pltpu.VMEM((width, 2 * span), BF),
+                    pltpu.VMEM((width, 2 * span), BF),
+                    pltpu.VMEM((2 * span, width), BF),
+                    pltpu.VMEM((g, 16, rows), BF),
+                    pltpu.SemaphoreType.DMA((5 + 2 * n * (2 + cuts) + 2 * g,)),
+                    pltpu.SemaphoreType.DMA((14,)),
+                ],
+                "sv" + "h" * (6 + 2 * n),
+                (
+                    place,
+                    jnp.broadcast_to(unit_index.astype(F32), (8, 2 * span)),
+                    *row_pieces,
+                    all_grads,
+                    *second_here,
+                    *second_far,
+                ),
+                out="h",
+                spare=16,
+            )
+            return got[:5], got[5:10], got[10:]
         group_rows = jnp.concatenate(row_pieces, axis=0)
         stacks = []
         for pieces in (second_here, second_far):
             out = jnp.zeros((n, *pieces[0].shape), BF)
-            for s in range(n):
-                out = lax.dynamic_update_index_in_dim(out, pieces[s], (z - s) % n, 0)
+            for k in range(n):
+                out = lax.dynamic_update_index_in_dim(out, pieces[k], (z - k) % n, 0)
             stacks.append(out)
         gate_matrix, up_matrix = (
             jnp.concatenate(
@@ -862,10 +886,10 @@
             axis=0,
         ).reshape(2 * span, width)
         grad_got = jnp.stack(
-            [lax.dynamic_index_in_dim(grad_all, p ^ r, 0, keepdims=False) for r in range(g)]
-        ).reshape(g, 2, rows + 16, width)
-        group_grads = grad_got[:, :, :rows].reshape(2 * g * rows, width)
-        group_codes = grad_got[:, :, rows, :rows].reshape(2 * g * rows, 1).astype(jnp.int32)
+            [lax.dynamic_index_in_dim(all_grads, p ^ r, 0, keepdims=False)[e] for r in range(g)]
+        )
+        group_grads = grad_got[:, :rows].reshape(all_rows, width)
+        group_codes = grad_got[:, rows, :rows].reshape(all_rows, 1).astype(jnp.int32)
         group_limits = jnp.where(
             group_codes < 0, 0, jnp.right_shift(jnp.int32(units), jnp.minimum(3 - group_codes, 3))
         )
@@ -883,39 +907,73 @@
         partial_input = (
             contract_cols(grad_gate, gate_matrix) + contract_cols(grad_lifted, up_matrix)
         ).astype(BF)
-        input_parts = split_rows(partial_input.reshape(g, 2 * rows, width))
-        partial_ffn = split_rows(dot(hidden, down_matrix).astype(BF).reshape(g, 2 * rows, width))
-
-    def unit_grads(half):
-        low = slice(half * span, (half + 1) * span)
+        partial_ffn = dot(hidden, down_matrix).astype(BF)
         return (
-            contract_rows(group_rows, grad_gate[:, low]),
-            contract_rows(group_rows, grad_lifted[:, low]),
-            contract_rows(hidden[:, low], group_grads),
-        )
-
-    to_one, to_two, *waiting = input_parts
-    got = cut(hop(to_one, 1), hop(to_two, 2), *(v.astype(BF) for v in unit_grads(1)))
-    reduced = plane_reduce_rest(*got[:2], *waiting)
-    gate_sum, up_sum, down_sum = (
-        (v + core(w).astype(F32)).astype(BF) for v, w in zip(unit_grads(0), got[2:])
+            list(split_rows(partial_input.reshape(g, rows, width))),
+            list(split_rows(partial_ffn.reshape(g, rows, width))),
+            [group_rows, group_grads, hidden, jnp.concatenate([grad_gate, grad_lifted], axis=1)],
+        )
+
+    def unit_grads(own, far):
+        if fast_units:
+            return call(
+                functools.partial(unit_sums_kernel, n, depth, strip),
+                [((n, 2 * depth + cuts * strip, span), BF)] * 2,
+                (),
+                "v" * 8,
+                (*own, *far),
+            )
+        group_rows, group_grads, hidden, grads_two = (
+            jnp.concatenate([v, w], axis=0) for v, w in zip(own, far)
+        )
+
+        def half_grads(half):
+            low = slice(half * span, (half + 1) * span)
+            made = contract_rows(hidden[:, low], group_grads).astype(BF)
+            made = made.reshape(n, strip, cuts, span).transpose(0, 2, 1, 3)
+            return jnp.concatenate(
+                [
+                    contract_rows(group_rows, v[:, low]).astype(BF).reshape(n, depth, span)
+                    for v in (grads_two[:, : 2 * span], grads_two[:, 2 * span :])
+                ]
+                + [made.reshape(n, cuts * strip, span)],
+                axis=1,
+            )
+
+        return [half_grads(0), half_grads(1)]
+
+    far_pieces = gather_rest(list(far_pieces))
+    own_out = together(functools.partial(feed_forward, 0), own_pieces)
+    (own_input, own_ffn, own_saved), far_pieces = cut(own_out, far_pieces)
+    to_one, to_two, *own_waiting = own_input
+    own_got, (far_input, far_ffn, far_saved) = cut(
+        (hop(to_one, 1), hop(to_two, 2)), together(functools.partial(feed_forward, 1), far_pieces)
     )
-    halves, gate_sum, up_sum, down_sum = cut(reduced, gate_sum, up_sum, down_sum)
-    gate_sum = gate_sum.reshape(n, depth, span)
-    up_sum = up_sum.reshape(n, depth, span)
-    down_sum = down_sum.reshape(n, strip, cuts, span)
+    to_one, to_two, *far_waiting = far_input
+    own_half, far_got, (sums_here, sums_there) = cut(
+        plane_reduce_rest(*own_got, *own_waiting),
+        (hop(to_one, 1), hop(to_two, 2)),
+        together(unit_grads, own_saved, far_saved),
+    )
+    far_sum, far_sums = cut(plane_reduce_rest(*far_got, *far_waiting), core(sums_there))
 
     def unit_sums(k):
-        own = lax.dynamic_index_in_dim(down_sum, k, 0, keepdims=False).transpose(1, 0, 2)
-        return jnp.concatenate(
-            [lax.dynamic_index_in_dim(v, k, 0, keepdims=False) for v in (gate_sum, up_sum)]
-            + [own.reshape(cuts * strip, span)],
-            axis=0,
-        )
-
-    own_half, far_half = halves[:rows], pair(halves[rows:].astype(BF))
-    to_one, to_two, *branch_waiting = partial_ffn
-    to_one, to_two = cut(to_one, to_two, halves)[:2]
+        here, there = (
+            lax.dynamic_index_in_dim(v, k, 0, keepdims=False).astype(F32)
+            for v in (sums_here, far_sums)
+        )
+        return (here + there).astype(BF)
+
+    def mixed(own, far):
+        half = own.shape[0] // 2
+        return jnp.concatenate([own[:half], far[:half], own[half:], far[half:]], axis=0)
+
+    far_half = pair(far_sum.astype(BF))
+    to_one, to_two, branch_own = (mixed(v, w) for v, w in zip(own_ffn[:3], far_ffn[:3]))
+    branch_waiting = [branch_own] + [
+        jnp.concatenate([v, w], axis=0) for v, w in zip(own_ffn[3:], far_ffn[3:])
+    ]
+    to_one, to_two = cut(to_one, to_two, far_sum)[:2]
     branch_got = hop(to_one, 1), hop(to_two, 2)
     messages = [unit_sums((z + k) % n) for k in range(n)]
     far_half, branch_got, *messages = cut(far_half, branch_got, *messages)
@@ -948,6 +1006,8 @@
             out_sum = (out_here.astype(F32) + out_there.astype(F32)).astype(BF)
         got_one, got_two, *branch_pieces = cut(*branch_got, *branch_pieces)
         branch_sum = plane_reduce_rest(got_one, got_two, *branch_waiting)
+        branch_sum = branch_sum.reshape(2, 2, rows // 2, width).transpose(1, 0, 2, 3)
+        branch_sum = branch_sum.reshape(2 * rows, width)
         grad_branch, grad_packed, *normed_parts = call(
             functools.partial(attend_back_kernel, rows, mine, head),
             [((all_rows, width), BF), ((all_rows, 3 * mine), BF), *split_shapes(rows, width)],
@@ -997,9 +1057,15 @@
             last_parts = [
                 lax.dynamic_index_in_dim(last_part, (z + k) % n, 0, keepdims=False) for k in range(n)
             ]
-        return grad_middle, normed_parts, last_parts, branch_sum
-
-    grad_middle, normed_parts, last_parts, branch_sum = together(
+        normed_parts = cut(*normed_parts, *last_parts)[:5]
+        grad_normed = plane_reduce(*normed_parts)
+        unit_first, inverse_first = unit(residual)
+        input_grad = (
+            grad_middle + norm_back(grad_normed, unit_first, inverse_first, gain_first)
+        ).astype(BF)
+        return input_grad, last_parts, branch_sum
+
+    input_grad, last_parts, branch_sum = together(
         attention_back, own_half, far_half, branch_got
     )
     cut_values = cut(*moved, *last_parts)
@@ -1009,17 +1075,10 @@
     even_sum, odd_sum = (v.astype(BF) for v in sums)
     last_moved = [ring(last_parts[k], k) for k in range(1, n)]
 
-    def units_out(even_sum, odd_sum, normed_parts):
-        unit_pieces = plane_gather(jnp.concatenate([even_sum, odd_sum], axis=0))
-        normed_parts = cut(*normed_parts, *unit_pieces)[:5]
-        grad_normed = plane_reduce(*normed_parts)
-        unit_first, inverse_first = unit(residual)
-        input_grad = (
-            grad_middle + norm_back(grad_normed, unit_first, inverse_first, gain_first)
-        ).astype(BF)
-        return list(unit_pieces), input_grad
-
-    unit_pieces, input_grad = together(units_out, even_sum, odd_sum, normed_parts)
+    def units_out(even_sum, odd_sum):
+        return plane_gather(jnp.concatenate([even_sum, odd_sum], axis=0))
+
+    unit_pieces = together(units_out, even_sum, odd_sum)
     got = cut(*unit_pieces, *last_moved)
     unit_pieces, last_moved = got[:5], got[5:]
     last_sum = last_parts[0].astype(F32) + sum(v.astype(F32) for v in last_moved)

time: 532 us -> 481 us (0.904)
  waiting for transfers between devices: 208 us -> 170 us
  Pallas kernels: 80.4 us -> 111 us
  matrix products: 21.8 us -> 0 us
  starting transfers between devices: 104 us -> 90.5 us
  other arithmetic: 41 us -> 29.5 us
    ppermute x42 -> x50, waiting for transfers between devices: 180 us -> 147 us  [hop(): return lax.ppermute(x, 'gran', [(i, i ^ r) for i in range(g)])]
    pallas_call x9 -> x16, Pallas kernels: 76.8 us -> 105 us  [call(): pl.pallas_call(kernel, out_shape=[jax.ShapeDtypeStruct(shape, dtype) for...]
    dot_general x6 -> x0, matrix products: 21.8 us -> none  [contract_rows(): lax.dot_general(left, right, (((0,), (0,)), ((), ())), preferred_element_...]
    ppermute x12, starting transfers between devices: 48.5 us -> 27.2 us  [ring(): return lax.ppermute(x, 'batch', [(i, (i + s) % n) for i in range(n)])]
    ppermute x42 -> x50, starting transfers between devices: 48.4 us -> 58.4 us  [hop(): return lax.ppermute(x, 'gran', [(i, i ^ r) for i in range(g)])]
    unnamed x94 -> x62, local copies, waits for them, and re-layouts: 12.7 us -> 3.9 us
    cond x43 -> x79, local copies, waits for them, and re-layouts: 5.68 us -> 13.6 us
    concatenate x6 -> x5, other arithmetic: 6.21 us -> 0.26 us  [the longest x3 0.21 us: mixed(): jnp.concatenate([own[:half], far[:half], own[half:], far[half:]], axis=0)]
  transfers between devices with their start and end apart: 78 -> 84, of which waited for: 39 -> 33; matrix products, arithmetic and copies ran while one was open for 18% -> 15% of each run, Pallas kernels for 9% -> 21%
where the time goes in v4:
time: 481 us; the launch traced here: 475 us
  waiting for transfers between devices  170 us (35%)
  Pallas kernels  111 us (23%)
  starting transfers between devices  90.5 us (19%)
  local copies, waits for them, and re-layouts  56.4 us (12%)
  other arithmetic  29.5 us (6%)
  between operations  15.3 us (3%)
    ppermute x50, waiting for transfers between devices, hop(): return lax.ppermute(x, 'gran', [(i, i ^ r) for i in range(g)])  147 us
    pallas_call x16, Pallas kernels, call(): pl.pallas_call(kernel, out_shape=[jax.ShapeDtypeStruct(shape, dtype) for...  105 us
    ppermute x50, starting transfers between devices, hop(): return lax.ppermute(x, 'gran', [(i, i ^ r) for i in range(g)])  58.4 us
    ppermute x12, starting transfers between devices, ring(): return lax.ppermute(x, 'batch', [(i, (i + s) % n) for i in range(n)])  27.2 us
    ppermute x4, waiting for transfers between devices, pair(): return lax.ppermute(x, 'batch', [(i, i ^ 1) for i in range(n)])  19.2 us
    cond x79, local copies, waits for them, and re-layouts  13.6 us
  transfers between devices with their start and end apart: 84, of which 33 were waited for; matrix products, arithmetic and copies ran while one was open for 15% of the time, Pallas kernels for 21%

profile of v4, /device:TPU:0, one launch (start us, length us, event | category | flops | bytes accessed | tf_op | source)
XLA Modules:
  0.0 474.7 jit_solution(7705909814379983980)
XLA Ops:
  20.5 47.2 %conditional.8 = (bf16[144,1536]{1,0:T(8,128)(2,1)}, bf16[144,1536]{1,0:T(8,128)(2,1)S(1)}, bf16[144,1536]{1,0:T(8,128)(2,1)}, bf16[64,1536]{1,0:T(8,128)(2,1)},...) conditional(s32[]{:T(128)} %bitcast.33, () %tuple.91, ...), branch_computations={%region_2.3_spmd, %region_3.4_spmd} | conditional | flops 442375 | bytes 38388228 | solution.py:663
  23.5 8.4 %collective-permute-done.40 = bf16[144,1536]{1,0:T(8,128)(2,1)} collective-permute-done((bf16[144,1536]{1,0:T(8,128)(2,1)}, bf16[144,1536]{1,0:T(8,128)(2,1)}, u32[]{:S(2)}, u32[]{:S(2)}) %collective-permute-start.40) | collective-permute-done | bytes 442400 | tf_op jit(solution)/shard_map/cond/branch_1_fun/ppermute | solution.py:599
  71.8 7.3 %collective-permute-start.49 = (bf16[1152,384]{1,0:T(8,128)(2,1)}, bf16[1152,384]{1,0:T(8,128)(2,1)}, u32[]{:S(2)}, u32[]{:S(2)}) collective-permute-start(bf16[1152,384]{1,0:T(8,128)(2,1)} %copy.101), channel_id=1, source_target_pairs={{0,24},{8,0},{16,8},{24,16},{1,25},{9,1},{17,9},{25,17},{2,26},{10... | collective-permute-start | bytes 2654216 | tf_op jit(solution)/shard_map/ppermute | solution.py:608
  79.2 36.7 %conditional.9 = (bf16[512,1536]{1,0:T(8,128)(2,1)}, bf16[1536,1152]{1,0:T(8,128)(2,1)}, bf16[384,1536]{1,0:T(8,128)(2,1)}, bf16[512,384]{1,0:T(8,128)(2,1)S(1)}...) conditional(s32[]{:T(128)} %bitcast.33, () %tuple.94, ...), branch_computations={%region_4.5_spmd, %region_5.6_spmd} | conditional | flops 2949507 | bytes 28334788 | solution.py:663
  88.2 12.0 %branch_1_fun.13 = (bf16[512,1536]{1,0:T(8,128)(2,1)}, bf16[1536,1152]{1,0:T(8,128)(2,1)}, bf16[512,384]{1,0:T(8,128)(2,1)S(1)}, bf16[512,384]{1,0:T(8,128)(2,1)...) custom-call(s32[3]{0:T(128)S(1)} %get-tuple-element.211.place, ...), custom_call_target="tpu_custom_call" | custom-call | flops 1 | bytes 1 | tf_op jit(solution)/shard_map/cond/branch_1_fun/pallas_call | solution.py:70
  101.5 7.0 %collective-permute-done.5.refs_3_ = bf16[1,2,192,384]{3,2,1,0:T(8,128)(2,1)S(1)} collective-permute-done((bf16[1,2,192,384]{3,2,1,0:T(8,128)(2,1)S(1)}, bf16[1,2,192,384]{3,2,1,0:T(8,128)(2,1)S(1)}, u32[]{:S(2)}, u32[]{:S(2)}) %collective-permute-start.5) | collective-permute-done | bytes 294944 | tf_op jit(solution)/shard_map/cond/branch_1_fun/ppermute | solution.py:599
  119.3 63.8 %conditional.10 = (f32[128,1536]{1,0:T(8,128)}, f32[128,1536]{1,0:T(8,128)S(1)}, f32[128,1]{0,1:T(1,128)S(1)}, bf16[128,1536]{1,0:T(8,128)(2,1)}, bf16[128,1536]...) conditional(s32[]{:T(128)} %bitcast.33, () %tuple.90, ...), branch_computations={%region_6.7_spmd, %region_7.9_spmd} | conditional | flops 2359425 | bytes 43472172 | solution.py:663
  122.8 17.4 %collective-permute-done.10.got_one = bf16[128,1536]{1,0:T(8,128)(2,1)S(1)} collective-permute-done((bf16[128,1536]{1,0:T(8,128)(2,1)}, bf16[128,1536]{1,0:T(8,128)(2,1)S(1)}, u32[]{:S(2)}, u32[]{:S(2)}) %collective-permute-start.10) | collective-permute-done | bytes 393248 | tf_op jit(solution)/shard_map/cond/branch_1_fun/ppermute | solution.py:599
  157.8 9.4 %collective-permute-done.21 = bf16[128,1536]{1,0:T(8,128)(2,1)} collective-permute-done((bf16[128,1536]{1,0:T(8,128)(2,1)}, bf16[128,1536]{1,0:T(8,128)(2,1)}, u32[]{:S(2)}, u32[]{:S(2)}) %collective-permute-start.21) | collective-permute-done | bytes 393248 | tf_op jit(solution)/shard_map/cond/branch_1_fun/ppermute | solution.py:602
  173.3 9.8 %collective-permute-done.19 = bf16[64,1536]{1,0:T(8,128)(2,1)} collective-permute-done((bf16[64,1536]{1,0:T(8,128)(2,1)S(1)}, bf16[64,1536]{1,0:T(8,128)(2,1)}, u32[]{:S(2)}, u32[]{:S(2)}) %collective-permute-start.19) | collective-permute-done | bytes 196640 | tf_op jit(solution)/shard_map/cond/branch_1_fun/ppermute | solution.py:599
  188.6 14.9 %conditional.11 = ((bf16[128,1536]{1,0:T(8,128)(2,1)}, bf16[128,1536]{1,0:T(8,128)(2,1)}, f32[128,1536]{1,0:T(8,128)}, bf16[64,1536]{1,0:T(8,128)(2,1)}, bf16[64...) conditional(s32[]{:T(128)} %bitcast.33, () %tuple.99, ...), branch_computations={%region_9.10_spmd, %region_10.11_spmd} | conditional | flops 769 | bytes 9437336 | solution.py:663
  189.8 13.7 %branch_1_fun.17 = (bf16[128,1536]{1,0:T(8,128)(2,1)}, bf16[128,1536]{1,0:T(8,128)(2,1)}, f32[128,1536]{1,0:T(8,128)}, bf16[64,1536]{1,0:T(8,128)(2,1)}, bf16[64...) custom-call(s32[3]{0:T(128)S(1)} %get-tuple-element.260.place, ...), custom_call_target="tpu_custom_call" | custom-call | flops 1 | bytes 1 | tf_op jit(solution)/shard_map/cond/branch_1_fun/pallas_call | solution.py:70
  205.7 15.1 %conditional.12 = ((bf16[128,1536]{1,0:T(8,128)(2,1)}, bf16[128,1536]{1,0:T(8,128)(2,1)}, f32[128,1536]{1,0:T(8,128)}, bf16[64,1536]{1,0:T(8,128)(2,1)}, bf16[64...) conditional(s32[]{:T(128)} %bitcast.33, () %tuple.103, ...), branch_computations={%region_11.12_spmd, %region_12.13_spmd} | conditional | flops 769 | bytes 9437336 | solution.py:663
  207.1 13.7 %branch_1_fun.18 = (bf16[128,1536]{1,0:T(8,128)(2,1)}, bf16[128,1536]{1,0:T(8,128)(2,1)}, f32[128,1536]{1,0:T(8,128)}, bf16[64,1536]{1,0:T(8,128)(2,1)}, bf16[64...) custom-call(s32[3]{0:T(128)S(1)} %get-tuple-element.276.place, ...), custom_call_target="tpu_custom_call" | custom-call | flops 1 | bytes 1 | tf_op jit(solution)/shard_map/cond/branch_1_fun/pallas_call | solution.py:70
  226.4 15.5 %conditional.13 = ((bf16[4,1152,384]{2,1,0:T(8,128)(2,1)}, bf16[4,1152,384]{2,1,0:T(8,128)(2,1)})) conditional(s32[]{:T(128)} %bitcast.33, () %tuple.106, (bf16[512,1536]{1,0:T(8,128)(2,1)}, bf16[512,1536]{1,0:T(8,128)(2,1)}, bf16[512,768]{1,0:T(8,128)(2,1)}, bf16[512,1536]{1,0:T(8,128)(2,1)}, bf16[512,1536]{1,0:T(8,128)(2,1)}, ...), branch_computations={%region_13.14_spmd, %region_14.15_spmd} | conditional | flops 1 | bytes 7077916 | solution.py:663
  226.6 15.4 %branch_1_fun.19 = (bf16[4,1152,384]{2,1,0:T(8,128)(2,1)}, bf16[4,1152,384]{2,1,0:T(8,128)(2,1)}) custom-call(bf16[512,1536]{1,0:T(8,128)(2,1)} %get-tuple-element.292.refs_0_, bf16[512,1536]{1,0:T(8,128)(2,1)} %get-tuple-element.293.refs_1_, bf16[512,768]{1,0:T(8,128)(2,1)} %get-tuple-element.294.refs_2_, bf16[512,1536]{1,0:T(8,128)(2,1)} %get-tuple-element.295.refs_3_, ...), custom_call_target="tpu_custom_call" | custom-call | flops 1 | bytes 1 | tf_op jit(solution)/shard_map/cond/branch_1_fun/pallas_call | solution.py:70
  280.4 81.6 %conditional.14 = (bf16[128,1536]{1,0:T(8,128)(2,1)}, bf16[768,384]{1,0:T(8,128)(2,1)}, bf16[768,384]{1,0:T(8,128)(2,1)}, bf16[768,384]{1,0:T(8,128)(2,1)}, bf16...) conditional(s32[]{:T(128)} %bitcast.33, () %tuple.98, (bf16[128,1536]{1,0:T(8,128)(2,1)S(1)}, ...), branch_computations={%region_15.16_spmd, %region_16.20_spmd} | conditional | flops 14745748 | bytes 87155056 | solution.py:663
  309.7 12.4 %branch_1_fun.21 = (bf16[512,1536]{1,0:T(8,128)(2,1)}, bf16[512,1152]{1,0:T(8,128)(2,1)S(1)}, bf16[128,1536]{1,0:T(8,128)(2,1)S(1)}, bf16[128,1536]{1,0:T(8,128)...) custom-call(bf16[128,1536]{1,0:T(8,128)(2,1)S(1)} %get-tuple-element.317.refs_0_, ...), custom_call_target="tpu_custom_call" | custom-call | flops 1 | bytes 1 | tf_op jit(solution)/shard_map/cond/branch_1_fun/pallas_call | solution.py:70
  344.2 7.5 %collective-permute-done.35.got_one = bf16[128,1536]{1,0:T(8,128)(2,1)S(1)} collective-permute-done((bf16[128,1536]{1,0:T(8,128)(2,1)S(1)}, bf16[128,1536]{1,0:T(8,128)(2,1)S(1)}, u32[]{:S(2)}, u32[]{:S(2)}) %collective-permute-start.35) | collective-permute-done | bytes 393248 | tf_op jit(solution)/shard_map/cond/branch_1_fun/ppermute | solution.py:599
  370.1 59.7 %conditional.15 = (bf16[2304,384]{1,0:T(8,128)(2,1)}, bf16[2304,384]{1,0:T(8,128)(2,1)}, bf16[2304,384]{1,0:T(8,128)(2,1)}, bf16[1152,384]{1,0:T(8,128)(2,1)}, bf16[1152,384]{1,0:T(8,128)(2,1)}) conditional(s32[]{:T(128)} %bitcast.33, () %tuple.114, (bf16[1152,384]{1,0:T(8,128)(2,1)S(1)}, bf16[1152,384]{1,0:T(8,128)(2,1)S(1)}) %tuple.115), branch_computations={%region_20.21_spmd, %region_21.22_spmd} | conditional | bytes 28311752 | solution.py:663
  373.1 36.4 %collective-permute-done.6 = bf16[2304,384]{1,0:T(8,128)(2,1)} collective-permute-done((bf16[2304,384]{1,0:T(8,128)(2,1)}, bf16[2304,384]{1,0:T(8,128)(2,1)}, u32[]{:S(2)}, u32[]{:S(2)}) %collective-permute-start.6) | collective-permute-done | bytes 1769504 | tf_op jit(solution)/shard_map/cond/branch_1_fun/ppermute | solution.py:599
  413.7 15.1 %collective-permute-done.8 = bf16[1152,384]{1,0:T(8,128)(2,1)} collective-permute-done((bf16[1152,384]{1,0:T(8,128)(2,1)S(1)}, bf16[1152,384]{1,0:T(8,128)(2,1)}, u32[]{:S(2)}, u32[]{:S(2)}) %collective-permute-start.8) | collective-permute-done | bytes 884768 | tf_op jit(solution)/shard_map/cond/branch_1_fun/ppermute | solution.py:599
  435.9 13.7 %shard_map.182 = (f32[9216,128]{1,0:T(8,128)}, f32[9216,128]{1,0:T(8,128)}, f32[9216,128]{1,0:T(8,128)}, f32[384,1]{1,0:T(8,128)S(1)}) custom-call(s32[3]{0:T(128)S(1)} %pad_add_fusion.place, bf16[2304,384]{1,0:T(8,128)(2,1)} %get-tuple-element.740.refs_0_, bf16[2304,384]{1,0:T(8,128)(2,1)} %get-tuple-element.741.refs_1_, ...), custom_call_target="tpu_custom_call" | custom-call | flops 1 | bytes 1 | tf_op jit(solution)/shard_map/pallas_call | solution.py:70
  460.1 6.7 %shard_map.183 = (f32[384,4608]{1,0:T(8,128)}, f32[384,1536]{1,0:T(8,128)}, f32[384,1]{1,0:T(8,128)S(1)}) custom-call(s32[3]{0:T(128)S(1)} %pad_add_fusion.place, bf16[768,384]{1,0:T(8,128)(2,1)S(1)} %add_convert_fusion.10.refs_0_, bf16[768,384]{1,0:T(8,128)(2,1)S(1)} %collective-permute-done.73.refs_1_, ...), custom_call_target="tpu_custom_call" | custom-call | flops 1 | bytes 1 | tf_op jit(solution)/shard_map/pallas_call | solution.py:70
  (415 shorter events, 251.4 us)
Async XLA Ops:
  7.2 176.0 %all-gather.3.cloned.1.call-start = ((), (), s32[]{:S(2)}) async-start(), calls=%async_computation | async-start | bytes 4423680 | tf_op jit(solution)/shard_map/all_gather | solution.py:733
  12.1 55.6 %collective-permute-start.45 = (bf16[784,384]{1,0:T(8,128)(2,1)}, bf16[784,384]{1,0:T(8,128)(2,1)}, u32[]{:S(2)}, u32[]{:S(2)}) collective-permute-start(bf16[784,384]{1,0:T(8,128)(2,1)} %shard_map.179), channel_id=1, source_target_pairs={{0,8},{8,16},{16,24},{24,0},{1,9},{9,17},{17,25},{25,1},{2,10},{10... | collective-permute-start | bytes 1806344 | tf_op jit(solution)/shard_map/ppermute | solution.py:608
  15.2 52.5 %collective-permute-start.46 = (bf16[784,384]{1,0:T(8,128)(2,1)}, bf16[784,384]{1,0:T(8,128)(2,1)}, u32[]{:S(2)}, u32[]{:S(2)}) collective-permute-start(bf16[784,384]{1,0:T(8,128)(2,1)} %shard_map.179), channel_id=1, source_target_pairs={{0,16},{8,24},{16,0},{24,8},{1,17},{9,25},{17,1},{25,9},{2,18},{10... | collective-permute-start | bytes 1806344 | tf_op jit(solution)/shard_map/ppermute | solution.py:608
  17.8 49.9 %collective-permute-start.47 = (bf16[784,384]{1,0:T(8,128)(2,1)}, bf16[784,384]{1,0:T(8,128)(2,1)}, u32[]{:S(2)}, u32[]{:S(2)}) collective-permute-start(bf16[784,384]{1,0:T(8,128)(2,1)} %shard_map.179), channel_id=1, source_target_pairs={{0,24},{8,0},{16,8},{24,16},{1,25},{9,1},{17,9},{25,17},{2,26},{10... | collective-permute-start | bytes 1806344 | tf_op jit(solution)/shard_map/ppermute | solution.py:608
  40.9 25.6 %collective-permute-start.44 = (bf16[144,1536]{1,0:T(8,128)(2,1)S(1)}, bf16[144,1536]{1,0:T(8,128)(2,1)}, u32[]{:S(2)}, u32[]{:S(2)}) collective-permute-start(bf16[144,1536]{1,0:T(8,128)(2,1)S(1)} %copy-done.38), channel_id=1, source_target_pairs={{0,8},{8,0},{16,24},{24,16},{1,9},{9,1},{17,25},{25,17},{2,10},{10... | collective-permute-start | bytes 1327112 | tf_op jit(solution)/shard_map/cond/branch_1_fun/ppermute | solution.py:602
  69.9 46.0 %collective-permute-start.48 = (bf16[1152,384]{1,0:T(8,128)(2,1)}, bf16[1152,384]{1,0:T(8,128)(2,1)}, u32[]{:S(2)}, u32[]{:S(2)}) collective-permute-start(bf16[1152,384]{1,0:T(8,128)(2,1)} %copy.101), channel_id=1, source_target_pairs={{0,8},{8,16},{16,24},{24,0},{1,9},{9,17},{17,25},{25,1},{2,10},{10... | collective-permute-start | bytes 2654216 | tf_op jit(solution)/shard_map/ppermute | solution.py:608
  71.8 44.1 %collective-permute-start.49 = (bf16[1152,384]{1,0:T(8,128)(2,1)}, bf16[1152,384]{1,0:T(8,128)(2,1)}, u32[]{:S(2)}, u32[]{:S(2)}) collective-permute-start(bf16[1152,384]{1,0:T(8,128)(2,1)} %copy.101), channel_id=1, source_target_pairs={{0,24},{8,0},{16,8},{24,16},{1,25},{9,1},{17,9},{25,17},{2,26},{10... | collective-permute-start | bytes 2654216 | tf_op jit(solution)/shard_map/ppermute | solution.py:608
  87.0 21.5 %collective-permute-start.5 = (bf16[1,2,192,384]{3,2,1,0:T(8,128)(2,1)S(1)}, bf16[1,2,192,384]{3,2,1,0:T(8,128)(2,1)S(1)}, u32[]{:S(2)}, u32[]{:S(2)}) collective-permute-start(bf16[1,2,192,384]{3,2,1,0:T(8,128)(2,1)S(1)} %maximum_bitcast_fusion.3), channel_id=1, source_target_pairs={{0,6},{2,4},{4,2},{6,0},{1,7},{3,5},{5,3},{7,1},{8,14},{10,12},{12... | collective-permute-start | bytes 884744 | tf_op jit(solution)/shard_map/cond/branch_1_fun/ppermute | solution.py:599
  117.3 65.8 %collective-permute-start.50 = (bf16[1152,384]{1,0:T(8,128)(2,1)}, bf16[1152,384]{1,0:T(8,128)(2,1)}, u32[]{:S(2)}, u32[]{:S(2)}) collective-permute-start(bf16[1152,384]{1,0:T(8,128)(2,1)} %copy.104), channel_id=1, source_target_pairs={{0,16},{8,24},{16,0},{24,8},{1,17},{9,25},{17,1},{25,9},{2,18},{10... | collective-permute-start | bytes 2654216 | tf_op jit(solution)/shard_map/ppermute | solution.py:608
  119.3 21.7 %collective-permute-start.12 = (bf16[1152,384]{1,0:T(8,128)(2,1)}, bf16[1152,384]{1,0:T(8,128)(2,1)S(1)}, u32[]{:S(2)}, u32[]{:S(2)}) collective-permute-start(bf16[1152,384]{1,0:T(8,128)(2,1)} %get-tuple-element.244), channel_id=1, source_target_pairs={{0,1},{1,0},{2,3},{3,2},{4,5},{5,4},{6,7},{7,6},{8,9},{9,8},{10,11... | collective-permute-start | bytes 2654216 | tf_op jit(solution)/shard_map/cond/branch_1_fun/ppermute | solution.py:605
  119.4 21.7 %collective-permute-start.13 = (bf16[1152,384]{1,0:T(8,128)(2,1)}, bf16[1152,384]{1,0:T(8,128)(2,1)}, u32[]{:S(2)}, u32[]{:S(2)}) collective-permute-start(bf16[1152,384]{1,0:T(8,128)(2,1)} %get-tuple-element.245), channel_id=1, source_target_pairs={{0,1},{1,0},{2,3},{3,2},{4,5},{5,4},{6,7},{7,6},{8,9},{9,8},{10,11... | collective-permute-start | bytes 2654216 | tf_op jit(solution)/shard_map/cond/branch_1_fun/ppermute | solution.py:605
  119.9 20.3 %collective-permute-start.10 = (bf16[128,1536]{1,0:T(8,128)(2,1)}, bf16[128,1536]{1,0:T(8,128)(2,1)S(1)}, u32[]{:S(2)}, u32[]{:S(2)}) collective-permute-start(bf16[128,1536]{1,0:T(8,128)(2,1)} %get-tuple-element.241), channel_id=1, source_target_pairs={{0,2},{2,0},{4,6},{6,4},{1,3},{3,1},{5,7},{7,5},{8,10},{10,8},{12,... | collective-permute-start | bytes 1179656 | tf_op jit(solution)/shard_map/cond/branch_1_fun/ppermute | solution.py:599
  120.8 20.2 %collective-permute-start.11 = (bf16[128,1536]{1,0:T(8,128)(2,1)}, bf16[128,1536]{1,0:T(8,128)(2,1)S(1)}, u32[]{:S(2)}, u32[]{:S(2)}) collective-permute-start(bf16[128,1536]{1,0:T(8,128)(2,1)} %get-tuple-element.242), channel_id=1, source_target_pairs={{0,4},{2,6},{4,0},{6,2},{1,5},{3,7},{5,1},{7,3},{8,12},{10,14},{12... | collective-permute-start | bytes 1179656 | tf_op jit(solution)/shard_map/cond/branch_1_fun/ppermute | solution.py:599
  222.3 19.6 %collective-permute-start.56 = (bf16[64,1536]{1,0:T(8,128)(2,1)S(1)}, bf16[64,1536]{1,0:T(8,128)(2,1)S(1)}, u32[]{:S(2)}, u32[]{:S(2)}) collective-permute-start(bf16[64,1536]{1,0:T(8,128)(2,1)S(1)} %get-tuple-element.662), channel_id=1, source_target_pairs={{0,4},{2,6},{4,0},{6,2},{1,5},{3,7},{5,1},{7,3},{8,12},{10,14},{12... | collective-permute-start | bytes 589832 | tf_op jit(solution)/shard_map/ppermute | solution.py:599
  222.8 19.1 %collective-permute-start.57 = (bf16[64,1536]{1,0:T(8,128)(2,1)S(1)}, bf16[64,1536]{1,0:T(8,128)(2,1)S(1)}, u32[]{:S(2)}, u32[]{:S(2)}) collective-permute-start(bf16[64,1536]{1,0:T(8,128)(2,1)S(1)} %get-tuple-element.663), channel_id=1, source_target_pairs={{0,2},{2,0},{4,6},{6,4},{1,3},{3,1},{5,7},{7,5},{8,10},{10,8},{12,... | collective-permute-start | bytes 589832 | tf_op jit(solution)/shard_map/ppermute | solution.py:599
  224.3 19.4 %collective-permute-start.58 = (bf16[128,1536]{1,0:T(8,128)(2,1)}, bf16[128,1536]{1,0:T(8,128)(2,1)S(1)}, u32[]{:S(2)}, u32[]{:S(2)}) collective-permute-start(bf16[128,1536]{1,0:T(8,128)(2,1)} %get-tuple-element.664), channel_id=1, source_target_pairs={{0,2},{2,0},{4,6},{6,4},{1,3},{3,1},{5,7},{7,5},{8,10},{10,8},{12,... | collective-permute-start | bytes 1179656 | tf_op jit(solution)/shard_map/ppermute | solution.py:599
  275.1 86.8 %collective-permute-start.67 = (bf16[1152,384]{1,0:T(8,128)(2,1)}, bf16[1152,384]{1,0:T(8,128)(2,1)}, u32[]{:S(2)}, u32[]{:S(2)}) collective-permute-start(bf16[1152,384]{1,0:T(8,128)(2,1)} %get-tuple-element.717), channel_id=1, source_target_pairs={{0,8},{8,16},{16,24},{24,0},{1,9},{9,17},{17,25},{25,1},{2,10},{10... | collective-permute-start | bytes 2654216 | tf_op jit(solution)/shard_map/ppermute | solution.py:608
  275.2 86.8 %collective-permute-start.68 = (bf16[1152,384]{1,0:T(8,128)(2,1)}, bf16[1152,384]{1,0:T(8,128)(2,1)}, u32[]{:S(2)}, u32[]{:S(2)}) collective-permute-start(bf16[1152,384]{1,0:T(8,128)(2,1)} %get-tuple-element.718), channel_id=1, source_target_pairs={{0,16},{8,24},{16,0},{24,8},{1,17},{9,25},{17,1},{25,9},{2,18},{10... | collective-permute-start | bytes 2654216 | tf_op jit(solution)/shard_map/ppermute | solution.py:608
  278.6 83.4 %collective-permute-start.69 = (bf16[1152,384]{1,0:T(8,128)(2,1)}, bf16[1152,384]{1,0:T(8,128)(2,1)}, u32[]{:S(2)}, u32[]{:S(2)}) collective-permute-start(bf16[1152,384]{1,0:T(8,128)(2,1)} %get-tuple-element.719), channel_id=1, source_target_pairs={{0,24},{8,0},{16,8},{24,16},{1,25},{9,1},{17,9},{25,17},{2,26},{10... | collective-permute-start | bytes 2654216 | tf_op jit(solution)/shard_map/ppermute | solution.py:608
  362.0 67.8 %collective-permute-start.70 = (bf16[768,384]{1,0:T(8,128)(2,1)}, bf16[768,384]{1,0:T(8,128)(2,1)S(1)}, u32[]{:S(2)}, u32[]{:S(2)}) collective-permute-start(bf16[768,384]{1,0:T(8,128)(2,1)} %get-tuple-element.734), channel_id=1, source_target_pairs={{0,8},{8,16},{16,24},{24,0},{1,9},{9,17},{17,25},{25,1},{2,10},{10... | collective-permute-start | bytes 1769480 | tf_op jit(solution)/shard_map/ppermute | solution.py:608
  363.1 66.7 %collective-permute-start.71 = (bf16[768,384]{1,0:T(8,128)(2,1)}, bf16[768,384]{1,0:T(8,128)(2,1)S(1)}, u32[]{:S(2)}, u32[]{:S(2)}) collective-permute-start(bf16[768,384]{1,0:T(8,128)(2,1)} %get-tuple-element.735), channel_id=1, source_target_pairs={{0,16},{8,24},{16,0},{24,8},{1,17},{9,25},{17,1},{25,9},{2,18},{10... | collective-permute-start | bytes 1769480 | tf_op jit(solution)/shard_map/ppermute | solution.py:608
  364.2 65.7 %collective-permute-start.72 = (bf16[768,384]{1,0:T(8,128)(2,1)}, bf16[768,384]{1,0:T(8,128)(2,1)S(1)}, u32[]{:S(2)}, u32[]{:S(2)}) collective-permute-start(bf16[768,384]{1,0:T(8,128)(2,1)} %get-tuple-element.736), channel_id=1, source_target_pairs={{0,24},{8,0},{16,8},{24,16},{1,25},{9,1},{17,9},{25,17},{2,26},{10... | collective-permute-start | bytes 1769480 | tf_op jit(solution)/shard_map/ppermute | solution.py:608
  372.1 37.3 %collective-permute-start.6 = (bf16[2304,384]{1,0:T(8,128)(2,1)}, bf16[2304,384]{1,0:T(8,128)(2,1)}, u32[]{:S(2)}, u32[]{:S(2)}) collective-permute-start(bf16[2304,384]{1,0:T(8,128)(2,1)} %constant_dynamic-update-slice_fusion), channel_id=1, source_target_pairs={{0,2},{2,0},{4,6},{6,4},{1,3},{3,1},{5,7},{7,5},{8,10},{10,8},{12,... | collective-permute-start | bytes 5308424 | tf_op jit(solution)/shard_map/cond/branch_1_fun/ppermute | solution.py:599
  372.5 38.5 %collective-permute-start.7 = (bf16[2304,384]{1,0:T(8,128)(2,1)}, bf16[2304,384]{1,0:T(8,128)(2,1)}, u32[]{:S(2)}, u32[]{:S(2)}) collective-permute-start(bf16[2304,384]{1,0:T(8,128)(2,1)} %constant_dynamic-update-slice_fusion), channel_id=1, source_target_pairs={{0,4},{2,6},{4,0},{6,2},{1,5},{3,7},{5,1},{7,3},{8,12},{10,14},{12... | collective-permute-start | bytes 5308424 | tf_op jit(solution)/shard_map/cond/branch_1_fun/ppermute | solution.py:599
  (126 other events, 1132.7 us)
Sparse Core Ops, SparseCore 0:
  68.7 74.6 all-gather.2

commit v5 on v4

--- a/solution.py
+++ b/solution.py
@@ -293,40 +293,37 @@
     return out
 
 
-def unit_results_kernel(n, members, depth, strip, place, *refs):
+def fetch_shares(members, rows, low, count, place, pieces, target, sems):
+    z, p = place[0], place[1]
+    copies = []
+    for r in range(members):
+        for odd in range(2):
+            share = (p ^ r) * 2 + (lax.rem(z, 2) ^ odd)
+            ref, top = (pieces[r], odd * rows + low) if r < 3 else (pieces[3 + odd], low)
+            copy = pltpu.make_async_copy(
+                ref.at[pl.ds(top, count), :], target.at[share], sems.at[len(copies)]
+            )
+            copy.start()
+            copies.append(copy)
+    return copies
+
+
+def columns_results_kernel(n, members, depth, strip, rows, place, *refs):
     pieces, w_gate, w_up = refs[:5], refs[5], refs[6]
-    gate, up, down, gain, held, sems = refs[7:]
-    shares, span = 2 * members, n * strip
-    cuts = (held.shape[1] - 2 * depth) // strip
-    z, p = place[0], place[1]
-    parts = [(0, depth), (depth, depth), (2 * depth, cuts * strip)]
-    copies = []
-    for low, count in parts:
-        group = []
-        for r in range(members):
-            for odd in range(2):
-                share = (p ^ r) * 2 + (lax.rem(z, 2) ^ odd)
-                if r < 3:
-                    ref, top = pieces[r], odd * held.shape[1] + low
-                else:
-                    ref, top = pieces[3 + odd], low
-                group.append(
-                    pltpu.make_async_copy(
-                        ref.at[pl.ds(top, count), :],
-                        held.at[share, pl.ds(low, count), :],
-                        sems.at[len(copies), r * 2 + odd],
-                    )
-                )
-        for copy in group:
-            copy.start()
-        copies.append(group)
+    gate, up, gain, held_gate, held_up, sems = refs[7:]
+    shares = 2 * members
+    copies = [
+        fetch_shares(members, rows, k * depth, depth, place, pieces, held, sems.at[k])
+        for k, held in enumerate((held_gate, held_up))
+    ]
     lanes = lax.broadcasted_iota(jnp.int32, (depth, 128), 1)
     row_tiles = n * shares * strip // 128
     total = jnp.zeros((depth, 128), F32)
-    for which, (out, weight) in enumerate(((gate, w_gate), (up, w_up))):
+    for which, (out, held, weight) in enumerate(
+        ((gate, held_gate, w_gate), (up, held_up, w_up))
+    ):
         for copy in copies[which]:
             copy.wait()
-        rows = slice(which * depth, (which + 1) * depth)
         for k in range(n):
             for tile in range(shares * strip // 128):
                 made = jnp.zeros((depth, 128), F32)
@@ -335,7 +332,7 @@
                     while count > 0:
                         source, offset = divmod(column, 128)
                         some = min(count, 128 - offset)
-                        value = held[share, rows, source * 128 : (source + 1) * 128].astype(F32)
+                        value = held[share, :, source * 128 : (source + 1) * 128].astype(F32)
                         if lane != offset:
                             value = pltpu.roll(value, (lane - offset) % 128, 1)
                         made = jnp.where((lanes >= lane) & (lanes < lane + some), value, made)
@@ -344,16 +341,21 @@
                 out[pl.ds(at, depth, stride=row_tiles), :] = made
                 total += made * weight[:, at * 128 : (at + 1) * 128].astype(F32)
     gain[...] = jnp.sum(total, axis=1, keepdims=True)
-    for copy in copies[2]:
+
+
+def rows_results_kernel(n, members, depth, strip, rows, place, *refs):
+    pieces, down, held, sems = refs[:5], refs[5], refs[6], refs[7]
+    span, cuts = n * strip, (rows - 2 * depth) // strip
+    copies = fetch_shares(members, rows, 2 * depth, cuts * strip, place, pieces, held, sems)
+    for copy in copies:
         copy.wait()
     wide = cuts * span // 128
-    for share in range(shares):
+    for share in range(2 * members):
         for k in range(cuts):
-            low = 2 * depth + k * strip
             for tile in range(span // 128):
-                value = held[share, low : low + strip, tile * 128 : (tile + 1) * 128].astype(F32)
+                block = slice(k * strip, (k + 1) * strip), slice(tile * 128, (tile + 1) * 128)
                 start = share * strip * wide + k * (span // 128) + tile
-                down[pl.ds(start, strip, stride=wide), :] = value
+                down[pl.ds(start, strip, stride=wide), :] = held[(share, *block)].astype(F32)
 
 
 def attention_results_kernel(members, depth, mine, place, *refs):
@@ -536,24 +538,52 @@
 
 
 def unit_sums_kernel(n, depth, strip, *refs):
-    parts, (here, there) = (refs[:4], refs[4:8]), refs[8:]
+    given, outs, held = refs[:8], refs[8:10], refs[10:18]
+    sums, in_sems, out_sems = refs[18:20], refs[20], refs[21]
+    parts = held[:4], held[4:]
     span = n * strip
+    fetched = [
+        pltpu.make_async_copy(given[i], held[i], in_sems.at[i]) for i in (0, 3, 4, 7, 1, 2, 5, 6)
+    ]
+    for copy in fetched:
+        copy.start()
+    for copy in fetched[:4]:
+        copy.wait()
+    finishing = []
+
+    def flush(half, plane, low, count):
+        place = (plane, pl.ds(low, count), slice(None))
+        copy = pltpu.make_async_copy(
+            sums[half].at[place], outs[half].at[place], out_sems.at[len(finishing)]
+        )
+        copy.start()
+        finishing.append(copy)
+
     for plane in range(n):
         block = slice(plane * depth, (plane + 1) * depth)
         made = sum(contract_rows(x[:, block], grads[...]) for x, _, _, grads in parts)
-        for k in range(2):
-            for half, out in enumerate((here, there)):
+        for half in range(2):
+            for k in range(2):
                 low = (2 * k + half) * span
                 value = made[:, low : low + span].astype(BF)
-                out[plane, k * depth : (k + 1) * depth, :] = value
-    for j in range(parts[0][1].shape[1] // span):
+                sums[half][plane, k * depth : (k + 1) * depth, :] = value
+            flush(half, plane, 0, 2 * depth)
+    for copy in fetched[4:]:
+        copy.wait()
+    cuts = held[1].shape[1] // span
+    for j in range(cuts):
         cols = slice(j * span, (j + 1) * span)
         made = sum(contract_rows(hidden[...], cot[:, cols]) for _, cot, hidden, _ in parts)
         made = made.astype(BF)
-        for half, out in enumerate((here, there)):
+        for half in range(2):
             for plane in range(n):
                 low, at = half * span + plane * strip, 2 * depth + j * strip
-                out[plane, at : at + strip, :] = made[low : low + strip]
+                sums[half][plane, at : at + strip, :] = made[low : low + strip]
+    for half in range(2):
+        for plane in range(n):
+            flush(half, plane, 2 * depth, cuts * strip)
+    for copy in finishing:
+        copy.wait()
 
 
 def move(kernel, outs, copies, operands, ins):
@@ -631,7 +661,7 @@
         )
 
     def plane_reduce(to_one, to_two, own, two_low, one_high):
-        return plane_reduce_rest(hop(to_one, 1), hop(to_two, 2), own, two_low, one_high)
+        return summed(*plane_reduce_rest(hop(to_one, 1), hop(to_two, 2), own, two_low, one_high))
 
     def plane_reduce_rest(got_one, got_two, own, two_low, one_high):
         half, columns = two_low.shape
@@ -642,7 +672,10 @@
             "v" * 5,
             (got_one, got_two, own, two_low, one_high),
         )
-        return total + jnp.concatenate([hop(two_low, 2), hop(one_high, 1)], axis=0).astype(F32)
+        return total, hop(two_low, 2), hop(one_high, 1)
+
+    def summed(total, low, high):
+        return total + jnp.concatenate([low, high], axis=0).astype(F32)
 
     def by_member(pieces):
         out = jnp.zeros((g, *pieces[0].shape), pieces[0].dtype)
@@ -812,7 +845,7 @@
             hop(to_one, 1), hop(to_two, 2), even_part, *(core(v) for v in odd_parts)
         )
         reduced, own_far = cut(plane_reduce_rest(got_one, got_two, *waiting), core(even_part))
-        middle = tokens.astype(F32) + reduced
+        middle = tokens.astype(F32) + summed(*reduced)
         unit_second, inverse_second = unit(middle)
         normed_ffn = (unit_second * gains[8:9]).astype(BF)
         far_rows = pair(normed_ffn)
@@ -919,9 +952,13 @@
             return call(
                 functools.partial(unit_sums_kernel, n, depth, strip),
                 [((n, 2 * depth + cuts * strip, span), BF)] * 2,
-                (),
-                "v" * 8,
+                [pltpu.VMEM(v.shape, BF) for v in (*own, *far)]
+                + [pltpu.VMEM((n, 2 * depth + cuts * strip, span), BF)] * 2
+                + [pltpu.SemaphoreType.DMA((8,)), pltpu.SemaphoreType.DMA((4 * n,))],
+                "h" * 8,
                 (*own, *far),
+                out="h",
+                spare=16,
             )
         group_rows, group_grads, hidden, grads_two = (
             jnp.concatenate([v, w], axis=0) for v, w in zip(own, far)
@@ -956,6 +993,7 @@
         together(unit_grads, own_saved, far_saved),
     )
     far_sum, far_sums = cut(plane_reduce_rest(*far_got, *far_waiting), core(sums_there))
+    far_sum = summed(*far_sum)
 
     def unit_sums(k):
         here, there = (
@@ -987,7 +1025,7 @@
         return lax.dynamic_index_in_dim(stacked, p ^ r, axis, keepdims=False)
 
     def attention_back(own_half, far_half, branch_got):
-        grad_normed_ffn = (own_half + far_half.astype(F32)).astype(BF).astype(F32)
+        grad_normed_ffn = (summed(*own_half) + far_half.astype(F32)).astype(BF).astype(F32)
         grad_middle = out_cotangent.astype(F32) + norm_back(
             grad_normed_ffn, unit_second, inverse_second, gain_second
         )
@@ -1006,8 +1044,6 @@
             out_sum = (out_here.astype(F32) + out_there.astype(F32)).astype(BF)
         got_one, got_two, *branch_pieces = cut(*branch_got, *branch_pieces)
         branch_sum = plane_reduce_rest(got_one, got_two, *branch_waiting)
-        branch_sum = branch_sum.reshape(2, 2, rows // 2, width).transpose(1, 0, 2, 3)
-        branch_sum = branch_sum.reshape(2 * rows, width)
         grad_branch, grad_packed, *normed_parts = call(
             functools.partial(attend_back_kernel, rows, mine, head),
             [((all_rows, width), BF), ((all_rows, 3 * mine), BF), *split_shapes(rows, width)],
@@ -1072,29 +1108,26 @@
     moved, last_parts = cut_values[: n - 1], cut_values[n - 1 :]
     for k in range(1, n):
         sums[k % 2] += moved[k - 1].astype(F32)
-    even_sum, odd_sum = (v.astype(BF) for v in sums)
+    pair_sums = jnp.concatenate([v.astype(BF) for v in sums], axis=0)
     last_moved = [ring(last_parts[k], k) for k in range(1, n)]
 
-    def units_out(even_sum, odd_sum):
-        return plane_gather(jnp.concatenate([even_sum, odd_sum], axis=0))
-
-    unit_pieces = together(units_out, even_sum, odd_sum)
+    unit_pieces = together(plane_gather, pair_sums)
     got = cut(*unit_pieces, *last_moved)
     unit_pieces, last_moved = got[:5], got[5:]
     last_sum = last_parts[0].astype(F32) + sum(v.astype(F32) for v in last_moved)
     last_one = gather_first(last_sum.astype(BF))
     if strip % 32 == 0:
-        share_gate, share_up, share_down, ffn_part = call(
-            functools.partial(unit_results_kernel, n, g, depth, strip),
+        share_gate, share_up, ffn_part = call(
+            functools.partial(columns_results_kernel, n, g, depth, strip, 2 * depth + cuts * strip),
             [
                 ((depth * units // 128, 128), F32),
                 ((depth * units // 128, 128), F32),
-                ((units // n * width // 128, 128), F32),
                 ((depth, 1), F32),
             ],
             [
-                pltpu.VMEM((shares, 2 * depth + cuts * strip, span), BF),
-                pltpu.SemaphoreType.DMA((3, shares)),
+                pltpu.VMEM((shares, depth, span), BF),
+                pltpu.VMEM((shares, depth, span), BF),
+                pltpu.SemaphoreType.DMA((2, shares)),
             ],
             "s" + "h" * 5 + "vv",
             (place, *unit_pieces, w_gate[:, 0], w_up[:, 0]),
@@ -1131,8 +1164,20 @@
         )
     *last_one, ffn_part = cut(*last_one, ffn_part)
     last_pieces = gather_rest(last_one)
+    if strip % 32 == 0:
+        [share_down] = call(
+            functools.partial(rows_results_kernel, n, g, depth, strip, 2 * depth + cuts * strip),
+            [((units // n * width // 128, 128), F32)],
+            [pltpu.VMEM((shares, cuts * strip, span), BF), pltpu.SemaphoreType.DMA((shares,))],
+            "s" + "h" * 5,
+            (place, *cut(*unit_pieces, ffn_part)[:5]),
+        )
+        *last_rest, share_down = cut(*last_pieces[3:], share_down)
+        last_pieces[3:] = last_rest
     share_gain_ffn = (ffn_part + core(ffn_part)) / gain_ffn.astype(F32)
-    branch_ffn = branch_sum[:rows] + pair(branch_sum[rows:].astype(BF)).astype(F32)
+    branch_sum = summed(*branch_sum).reshape(2, 2, rows // 2, width)
+    branch_ffn, branch_far = (branch_sum[:, k].reshape(rows, width) for k in (0, 1))
+    branch_ffn += pair(branch_far.astype(BF)).astype(F32)
     outputs = (middle + branch_ffn.astype(BF).astype(F32)).astype(BF)
     if hs % 16 == 0:
         share_qkv, share_out, attn_part = call(

time: 481 us -> 476 us (0.990)
  local copies, waits for them, and re-layouts: 56.4 us -> 46 us
  waiting for transfers between devices: 170 us -> 176 us
    ppermute x4, waiting for transfers between devices: 19.2 us -> 25.5 us  [pair(): return lax.ppermute(x, 'batch', [(i, i ^ 1) for i in range(n)])]
    cond x79 -> x57, local copies, waits for them, and re-layouts: 13.6 us -> 8.96 us
    pallas_call x16 -> x17, Pallas kernels: 105 us -> 103 us  [call(): pl.pallas_call(kernel, out_shape=[jax.ShapeDtypeStruct(shape, dtype) for...]
  transfers between devices with their start and end apart: 84 -> 84, of which waited for: 33 -> 33; matrix products, arithmetic and copies ran while one was open for 15% -> 14% of each run, Pallas kernels for 21% -> 21%
where the time goes in v5:
time: 476 us; the launch traced here: 470 us
  waiting for transfers between devices  176 us (37%)
  Pallas kernels  109 us (23%)
  starting transfers between devices  90.8 us (19%)
  local copies, waits for them, and re-layouts  46 us (10%)
  other arithmetic  31 us (7%)
  between operations  15.3 us (3%)
    ppermute x50, waiting for transfers between devices, hop(): return lax.ppermute(x, 'gran', [(i, i ^ r) for i in range(g)])  148 us
    pallas_call x17, Pallas kernels, call(): pl.pallas_call(kernel, out_shape=[jax.ShapeDtypeStruct(shape, dtype) for...  103 us
    ppermute x50, starting transfers between devices, hop(): return lax.ppermute(x, 'gran', [(i, i ^ r) for i in range(g)])  57.5 us
    ppermute x12, starting transfers between devices, ring(): return lax.ppermute(x, 'batch', [(i, (i + s) % n) for i in range(n)])  28.2 us
    ppermute x4, waiting for transfers between devices, pair(): return lax.ppermute(x, 'batch', [(i, i ^ 1) for i in range(n)])  25.5 us
  transfers between devices with their start and end apart: 84, of which 33 were waited for; matrix products, arithmetic and copies ran while one was open for 14% of the time, Pallas kernels for 21%

profile of v5, /device:TPU:0, one launch (start us, length us, event | category | flops | bytes accessed | tf_op | source)
XLA Modules:
  0.0 470.3 jit_solution(8615391156277713516)
XLA Ops:
  20.5 48.1 %conditional.8 = (bf16[144,1536]{1,0:T(8,128)(2,1)}, bf16[144,1536]{1,0:T(8,128)(2,1)}, bf16[144,1536]{1,0:T(8,128)(2,1)}, bf16[64,1536]{1,0:T(8,128)(2,1)}, bf1...) conditional(s32[]{:T(128)} %bitcast.29, () %tuple.93, ...), branch_computations={%region_2.3_spmd, %region_3.4_spmd} | conditional | flops 442375 | bytes 31900052 | solution.py:696
  23.5 8.4 %collective-permute-done.40 = bf16[144,1536]{1,0:T(8,128)(2,1)} collective-permute-done((bf16[144,1536]{1,0:T(8,128)(2,1)}, bf16[144,1536]{1,0:T(8,128)(2,1)}, u32[]{:S(2)}, u32[]{:S(2)}) %collective-permute-start.40) | collective-permute-done | bytes 442400 | tf_op jit(solution)/shard_map/cond/branch_1_fun/ppermute | solution.py:629
  57.1 9.3 %collective-permute-done.44 = bf16[144,1536]{1,0:T(8,128)(2,1)} collective-permute-done((bf16[144,1536]{1,0:T(8,128)(2,1)}, bf16[144,1536]{1,0:T(8,128)(2,1)}, u32[]{:S(2)}, u32[]{:S(2)}) %collective-permute-start.44) | collective-permute-done | bytes 442400 | tf_op jit(solution)/shard_map/cond/branch_1_fun/ppermute | solution.py:632
  72.7 7.8 %collective-permute-start.49 = (bf16[1152,384]{1,0:T(8,128)(2,1)}, bf16[1152,384]{1,0:T(8,128)(2,1)}, u32[]{:S(2)}, u32[]{:S(2)}) collective-permute-start(bf16[1152,384]{1,0:T(8,128)(2,1)} %copy.105), channel_id=1, source_target_pairs={{0,24},{8,0},{16,8},{24,16},{1,25},{9,1},{17,9},{25,17},{2,26},{10... | collective-permute-start | bytes 2654216 | tf_op jit(solution)/shard_map/ppermute | solution.py:638
  80.6 35.2 %conditional.9 = (bf16[512,1536]{1,0:T(8,128)(2,1)}, bf16[1536,1152]{1,0:T(8,128)(2,1)}, bf16[384,1536]{1,0:T(8,128)(2,1)}, bf16[512,384]{1,0:T(8,128)(2,1)}, bf...) conditional(s32[]{:T(128)} %bitcast.29, () %tuple.96, ...), branch_computations={%region_4.5_spmd, %region_5.6_spmd} | conditional | flops 2949507 | bytes 24795788 | solution.py:696
  88.9 10.7 %branch_1_fun.13 = (bf16[512,1536]{1,0:T(8,128)(2,1)}, bf16[1536,1152]{1,0:T(8,128)(2,1)}, bf16[512,384]{1,0:T(8,128)(2,1)}, bf16[512,384]{1,0:T(8,128)(2,1)}, b...) custom-call(s32[3]{0:T(128)S(1)} %get-tuple-element.212.place, ...), custom_call_target="tpu_custom_call" | custom-call | flops 1 | bytes 1 | tf_op jit(solution)/shard_map/cond/branch_1_fun/pallas_call | solution.py:70
  101.7 6.9 %collective-permute-done.9.refs_3_ = bf16[1,2,192,384]{3,2,1,0:T(8,128)(2,1)S(1)} collective-permute-done((bf16[1,2,192,384]{3,2,1,0:T(8,128)(2,1)S(1)}, bf16[1,2,192,384]{3,2,1,0:T(8,128)(2,1)S(1)}, u32[]{:S(2)}, u32[]{:S(2)}) %collective-permute-start.9) | collective-permute-done | bytes 294944 | tf_op jit(solution)/shard_map/cond/branch_1_fun/ppermute | solution.py:629
  119.5 63.5 %conditional.10 = (f32[128,1536]{1,0:T(8,128)}, f32[128,1536]{1,0:T(8,128)S(1)}, f32[128,1]{0,1:T(1,128)S(1)}, bf16[128,1536]{1,0:T(8,128)(2,1)}, bf16[128,1536]...) conditional(s32[]{:T(128)} %bitcast.29, () %tuple.92, ...), branch_computations={%region_6.7_spmd, %region_7.9_spmd} | conditional | flops 2359425 | bytes 33248472 | solution.py:696
  122.6 17.8 %collective-permute-done.10.got_one = bf16[128,1536]{1,0:T(8,128)(2,1)S(1)} collective-permute-done((bf16[128,1536]{1,0:T(8,128)(2,1)}, bf16[128,1536]{1,0:T(8,128)(2,1)S(1)}, u32[]{:S(2)}, u32[]{:S(2)}) %collective-permute-start.10) | collective-permute-done | bytes 393248 | tf_op jit(solution)/shard_map/cond/branch_1_fun/ppermute | solution.py:629
  156.2 11.0 %collective-permute-done.21 = bf16[128,1536]{1,0:T(8,128)(2,1)} collective-permute-done((bf16[128,1536]{1,0:T(8,128)(2,1)}, bf16[128,1536]{1,0:T(8,128)(2,1)}, u32[]{:S(2)}, u32[]{:S(2)}) %collective-permute-start.21) | collective-permute-done | bytes 393248 | tf_op jit(solution)/shard_map/cond/branch_1_fun/ppermute | solution.py:632
  173.3 9.7 %collective-permute-done.19 = bf16[64,1536]{1,0:T(8,128)(2,1)} collective-permute-done((bf16[64,1536]{1,0:T(8,128)(2,1)S(1)}, bf16[64,1536]{1,0:T(8,128)(2,1)}, u32[]{:S(2)}, u32[]{:S(2)}) %collective-permute-start.19) | collective-permute-done | bytes 196640 | tf_op jit(solution)/shard_map/cond/branch_1_fun/ppermute | solution.py:629
  188.2 15.8 %conditional.11 = ((bf16[128,1536]{1,0:T(8,128)(2,1)}, bf16[128,1536]{1,0:T(8,128)(2,1)}, f32[128,1536]{1,0:T(8,128)}, bf16[64,1536]{1,0:T(8,128)(2,1)}, bf16[64...) conditional(s32[]{:T(128)} %bitcast.29, () %tuple.101, ...), branch_computations={%region_9.10_spmd, %region_10.11_spmd} | conditional | flops 769 | bytes 9437336 | solution.py:696
  190.2 13.8 %branch_1_fun.17 = (bf16[128,1536]{1,0:T(8,128)(2,1)}, bf16[128,1536]{1,0:T(8,128)(2,1)}, f32[128,1536]{1,0:T(8,128)}, bf16[64,1536]{1,0:T(8,128)(2,1)}, bf16[64...) custom-call(s32[3]{0:T(128)S(1)} %get-tuple-element.263.place, ...), custom_call_target="tpu_custom_call" | custom-call | flops 1 | bytes 1 | tf_op jit(solution)/shard_map/cond/branch_1_fun/pallas_call | solution.py:70
  206.1 16.6 %conditional.12 = ((bf16[128,1536]{1,0:T(8,128)(2,1)}, bf16[128,1536]{1,0:T(8,128)(2,1)}, f32[128,1536]{1,0:T(8,128)}, bf16[64,1536]{1,0:T(8,128)(2,1)}, bf16[64...) conditional(s32[]{:T(128)} %bitcast.29, () %tuple.105, ...), branch_computations={%region_11.12_spmd, %region_12.13_spmd} | conditional | flops 769 | bytes 9437336 | solution.py:696
  208.8 13.9 %branch_1_fun.18 = (bf16[128,1536]{1,0:T(8,128)(2,1)}, bf16[128,1536]{1,0:T(8,128)(2,1)}, f32[128,1536]{1,0:T(8,128)}, bf16[64,1536]{1,0:T(8,128)(2,1)}, bf16[64...) custom-call(s32[3]{0:T(128)S(1)} %get-tuple-element.279.place, ...), custom_call_target="tpu_custom_call" | custom-call | flops 1 | bytes 1 | tf_op jit(solution)/shard_map/cond/branch_1_fun/pallas_call | solution.py:70
  229.1 13.1 %conditional.13 = ((bf16[4,1152,384]{2,1,0:T(8,128)(2,1)}, bf16[4,1152,384]{2,1,0:T(8,128)(2,1)})) conditional(s32[]{:T(128)} %bitcast.29, () %tuple.108, (bf16[512,1536]{1,0:T(8,128)(2,1)}, bf16[512,1536]{1,0:T(8,128)(2,1)}, bf16[512,768]{1,0:T(8,128)(2,1)}, bf16[512,1536]{1,0:T(8,128)(2,1)}, bf16[512,1536]{1,0:T(8,128)(2,1)}, ...), branch_computations={%region_13.14_spmd, %region_14.15_spmd} | conditional | flops 1 | bytes 7077916 | solution.py:696
  229.3 12.9 %branch_1_fun.19 = (bf16[4,1152,384]{2,1,0:T(8,128)(2,1)}, bf16[4,1152,384]{2,1,0:T(8,128)(2,1)}) custom-call(bf16[512,1536]{1,0:T(8,128)(2,1)} %get-tuple-element.295.refs_0_, bf16[512,1536]{1,0:T(8,128)(2,1)} %get-tuple-element.296.refs_1_, bf16[512,768]{1,0:T(8,128)(2,1)} %get-tuple-element.297.refs_2_, bf16[512,1536]{1,0:T(8,128)(2,1)} %get-tuple-element.298.refs_3_, ...), custom_call_target="tpu_custom_call" | custom-call | flops 1 | bytes 1 | tf_op jit(solution)/shard_map/cond/branch_1_fun/pallas_call | solution.py:70
  278.5 79.0 %conditional.14 = (bf16[128,1536]{1,0:T(8,128)(2,1)}, bf16[768,384]{1,0:T(8,128)(2,1)}, bf16[768,384]{1,0:T(8,128)(2,1)}, bf16[768,384]{1,0:T(8,128)(2,1)}, bf16...) conditional(s32[]{:T(128)} %bitcast.29, () %tuple.100, ...), branch_computations={%region_15.16_spmd, %region_16.20_spmd} | conditional | flops 14549140 | bytes 76152016 | solution.py:696
  307.2 12.5 %branch_1_fun.21 = (bf16[512,1536]{1,0:T(8,128)(2,1)}, bf16[512,1152]{1,0:T(8,128)(2,1)S(1)}, bf16[128,1536]{1,0:T(8,128)(2,1)S(1)}, bf16[128,1536]{1,0:T(8,128)...) custom-call(bf16[128,1536]{1,0:T(8,128)(2,1)S(1)} %get-tuple-element.322.refs_0_, ...), custom_call_target="tpu_custom_call" | custom-call | flops 1 | bytes 1 | tf_op jit(solution)/shard_map/cond/branch_1_fun/pallas_call | solution.py:70
  339.8 7.6 %collective-permute-done.35.got_one = bf16[128,1536]{1,0:T(8,128)(2,1)S(1)} collective-permute-done((bf16[128,1536]{1,0:T(8,128)(2,1)S(1)}, bf16[128,1536]{1,0:T(8,128)(2,1)S(1)}, u32[]{:S(2)}, u32[]{:S(2)}) %collective-permute-start.35) | collective-permute-done | bytes 393248 | tf_op jit(solution)/shard_map/cond/branch_1_fun/ppermute | solution.py:629
  365.8 56.6 %conditional.15 = (bf16[2304,384]{1,0:T(8,128)(2,1)S(1)}, bf16[2304,384]{1,0:T(8,128)(2,1)}, bf16[2304,384]{1,0:T(8,128)(2,1)}, bf16[1152,384]{1,0:T(8,128)(2,1)}, bf16[1152,384]{1,0:T(8,128)(2,1)}) conditional(s32[]{:T(128)} %bitcast.29, () %tuple.116, bf16[2304,384]{1,0:T(8,128)(2,1)S(1)} %pad_maximum_fusion.5), branch_computations={%region_20.21_spmd, %region_21.22_spmd} | conditional | bytes 35389668 | solution.py:696
  367.5 35.5 %collective-permute-done = bf16[2304,384]{1,0:T(8,128)(2,1)S(1)} collective-permute-done((bf16[2304,384]{1,0:T(8,128)(2,1)S(1)}, bf16[2304,384]{1,0:T(8,128)(2,1)S(1)}, u32[]{:S(2)}, u32[]{:S(2)}) %collective-permute-start) | collective-permute-done | bytes 1769504 | tf_op jit(solution)/shard_map/cond/branch_1_fun/ppermute | solution.py:629
  408.6 13.8 %collective-permute-done.2 = bf16[1152,384]{1,0:T(8,128)(2,1)} collective-permute-done((bf16[1152,384]{1,0:T(8,128)(2,1)S(1)}, bf16[1152,384]{1,0:T(8,128)(2,1)}, u32[]{:S(2)}, u32[]{:S(2)}) %collective-permute-start.2) | collective-permute-done | bytes 884768 | tf_op jit(solution)/shard_map/cond/branch_1_fun/ppermute | solution.py:629
  430.4 10.9 %shard_map.182 = (f32[9216,128]{1,0:T(8,128)}, f32[9216,128]{1,0:T(8,128)}, f32[384,1]{1,0:T(8,128)S(1)}) custom-call(s32[3]{0:T(128)S(1)} %pad_add_fusion.place, bf16[2304,384]{1,0:T(8,128)(2,1)} %copy-done.8, bf16[2304,384]{1,0:T(8,128)(2,1)S(1)} %copy-done.6, bf16[2304,384]{1,0:T(8,128)(2,1)} %get-tuple-element.776.refs_2_, ...), custom_call_target="tpu_custom_call" | custom-call | flops 1 | bytes 1 | tf_op jit(solution)/shard_map/pallas_call | solution.py:70
  (397 shorter events, 250.5 us)
Async XLA Ops:
  7.2 175.9 %all-gather.3.cloned.1.call-start = ((), (), s32[]{:S(2)}) async-start(), calls=%async_computation | async-start | bytes 4423680 | tf_op jit(solution)/shard_map/all_gather | solution.py:766
  12.1 56.4 %collective-permute-start.45 = (bf16[784,384]{1,0:T(8,128)(2,1)}, bf16[784,384]{1,0:T(8,128)(2,1)}, u32[]{:S(2)}, u32[]{:S(2)}) collective-permute-start(bf16[784,384]{1,0:T(8,128)(2,1)} %shard_map.179), channel_id=1, source_target_pairs={{0,8},{8,16},{16,24},{24,0},{1,9},{9,17},{17,25},{25,1},{2,10},{10... | collective-permute-start | bytes 1806344 | tf_op jit(solution)/shard_map/ppermute | solution.py:638
  15.2 53.4 %collective-permute-start.46 = (bf16[784,384]{1,0:T(8,128)(2,1)}, bf16[784,384]{1,0:T(8,128)(2,1)}, u32[]{:S(2)}, u32[]{:S(2)}) collective-permute-start(bf16[784,384]{1,0:T(8,128)(2,1)} %shard_map.179), channel_id=1, source_target_pairs={{0,16},{8,24},{16,0},{24,8},{1,17},{9,25},{17,1},{25,9},{2,18},{10... | collective-permute-start | bytes 1806344 | tf_op jit(solution)/shard_map/ppermute | solution.py:638
  17.8 50.8 %collective-permute-start.47 = (bf16[784,384]{1,0:T(8,128)(2,1)}, bf16[784,384]{1,0:T(8,128)(2,1)}, u32[]{:S(2)}, u32[]{:S(2)}) collective-permute-start(bf16[784,384]{1,0:T(8,128)(2,1)} %shard_map.179), channel_id=1, source_target_pairs={{0,24},{8,0},{16,8},{24,16},{1,25},{9,1},{17,9},{25,17},{2,26},{10... | collective-permute-start | bytes 1806344 | tf_op jit(solution)/shard_map/ppermute | solution.py:638
  41.2 25.3 %collective-permute-start.44 = (bf16[144,1536]{1,0:T(8,128)(2,1)}, bf16[144,1536]{1,0:T(8,128)(2,1)}, u32[]{:S(2)}, u32[]{:S(2)}) collective-permute-start(bf16[144,1536]{1,0:T(8,128)(2,1)} %get-tuple-element.207), channel_id=1, source_target_pairs={{0,8},{8,0},{16,24},{24,16},{1,9},{9,1},{17,25},{25,17},{2,10},{10... | collective-permute-start | bytes 1327112 | tf_op jit(solution)/shard_map/cond/branch_1_fun/ppermute | solution.py:632
  70.8 44.9 %collective-permute-start.48 = (bf16[1152,384]{1,0:T(8,128)(2,1)}, bf16[1152,384]{1,0:T(8,128)(2,1)}, u32[]{:S(2)}, u32[]{:S(2)}) collective-permute-start(bf16[1152,384]{1,0:T(8,128)(2,1)} %copy.105), channel_id=1, source_target_pairs={{0,8},{8,16},{16,24},{24,0},{1,9},{9,17},{17,25},{25,1},{2,10},{10... | collective-permute-start | bytes 2654216 | tf_op jit(solution)/shard_map/ppermute | solution.py:638
  72.7 43.0 %collective-permute-start.49 = (bf16[1152,384]{1,0:T(8,128)(2,1)}, bf16[1152,384]{1,0:T(8,128)(2,1)}, u32[]{:S(2)}, u32[]{:S(2)}) collective-permute-start(bf16[1152,384]{1,0:T(8,128)(2,1)} %copy.105), channel_id=1, source_target_pairs={{0,24},{8,0},{16,8},{24,16},{1,25},{9,1},{17,9},{25,17},{2,26},{10... | collective-permute-start | bytes 2654216 | tf_op jit(solution)/shard_map/ppermute | solution.py:638
  87.4 21.2 %collective-permute-start.9 = (bf16[1,2,192,384]{3,2,1,0:T(8,128)(2,1)S(1)}, bf16[1,2,192,384]{3,2,1,0:T(8,128)(2,1)S(1)}, u32[]{:S(2)}, u32[]{:S(2)}) collective-permute-start(bf16[1,2,192,384]{3,2,1,0:T(8,128)(2,1)S(1)} %maximum_bitcast_fusion.3), channel_id=1, source_target_pairs={{0,6},{2,4},{4,2},{6,0},{1,7},{3,5},{5,3},{7,1},{8,14},{10,12},{12... | collective-permute-start | bytes 884744 | tf_op jit(solution)/shard_map/cond/branch_1_fun/ppermute | solution.py:629
  117.1 65.9 %collective-permute-start.50 = (bf16[1152,384]{1,0:T(8,128)(2,1)}, bf16[1152,384]{1,0:T(8,128)(2,1)}, u32[]{:S(2)}, u32[]{:S(2)}) collective-permute-start(bf16[1152,384]{1,0:T(8,128)(2,1)} %copy.108), channel_id=1, source_target_pairs={{0,16},{8,24},{16,0},{24,8},{1,17},{9,25},{17,1},{25,9},{2,18},{10... | collective-permute-start | bytes 2654216 | tf_op jit(solution)/shard_map/ppermute | solution.py:638
  119.5 21.4 %collective-permute-start.12 = (bf16[1152,384]{1,0:T(8,128)(2,1)}, bf16[1152,384]{1,0:T(8,128)(2,1)}, u32[]{:S(2)}, u32[]{:S(2)}) collective-permute-start(bf16[1152,384]{1,0:T(8,128)(2,1)} %get-tuple-element.245), channel_id=1, source_target_pairs={{0,1},{1,0},{2,3},{3,2},{4,5},{5,4},{6,7},{7,6},{8,9},{9,8},{10,11... | collective-permute-start | bytes 2654216 | tf_op jit(solution)/shard_map/cond/branch_1_fun/ppermute | solution.py:635
  119.6 21.3 %collective-permute-start.13 = (bf16[1152,384]{1,0:T(8,128)(2,1)}, bf16[1152,384]{1,0:T(8,128)(2,1)}, u32[]{:S(2)}, u32[]{:S(2)}) collective-permute-start(bf16[1152,384]{1,0:T(8,128)(2,1)} %get-tuple-element.246), channel_id=1, source_target_pairs={{0,1},{1,0},{2,3},{3,2},{4,5},{5,4},{6,7},{7,6},{8,9},{9,8},{10,11... | collective-permute-start | bytes 2654216 | tf_op jit(solution)/shard_map/cond/branch_1_fun/ppermute | solution.py:635
  120.1 20.3 %collective-permute-start.10 = (bf16[128,1536]{1,0:T(8,128)(2,1)}, bf16[128,1536]{1,0:T(8,128)(2,1)S(1)}, u32[]{:S(2)}, u32[]{:S(2)}) collective-permute-start(bf16[128,1536]{1,0:T(8,128)(2,1)} %get-tuple-element.242), channel_id=1, source_target_pairs={{0,2},{2,0},{4,6},{6,4},{1,3},{3,1},{5,7},{7,5},{8,10},{10,8},{12,... | collective-permute-start | bytes 1179656 | tf_op jit(solution)/shard_map/cond/branch_1_fun/ppermute | solution.py:629
  120.7 20.2 %collective-permute-start.11 = (bf16[128,1536]{1,0:T(8,128)(2,1)}, bf16[128,1536]{1,0:T(8,128)(2,1)S(1)}, u32[]{:S(2)}, u32[]{:S(2)}) collective-permute-start(bf16[128,1536]{1,0:T(8,128)(2,1)} %get-tuple-element.243), channel_id=1, source_target_pairs={{0,4},{2,6},{4,0},{6,2},{1,5},{3,7},{5,1},{7,3},{8,12},{10,14},{12... | collective-permute-start | bytes 1179656 | tf_op jit(solution)/shard_map/cond/branch_1_fun/ppermute | solution.py:629
  184.1 19.9 %collective-permute-start.52 = (bf16[64,1536]{1,0:T(8,128)(2,1)S(1)}, bf16[64,1536]{1,0:T(8,128)(2,1)S(1)}, u32[]{:S(2)}, u32[]{:S(2)}) collective-permute-start(bf16[64,1536]{1,0:T(8,128)(2,1)S(1)} %slice.149), channel_id=1, source_target_pairs={{0,4},{2,6},{4,0},{6,2},{1,5},{3,7},{5,1},{7,3},{8,12},{10,14},{12... | collective-permute-start | bytes 589832 | tf_op jit(solution)/shard_map/ppermute | solution.py:629
  222.7 19.5 %collective-permute-start.58 = (bf16[128,1536]{1,0:T(8,128)(2,1)}, bf16[128,1536]{1,0:T(8,128)(2,1)S(1)}, u32[]{:S(2)}, u32[]{:S(2)}) collective-permute-start(bf16[128,1536]{1,0:T(8,128)(2,1)} %get-tuple-element.682), channel_id=1, source_target_pairs={{0,2},{2,0},{4,6},{6,4},{1,3},{3,1},{5,7},{7,5},{8,10},{10,8},{12,... | collective-permute-start | bytes 1179656 | tf_op jit(solution)/shard_map/ppermute | solution.py:629
  272.9 84.6 %collective-permute-start.67 = (bf16[1152,384]{1,0:T(8,128)(2,1)}, bf16[1152,384]{1,0:T(8,128)(2,1)}, u32[]{:S(2)}, u32[]{:S(2)}) collective-permute-start(bf16[1152,384]{1,0:T(8,128)(2,1)} %get-tuple-element.741), channel_id=1, source_target_pairs={{0,8},{8,16},{16,24},{24,0},{1,9},{9,17},{17,25},{25,1},{2,10},{10... | collective-permute-start | bytes 2654216 | tf_op jit(solution)/shard_map/ppermute | solution.py:638
  272.9 84.6 %collective-permute-start.68 = (bf16[1152,384]{1,0:T(8,128)(2,1)}, bf16[1152,384]{1,0:T(8,128)(2,1)}, u32[]{:S(2)}, u32[]{:S(2)}) collective-permute-start(bf16[1152,384]{1,0:T(8,128)(2,1)} %get-tuple-element.742), channel_id=1, source_target_pairs={{0,16},{8,24},{16,0},{24,8},{1,17},{9,25},{17,1},{25,9},{2,18},{10... | collective-permute-start | bytes 2654216 | tf_op jit(solution)/shard_map/ppermute | solution.py:638
  276.7 80.8 %collective-permute-start.69 = (bf16[1152,384]{1,0:T(8,128)(2,1)}, bf16[1152,384]{1,0:T(8,128)(2,1)}, u32[]{:S(2)}, u32[]{:S(2)}) collective-permute-start(bf16[1152,384]{1,0:T(8,128)(2,1)} %get-tuple-element.743), channel_id=1, source_target_pairs={{0,24},{8,0},{16,8},{24,16},{1,25},{9,1},{17,9},{25,17},{2,26},{10... | collective-permute-start | bytes 2654216 | tf_op jit(solution)/shard_map/ppermute | solution.py:638
  357.5 64.9 %collective-permute-start.70 = (bf16[768,384]{1,0:T(8,128)(2,1)}, bf16[768,384]{1,0:T(8,128)(2,1)}, u32[]{:S(2)}, u32[]{:S(2)}) collective-permute-start(bf16[768,384]{1,0:T(8,128)(2,1)} %get-tuple-element.758), channel_id=1, source_target_pairs={{0,8},{8,16},{16,24},{24,0},{1,9},{9,17},{17,25},{25,1},{2,10},{10... | collective-permute-start | bytes 1769480 | tf_op jit(solution)/shard_map/ppermute | solution.py:638
  359.4 63.0 %collective-permute-start.71 = (bf16[768,384]{1,0:T(8,128)(2,1)}, bf16[768,384]{1,0:T(8,128)(2,1)}, u32[]{:S(2)}, u32[]{:S(2)}) collective-permute-start(bf16[768,384]{1,0:T(8,128)(2,1)} %get-tuple-element.759), channel_id=1, source_target_pairs={{0,16},{8,24},{16,0},{24,8},{1,17},{9,25},{17,1},{25,9},{2,18},{10... | collective-permute-start | bytes 1769480 | tf_op jit(solution)/shard_map/ppermute | solution.py:638
  359.5 62.9 %collective-permute-start.72 = (bf16[768,384]{1,0:T(8,128)(2,1)}, bf16[768,384]{1,0:T(8,128)(2,1)}, u32[]{:S(2)}, u32[]{:S(2)}) collective-permute-start(bf16[768,384]{1,0:T(8,128)(2,1)} %get-tuple-element.760), channel_id=1, source_target_pairs={{0,24},{8,0},{16,8},{24,16},{1,25},{9,1},{17,9},{25,17},{2,26},{10... | collective-permute-start | bytes 1769480 | tf_op jit(solution)/shard_map/ppermute | solution.py:638
  365.9 37.1 %collective-permute-start = (bf16[2304,384]{1,0:T(8,128)(2,1)S(1)}, bf16[2304,384]{1,0:T(8,128)(2,1)S(1)}, u32[]{:S(2)}, u32[]{:S(2)}) collective-permute-start(bf16[2304,384]{1,0:T(8,128)(2,1)S(1)} %param.15), channel_id=1, source_target_pairs={{0,2},{2,0},{4,6},{6,4},{1,3},{3,1},{5,7},{7,5},{8,10},{10,8},{12,... | collective-permute-start | bytes 5308424 | tf_op jit(solution)/shard_map/cond/branch_1_fun/ppermute | solution.py:629
  366.3 39.0 %collective-permute-start.1 = (bf16[2304,384]{1,0:T(8,128)(2,1)S(1)}, bf16[2304,384]{1,0:T(8,128)(2,1)}, u32[]{:S(2)}, u32[]{:S(2)}) collective-permute-start(bf16[2304,384]{1,0:T(8,128)(2,1)S(1)} %param.15), channel_id=1, source_target_pairs={{0,4},{2,6},{4,0},{6,2},{1,5},{3,7},{5,1},{7,3},{8,12},{10,14},{12... | collective-permute-start | bytes 5308424 | tf_op jit(solution)/shard_map/cond/branch_1_fun/ppermute | solution.py:629
  430.0 22.3 %collective-permute-start.66 = (bf16[128,1536]{1,0:T(8,128)(2,1)}, bf16[128,1536]{1,0:T(8,128)(2,1)}, u32[]{:S(2)}, u32[]{:S(2)}) collective-permute-start(bf16[128,1536]{1,0:T(8,128)(2,1)} %bitcast.42), channel_id=1, source_target_pairs={{0,8},{8,0},{16,24},{24,16},{1,9},{9,1},{17,25},{25,17},{2,10},{10... | collective-permute-start | bytes 1179656 | tf_op jit(solution)/shard_map/ppermute | solution.py:632
  (117 other events, 1048.8 us)
Sparse Core Ops, SparseCore 0:
  68.7 74.7 all-gather.2

commit v6 on v5

--- a/solution.py
+++ b/solution.py
@@ -1014,7 +1014,7 @@
     to_one, to_two = cut(to_one, to_two, far_sum)[:2]
     branch_got = hop(to_one, 1), hop(to_two, 2)
     messages = [unit_sums((z + k) % n) for k in range(n)]
-    far_half, branch_got, *messages = cut(far_half, branch_got, *messages)
+    far_half, *messages = cut(far_half, *messages)
     sums = [messages[0].astype(F32), 0.0]
     moved = [ring(messages[k], k) for k in range(1, n)]
 

time: 476 us -> 474 us (level)
  no operation moved by 1% of the time
where the time goes in v6:
time: 474 us; the launch traced here: 469 us
  waiting for transfers between devices  174 us (37%)
  Pallas kernels  109 us (23%)
  starting transfers between devices  90.3 us (19%)
  local copies, waits for them, and re-layouts  47.2 us (10%)
  other arithmetic  30.9 us (7%)
  between operations  15.3 us (3%)
    ppermute x50, waiting for transfers between devices, hop(): return lax.ppermute(x, 'gran', [(i, i ^ r) for i in range(g)])  147 us
    pallas_call x17, Pallas kernels, call(): pl.pallas_call(kernel, out_shape=[jax.ShapeDtypeStruct(shape, dtype) for...  103 us
    ppermute x50, starting transfers between devices, hop(): return lax.ppermute(x, 'gran', [(i, i ^ r) for i in range(g)])  55.4 us
    ppermute x12, starting transfers between devices, ring(): return lax.ppermute(x, 'batch', [(i, (i + s) % n) for i in range(n)])  30.3 us
    ppermute x4, waiting for transfers between devices, pair(): return lax.ppermute(x, 'batch', [(i, i ^ 1) for i in range(n)])  23.9 us
  transfers between devices with their start and end apart: 84, of which 33 were waited for; matrix products, arithmetic and copies ran while one was open for 14% of the time, Pallas kernels for 21%

profile of v6, /device:TPU:0, one launch (start us, length us, event | category | flops | bytes accessed | tf_op | source)
XLA Modules:
  0.0 468.6 jit_solution(10755596856968250429)
XLA Ops:
  20.5 48.1 %conditional.8 = (bf16[144,1536]{1,0:T(8,128)(2,1)}, bf16[144,1536]{1,0:T(8,128)(2,1)}, bf16[144,1536]{1,0:T(8,128)(2,1)}, bf16[64,1536]{1,0:T(8,128)(2,1)}, bf1...) conditional(s32[]{:T(128)} %bitcast.29, () %tuple.93, ...), branch_computations={%region_2.3_spmd, %region_3.4_spmd} | conditional | flops 442375 | bytes 31900052 | solution.py:696
  23.5 8.4 %collective-permute-done.40 = bf16[144,1536]{1,0:T(8,128)(2,1)} collective-permute-done((bf16[144,1536]{1,0:T(8,128)(2,1)}, bf16[144,1536]{1,0:T(8,128)(2,1)}, u32[]{:S(2)}, u32[]{:S(2)}) %collective-permute-start.40) | collective-permute-done | bytes 442400 | tf_op jit(solution)/shard_map/cond/branch_1_fun/ppermute | solution.py:629
  57.1 9.3 %collective-permute-done.44 = bf16[144,1536]{1,0:T(8,128)(2,1)} collective-permute-done((bf16[144,1536]{1,0:T(8,128)(2,1)}, bf16[144,1536]{1,0:T(8,128)(2,1)}, u32[]{:S(2)}, u32[]{:S(2)}) %collective-permute-start.44) | collective-permute-done | bytes 442400 | tf_op jit(solution)/shard_map/cond/branch_1_fun/ppermute | solution.py:632
  72.7 7.8 %collective-permute-start.49 = (bf16[1152,384]{1,0:T(8,128)(2,1)}, bf16[1152,384]{1,0:T(8,128)(2,1)}, u32[]{:S(2)}, u32[]{:S(2)}) collective-permute-start(bf16[1152,384]{1,0:T(8,128)(2,1)} %copy.105), channel_id=1, source_target_pairs={{0,24},{8,0},{16,8},{24,16},{1,25},{9,1},{17,9},{25,17},{2,26},{10... | collective-permute-start | bytes 2654216 | tf_op jit(solution)/shard_map/ppermute | solution.py:638
  80.6 35.2 %conditional.9 = (bf16[512,1536]{1,0:T(8,128)(2,1)}, bf16[1536,1152]{1,0:T(8,128)(2,1)}, bf16[384,1536]{1,0:T(8,128)(2,1)}, bf16[512,384]{1,0:T(8,128)(2,1)}, bf...) conditional(s32[]{:T(128)} %bitcast.29, () %tuple.96, ...), branch_computations={%region_4.5_spmd, %region_5.6_spmd} | conditional | flops 2949507 | bytes 24795788 | solution.py:696
  88.9 10.7 %branch_1_fun.13 = (bf16[512,1536]{1,0:T(8,128)(2,1)}, bf16[1536,1152]{1,0:T(8,128)(2,1)}, bf16[512,384]{1,0:T(8,128)(2,1)}, bf16[512,384]{1,0:T(8,128)(2,1)}, b...) custom-call(s32[3]{0:T(128)S(1)} %get-tuple-element.212.place, ...), custom_call_target="tpu_custom_call" | custom-call | flops 1 | bytes 1 | tf_op jit(solution)/shard_map/cond/branch_1_fun/pallas_call | solution.py:70
  119.5 63.5 %conditional.10 = (f32[128,1536]{1,0:T(8,128)}, f32[128,1536]{1,0:T(8,128)S(1)}, f32[128,1]{0,1:T(1,128)S(1)}, bf16[128,1536]{1,0:T(8,128)(2,1)}, bf16[128,1536]...) conditional(s32[]{:T(128)} %bitcast.29, () %tuple.92, ...), branch_computations={%region_6.7_spmd, %region_7.9_spmd} | conditional | flops 2359425 | bytes 33248472 | solution.py:696
  122.6 17.8 %collective-permute-done.10.got_one = bf16[128,1536]{1,0:T(8,128)(2,1)S(1)} collective-permute-done((bf16[128,1536]{1,0:T(8,128)(2,1)}, bf16[128,1536]{1,0:T(8,128)(2,1)S(1)}, u32[]{:S(2)}, u32[]{:S(2)}) %collective-permute-start.10) | collective-permute-done | bytes 393248 | tf_op jit(solution)/shard_map/cond/branch_1_fun/ppermute | solution.py:629
  156.2 10.9 %collective-permute-done.21 = bf16[128,1536]{1,0:T(8,128)(2,1)} collective-permute-done((bf16[128,1536]{1,0:T(8,128)(2,1)}, bf16[128,1536]{1,0:T(8,128)(2,1)}, u32[]{:S(2)}, u32[]{:S(2)}) %collective-permute-start.21) | collective-permute-done | bytes 393248 | tf_op jit(solution)/shard_map/cond/branch_1_fun/ppermute | solution.py:632
  173.3 9.7 %collective-permute-done.19 = bf16[64,1536]{1,0:T(8,128)(2,1)} collective-permute-done((bf16[64,1536]{1,0:T(8,128)(2,1)S(1)}, bf16[64,1536]{1,0:T(8,128)(2,1)}, u32[]{:S(2)}, u32[]{:S(2)}) %collective-permute-start.19) | collective-permute-done | bytes 196640 | tf_op jit(solution)/shard_map/cond/branch_1_fun/ppermute | solution.py:629
  188.1 15.9 %conditional.11 = ((bf16[128,1536]{1,0:T(8,128)(2,1)}, bf16[128,1536]{1,0:T(8,128)(2,1)}, f32[128,1536]{1,0:T(8,128)}, bf16[64,1536]{1,0:T(8,128)(2,1)}, bf16[64...) conditional(s32[]{:T(128)} %bitcast.29, () %tuple.101, ...), branch_computations={%region_9.10_spmd, %region_10.11_spmd} | conditional | flops 769 | bytes 9437336 | solution.py:696
  190.2 13.8 %branch_1_fun.17 = (bf16[128,1536]{1,0:T(8,128)(2,1)}, bf16[128,1536]{1,0:T(8,128)(2,1)}, f32[128,1536]{1,0:T(8,128)}, bf16[64,1536]{1,0:T(8,128)(2,1)}, bf16[64...) custom-call(s32[3]{0:T(128)S(1)} %get-tuple-element.263.place, ...), custom_call_target="tpu_custom_call" | custom-call | flops 1 | bytes 1 | tf_op jit(solution)/shard_map/cond/branch_1_fun/pallas_call | solution.py:70
  206.1 16.6 %conditional.12 = ((bf16[128,1536]{1,0:T(8,128)(2,1)}, bf16[128,1536]{1,0:T(8,128)(2,1)}, f32[128,1536]{1,0:T(8,128)}, bf16[64,1536]{1,0:T(8,128)(2,1)}, bf16[64...) conditional(s32[]{:T(128)} %bitcast.29, () %tuple.105, ...), branch_computations={%region_11.12_spmd, %region_12.13_spmd} | conditional | flops 769 | bytes 9437336 | solution.py:696
  208.8 13.9 %branch_1_fun.18 = (bf16[128,1536]{1,0:T(8,128)(2,1)}, bf16[128,1536]{1,0:T(8,128)(2,1)}, f32[128,1536]{1,0:T(8,128)}, bf16[64,1536]{1,0:T(8,128)(2,1)}, bf16[64...) custom-call(s32[3]{0:T(128)S(1)} %get-tuple-element.279.place, ...), custom_call_target="tpu_custom_call" | custom-call | flops 1 | bytes 1 | tf_op jit(solution)/shard_map/cond/branch_1_fun/pallas_call | solution.py:70
  229.1 13.0 %conditional.13 = ((bf16[4,1152,384]{2,1,0:T(8,128)(2,1)}, bf16[4,1152,384]{2,1,0:T(8,128)(2,1)})) conditional(s32[]{:T(128)} %bitcast.29, () %tuple.108, (bf16[512,1536]{1,0:T(8,128)(2,1)}, bf16[512,1536]{1,0:T(8,128)(2,1)}, bf16[512,768]{1,0:T(8,128)(2,1)}, bf16[512,1536]{1,0:T(8,128)(2,1)}, bf16[512,1536]{1,0:T(8,128)(2,1)}, ...), branch_computations={%region_13.14_spmd, %region_14.15_spmd} | conditional | flops 1 | bytes 7077916 | solution.py:696
  229.3 12.8 %branch_1_fun.19 = (bf16[4,1152,384]{2,1,0:T(8,128)(2,1)}, bf16[4,1152,384]{2,1,0:T(8,128)(2,1)}) custom-call(bf16[512,1536]{1,0:T(8,128)(2,1)} %get-tuple-element.295.refs_0_, bf16[512,1536]{1,0:T(8,128)(2,1)} %get-tuple-element.296.refs_1_, bf16[512,768]{1,0:T(8,128)(2,1)} %get-tuple-element.297.refs_2_, bf16[512,1536]{1,0:T(8,128)(2,1)} %get-tuple-element.298.refs_3_, ...), custom_call_target="tpu_custom_call" | custom-call | flops 1 | bytes 1 | tf_op jit(solution)/shard_map/cond/branch_1_fun/pallas_call | solution.py:70
  274.9 78.9 %conditional.14 = (bf16[128,1536]{1,0:T(8,128)(2,1)}, bf16[768,384]{1,0:T(8,128)(2,1)}, bf16[768,384]{1,0:T(8,128)(2,1)}, bf16[768,384]{1,0:T(8,128)(2,1)}, bf16...) conditional(s32[]{:T(128)} %bitcast.29, () %tuple.100, ...), branch_computations={%region_15.16_spmd, %region_16.20_spmd} | conditional | flops 14549140 | bytes 76152016 | solution.py:696
  279.8 7.3 %collective-permute-done.24.refs_1_ = bf16[128,1536]{1,0:T(8,128)(2,1)S(1)} collective-permute-done((bf16[128,1536]{1,0:T(8,128)(2,1)S(1)}, bf16[128,1536]{1,0:T(8,128)(2,1)S(1)}, u32[]{:S(2)}, u32[]{:S(2)}) %collective-permute-start.24) | collective-permute-done | bytes 393248 | tf_op jit(solution)/shard_map/cond/branch_1_fun/ppermute | solution.py:629
  303.5 12.5 %branch_1_fun.21 = (bf16[512,1536]{1,0:T(8,128)(2,1)}, bf16[512,1152]{1,0:T(8,128)(2,1)S(1)}, bf16[128,1536]{1,0:T(8,128)(2,1)S(1)}, bf16[128,1536]{1,0:T(8,128)...) custom-call(bf16[128,1536]{1,0:T(8,128)(2,1)S(1)} %get-tuple-element.322.refs_0_, ...), custom_call_target="tpu_custom_call" | custom-call | flops 1 | bytes 1 | tf_op jit(solution)/shard_map/cond/branch_1_fun/pallas_call | solution.py:70
  336.1 8.1 %collective-permute-done.35.got_one = bf16[128,1536]{1,0:T(8,128)(2,1)S(1)} collective-permute-done((bf16[128,1536]{1,0:T(8,128)(2,1)S(1)}, bf16[128,1536]{1,0:T(8,128)(2,1)S(1)}, u32[]{:S(2)}, u32[]{:S(2)}) %collective-permute-start.35) | collective-permute-done | bytes 393248 | tf_op jit(solution)/shard_map/cond/branch_1_fun/ppermute | solution.py:629
  364.1 56.6 %conditional.15 = (bf16[2304,384]{1,0:T(8,128)(2,1)S(1)}, bf16[2304,384]{1,0:T(8,128)(2,1)}, bf16[2304,384]{1,0:T(8,128)(2,1)}, bf16[1152,384]{1,0:T(8,128)(2,1)}, bf16[1152,384]{1,0:T(8,128)(2,1)}) conditional(s32[]{:T(128)} %bitcast.29, () %tuple.116, bf16[2304,384]{1,0:T(8,128)(2,1)S(1)} %pad_maximum_fusion.5), branch_computations={%region_20.21_spmd, %region_21.22_spmd} | conditional | bytes 35389668 | solution.py:696
  365.4 35.9 %collective-permute-done = bf16[2304,384]{1,0:T(8,128)(2,1)S(1)} collective-permute-done((bf16[2304,384]{1,0:T(8,128)(2,1)S(1)}, bf16[2304,384]{1,0:T(8,128)(2,1)S(1)}, u32[]{:S(2)}, u32[]{:S(2)}) %collective-permute-start) | collective-permute-done | bytes 1769504 | tf_op jit(solution)/shard_map/cond/branch_1_fun/ppermute | solution.py:629
  406.9 13.8 %collective-permute-done.2 = bf16[1152,384]{1,0:T(8,128)(2,1)} collective-permute-done((bf16[1152,384]{1,0:T(8,128)(2,1)S(1)}, bf16[1152,384]{1,0:T(8,128)(2,1)}, u32[]{:S(2)}, u32[]{:S(2)}) %collective-permute-start.2) | collective-permute-done | bytes 884768 | tf_op jit(solution)/shard_map/cond/branch_1_fun/ppermute | solution.py:629
  428.7 10.9 %shard_map.182 = (f32[9216,128]{1,0:T(8,128)}, f32[9216,128]{1,0:T(8,128)}, f32[384,1]{1,0:T(8,128)S(1)}) custom-call(s32[3]{0:T(128)S(1)} %pad_add_fusion.place, bf16[2304,384]{1,0:T(8,128)(2,1)} %copy-done.8, bf16[2304,384]{1,0:T(8,128)(2,1)S(1)} %copy-done.6, bf16[2304,384]{1,0:T(8,128)(2,1)} %get-tuple-element.772.refs_2_, ...), custom_call_target="tpu_custom_call" | custom-call | flops 1 | bytes 1 | tf_op jit(solution)/shard_map/pallas_call | solution.py:70
  (395 shorter events, 247.5 us)
Async XLA Ops:
  7.2 175.9 %all-gather.3.cloned.1.call-start = ((), (), s32[]{:S(2)}) async-start(), calls=%async_computation | async-start | bytes 4423680 | tf_op jit(solution)/shard_map/all_gather | solution.py:766
  12.1 56.4 %collective-permute-start.45 = (bf16[784,384]{1,0:T(8,128)(2,1)}, bf16[784,384]{1,0:T(8,128)(2,1)}, u32[]{:S(2)}, u32[]{:S(2)}) collective-permute-start(bf16[784,384]{1,0:T(8,128)(2,1)} %shard_map.179), channel_id=1, source_target_pairs={{0,8},{8,16},{16,24},{24,0},{1,9},{9,17},{17,25},{25,1},{2,10},{10... | collective-permute-start | bytes 1806344 | tf_op jit(solution)/shard_map/ppermute | solution.py:638
  15.2 53.4 %collective-permute-start.46 = (bf16[784,384]{1,0:T(8,128)(2,1)}, bf16[784,384]{1,0:T(8,128)(2,1)}, u32[]{:S(2)}, u32[]{:S(2)}) collective-permute-start(bf16[784,384]{1,0:T(8,128)(2,1)} %shard_map.179), channel_id=1, source_target_pairs={{0,16},{8,24},{16,0},{24,8},{1,17},{9,25},{17,1},{25,9},{2,18},{10... | collective-permute-start | bytes 1806344 | tf_op jit(solution)/shard_map/ppermute | solution.py:638
  17.8 50.8 %collective-permute-start.47 = (bf16[784,384]{1,0:T(8,128)(2,1)}, bf16[784,384]{1,0:T(8,128)(2,1)}, u32[]{:S(2)}, u32[]{:S(2)}) collective-permute-start(bf16[784,384]{1,0:T(8,128)(2,1)} %shard_map.179), channel_id=1, source_target_pairs={{0,24},{8,0},{16,8},{24,16},{1,25},{9,1},{17,9},{25,17},{2,26},{10... | collective-permute-start | bytes 1806344 | tf_op jit(solution)/shard_map/ppermute | solution.py:638
  41.2 25.3 %collective-permute-start.44 = (bf16[144,1536]{1,0:T(8,128)(2,1)}, bf16[144,1536]{1,0:T(8,128)(2,1)}, u32[]{:S(2)}, u32[]{:S(2)}) collective-permute-start(bf16[144,1536]{1,0:T(8,128)(2,1)} %get-tuple-element.207), channel_id=1, source_target_pairs={{0,8},{8,0},{16,24},{24,16},{1,9},{9,1},{17,25},{25,17},{2,10},{10... | collective-permute-start | bytes 1327112 | tf_op jit(solution)/shard_map/cond/branch_1_fun/ppermute | solution.py:632
  70.8 44.9 %collective-permute-start.48 = (bf16[1152,384]{1,0:T(8,128)(2,1)}, bf16[1152,384]{1,0:T(8,128)(2,1)}, u32[]{:S(2)}, u32[]{:S(2)}) collective-permute-start(bf16[1152,384]{1,0:T(8,128)(2,1)} %copy.105), channel_id=1, source_target_pairs={{0,8},{8,16},{16,24},{24,0},{1,9},{9,17},{17,25},{25,1},{2,10},{10... | collective-permute-start | bytes 2654216 | tf_op jit(solution)/shard_map/ppermute | solution.py:638
  72.7 43.0 %collective-permute-start.49 = (bf16[1152,384]{1,0:T(8,128)(2,1)}, bf16[1152,384]{1,0:T(8,128)(2,1)}, u32[]{:S(2)}, u32[]{:S(2)}) collective-permute-start(bf16[1152,384]{1,0:T(8,128)(2,1)} %copy.105), channel_id=1, source_target_pairs={{0,24},{8,0},{16,8},{24,16},{1,25},{9,1},{17,9},{25,17},{2,26},{10... | collective-permute-start | bytes 2654216 | tf_op jit(solution)/shard_map/ppermute | solution.py:638
  87.4 21.2 %collective-permute-start.9 = (bf16[1,2,192,384]{3,2,1,0:T(8,128)(2,1)S(1)}, bf16[1,2,192,384]{3,2,1,0:T(8,128)(2,1)S(1)}, u32[]{:S(2)}, u32[]{:S(2)}) collective-permute-start(bf16[1,2,192,384]{3,2,1,0:T(8,128)(2,1)S(1)} %maximum_bitcast_fusion.3), channel_id=1, source_target_pairs={{0,6},{2,4},{4,2},{6,0},{1,7},{3,5},{5,3},{7,1},{8,14},{10,12},{12... | collective-permute-start | bytes 884744 | tf_op jit(solution)/shard_map/cond/branch_1_fun/ppermute | solution.py:629
  117.1 65.9 %collective-permute-start.50 = (bf16[1152,384]{1,0:T(8,128)(2,1)}, bf16[1152,384]{1,0:T(8,128)(2,1)}, u32[]{:S(2)}, u32[]{:S(2)}) collective-permute-start(bf16[1152,384]{1,0:T(8,128)(2,1)} %copy.108), channel_id=1, source_target_pairs={{0,16},{8,24},{16,0},{24,8},{1,17},{9,25},{17,1},{25,9},{2,18},{10... | collective-permute-start | bytes 2654216 | tf_op jit(solution)/shard_map/ppermute | solution.py:638
  119.5 21.4 %collective-permute-start.12 = (bf16[1152,384]{1,0:T(8,128)(2,1)}, bf16[1152,384]{1,0:T(8,128)(2,1)}, u32[]{:S(2)}, u32[]{:S(2)}) collective-permute-start(bf16[1152,384]{1,0:T(8,128)(2,1)} %get-tuple-element.245), channel_id=1, source_target_pairs={{0,1},{1,0},{2,3},{3,2},{4,5},{5,4},{6,7},{7,6},{8,9},{9,8},{10,11... | collective-permute-start | bytes 2654216 | tf_op jit(solution)/shard_map/cond/branch_1_fun/ppermute | solution.py:635
  119.6 21.3 %collective-permute-start.13 = (bf16[1152,384]{1,0:T(8,128)(2,1)}, bf16[1152,384]{1,0:T(8,128)(2,1)}, u32[]{:S(2)}, u32[]{:S(2)}) collective-permute-start(bf16[1152,384]{1,0:T(8,128)(2,1)} %get-tuple-element.246), channel_id=1, source_target_pairs={{0,1},{1,0},{2,3},{3,2},{4,5},{5,4},{6,7},{7,6},{8,9},{9,8},{10,11... | collective-permute-start | bytes 2654216 | tf_op jit(solution)/shard_map/cond/branch_1_fun/ppermute | solution.py:635
  120.1 20.3 %collective-permute-start.10 = (bf16[128,1536]{1,0:T(8,128)(2,1)}, bf16[128,1536]{1,0:T(8,128)(2,1)S(1)}, u32[]{:S(2)}, u32[]{:S(2)}) collective-permute-start(bf16[128,1536]{1,0:T(8,128)(2,1)} %get-tuple-element.242), channel_id=1, source_target_pairs={{0,2},{2,0},{4,6},{6,4},{1,3},{3,1},{5,7},{7,5},{8,10},{10,8},{12,... | collective-permute-start | bytes 1179656 | tf_op jit(solution)/shard_map/cond/branch_1_fun/ppermute | solution.py:629
  120.7 20.2 %collective-permute-start.11 = (bf16[128,1536]{1,0:T(8,128)(2,1)}, bf16[128,1536]{1,0:T(8,128)(2,1)S(1)}, u32[]{:S(2)}, u32[]{:S(2)}) collective-permute-start(bf16[128,1536]{1,0:T(8,128)(2,1)} %get-tuple-element.243), channel_id=1, source_target_pairs={{0,4},{2,6},{4,0},{6,2},{1,5},{3,7},{5,1},{7,3},{8,12},{10,14},{12... | collective-permute-start | bytes 1179656 | tf_op jit(solution)/shard_map/cond/branch_1_fun/ppermute | solution.py:629
  184.1 19.9 %collective-permute-start.52 = (bf16[64,1536]{1,0:T(8,128)(2,1)S(1)}, bf16[64,1536]{1,0:T(8,128)(2,1)S(1)}, u32[]{:S(2)}, u32[]{:S(2)}) collective-permute-start(bf16[64,1536]{1,0:T(8,128)(2,1)S(1)} %slice.149), channel_id=1, source_target_pairs={{0,4},{2,6},{4,0},{6,2},{1,5},{3,7},{5,1},{7,3},{8,12},{10,14},{12... | collective-permute-start | bytes 589832 | tf_op jit(solution)/shard_map/ppermute | solution.py:629
  222.8 19.4 %collective-permute-start.58 = (bf16[128,1536]{1,0:T(8,128)(2,1)}, bf16[128,1536]{1,0:T(8,128)(2,1)S(1)}, u32[]{:S(2)}, u32[]{:S(2)}) collective-permute-start(bf16[128,1536]{1,0:T(8,128)(2,1)} %get-tuple-element.680), channel_id=1, source_target_pairs={{0,2},{2,0},{4,6},{6,4},{1,3},{3,1},{5,7},{7,5},{8,10},{10,8},{12,... | collective-permute-start | bytes 1179656 | tf_op jit(solution)/shard_map/ppermute | solution.py:629
  265.8 88.0 %collective-permute-start.67 = (bf16[1152,384]{1,0:T(8,128)(2,1)}, bf16[1152,384]{1,0:T(8,128)(2,1)}, u32[]{:S(2)}, u32[]{:S(2)}) collective-permute-start(bf16[1152,384]{1,0:T(8,128)(2,1)} %get-tuple-element.737), channel_id=1, source_target_pairs={{0,8},{8,16},{16,24},{24,0},{1,9},{9,17},{17,25},{25,1},{2,10},{10... | collective-permute-start | bytes 2654216 | tf_op jit(solution)/shard_map/ppermute | solution.py:638
  266.1 87.7 %collective-permute-start.68 = (bf16[1152,384]{1,0:T(8,128)(2,1)}, bf16[1152,384]{1,0:T(8,128)(2,1)}, u32[]{:S(2)}, u32[]{:S(2)}) collective-permute-start(bf16[1152,384]{1,0:T(8,128)(2,1)} %get-tuple-element.738), channel_id=1, source_target_pairs={{0,16},{8,24},{16,0},{24,8},{1,17},{9,25},{17,1},{25,9},{2,18},{10... | collective-permute-start | bytes 2654216 | tf_op jit(solution)/shard_map/ppermute | solution.py:638
  269.0 84.9 %collective-permute-start.69 = (bf16[1152,384]{1,0:T(8,128)(2,1)}, bf16[1152,384]{1,0:T(8,128)(2,1)}, u32[]{:S(2)}, u32[]{:S(2)}) collective-permute-start(bf16[1152,384]{1,0:T(8,128)(2,1)} %get-tuple-element.739), channel_id=1, source_target_pairs={{0,24},{8,0},{16,8},{24,16},{1,25},{9,1},{17,9},{25,17},{2,26},{10... | collective-permute-start | bytes 2654216 | tf_op jit(solution)/shard_map/ppermute | solution.py:638
  353.9 66.8 %collective-permute-start.70 = (bf16[768,384]{1,0:T(8,128)(2,1)}, bf16[768,384]{1,0:T(8,128)(2,1)}, u32[]{:S(2)}, u32[]{:S(2)}) collective-permute-start(bf16[768,384]{1,0:T(8,128)(2,1)} %get-tuple-element.754), channel_id=1, source_target_pairs={{0,8},{8,16},{16,24},{24,0},{1,9},{9,17},{17,25},{25,1},{2,10},{10... | collective-permute-start | bytes 1769480 | tf_op jit(solution)/shard_map/ppermute | solution.py:638
  355.9 64.8 %collective-permute-start.71 = (bf16[768,384]{1,0:T(8,128)(2,1)}, bf16[768,384]{1,0:T(8,128)(2,1)}, u32[]{:S(2)}, u32[]{:S(2)}) collective-permute-start(bf16[768,384]{1,0:T(8,128)(2,1)} %get-tuple-element.755), channel_id=1, source_target_pairs={{0,16},{8,24},{16,0},{24,8},{1,17},{9,25},{17,1},{25,9},{2,18},{10... | collective-permute-start | bytes 1769480 | tf_op jit(solution)/shard_map/ppermute | solution.py:638
  358.1 62.6 %collective-permute-start.72 = (bf16[768,384]{1,0:T(8,128)(2,1)}, bf16[768,384]{1,0:T(8,128)(2,1)}, u32[]{:S(2)}, u32[]{:S(2)}) collective-permute-start(bf16[768,384]{1,0:T(8,128)(2,1)} %get-tuple-element.756), channel_id=1, source_target_pairs={{0,24},{8,0},{16,8},{24,16},{1,25},{9,1},{17,9},{25,17},{2,26},{10... | collective-permute-start | bytes 1769480 | tf_op jit(solution)/shard_map/ppermute | solution.py:638
  364.1 37.1 %collective-permute-start = (bf16[2304,384]{1,0:T(8,128)(2,1)S(1)}, bf16[2304,384]{1,0:T(8,128)(2,1)S(1)}, u32[]{:S(2)}, u32[]{:S(2)}) collective-permute-start(bf16[2304,384]{1,0:T(8,128)(2,1)S(1)} %param.15), channel_id=1, source_target_pairs={{0,2},{2,0},{4,6},{6,4},{1,3},{3,1},{5,7},{7,5},{8,10},{10,8},{12,... | collective-permute-start | bytes 5308424 | tf_op jit(solution)/shard_map/cond/branch_1_fun/ppermute | solution.py:629
  364.6 39.0 %collective-permute-start.1 = (bf16[2304,384]{1,0:T(8,128)(2,1)S(1)}, bf16[2304,384]{1,0:T(8,128)(2,1)}, u32[]{:S(2)}, u32[]{:S(2)}) collective-permute-start(bf16[2304,384]{1,0:T(8,128)(2,1)S(1)} %param.15), channel_id=1, source_target_pairs={{0,4},{2,6},{4,0},{6,2},{1,5},{3,7},{5,1},{7,3},{8,12},{10,14},{12... | collective-permute-start | bytes 5308424 | tf_op jit(solution)/shard_map/cond/branch_1_fun/ppermute | solution.py:629
  428.2 22.3 %collective-permute-start.66 = (bf16[128,1536]{1,0:T(8,128)(2,1)}, bf16[128,1536]{1,0:T(8,128)(2,1)}, u32[]{:S(2)}, u32[]{:S(2)}) collective-permute-start(bf16[128,1536]{1,0:T(8,128)(2,1)} %bitcast.42), channel_id=1, source_target_pairs={{0,8},{8,0},{16,24},{24,16},{1,9},{9,1},{17,25},{25,17},{2,10},{10... | collective-permute-start | bytes 1179656 | tf_op jit(solution)/shard_map/ppermute | solution.py:632
  (116 other events, 1041.8 us)
Sparse Core Ops, SparseCore 0:
  68.7 74.7 all-gather.2

commit v7 on v6

--- a/solution.py
+++ b/solution.py
@@ -1094,14 +1094,11 @@
                 lax.dynamic_index_in_dim(last_part, (z + k) % n, 0, keepdims=False) for k in range(n)
             ]
         normed_parts = cut(*normed_parts, *last_parts)[:5]
-        grad_normed = plane_reduce(*normed_parts)
-        unit_first, inverse_first = unit(residual)
-        input_grad = (
-            grad_middle + norm_back(grad_normed, unit_first, inverse_first, gain_first)
-        ).astype(BF)
-        return input_grad, last_parts, branch_sum
-
-    input_grad, last_parts, branch_sum = together(
+        to_one, to_two, *waiting = normed_parts
+        normed_sum = plane_reduce_rest(hop(to_one, 1), hop(to_two, 2), *waiting)
+        return grad_middle, normed_sum, last_parts, branch_sum
+
+    grad_middle, normed_sum, last_parts, branch_sum = together(
         attention_back, own_half, far_half, branch_got
     )
     cut_values = cut(*moved, *last_parts)
@@ -1111,7 +1108,19 @@
     pair_sums = jnp.concatenate([v.astype(BF) for v in sums], axis=0)
     last_moved = [ring(last_parts[k], k) for k in range(1, n)]
 
-    unit_pieces = together(plane_gather, pair_sums)
+    def rows_done(pair_sums, branch_sum, normed_sum):
+        unit_pieces = plane_gather(pair_sums)
+        unit_first, inverse_first = unit(residual)
+        input_grad = grad_middle + norm_back(
+            summed(*normed_sum), unit_first, inverse_first, gain_first
+        )
+        branch = summed(*branch_sum).reshape(2, 2, rows // 2, width)
+        branch_ffn, branch_far = (branch[:, k].reshape(rows, width) for k in (0, 1))
+        return unit_pieces, input_grad.astype(BF), branch_ffn, branch_far.astype(BF)
+
+    unit_pieces, input_grad, branch_ffn, branch_far = together(
+        rows_done, pair_sums, branch_sum, normed_sum
+    )
     got = cut(*unit_pieces, *last_moved)
     unit_pieces, last_moved = got[:5], got[5:]
     last_sum = last_parts[0].astype(F32) + sum(v.astype(F32) for v in last_moved)
@@ -1175,9 +1184,7 @@
         *last_rest, share_down = cut(*last_pieces[3:], share_down)
         last_pieces[3:] = last_rest
     share_gain_ffn = (ffn_part + core(ffn_part)) / gain_ffn.astype(F32)
-    branch_sum = summed(*branch_sum).reshape(2, 2, rows // 2, width)
-    branch_ffn, branch_far = (branch_sum[:, k].reshape(rows, width) for k in (0, 1))
-    branch_ffn += pair(branch_far.astype(BF)).astype(F32)
+    branch_ffn += pair(branch_far).astype(F32)
     outputs = (middle + branch_ffn.astype(BF).astype(F32)).astype(BF)
     if hs % 16 == 0:
         share_qkv, share_out, attn_part = call(

time: 474 us -> 475 us (level)
  waiting for transfers between devices: 174 us -> 152 us
  local copies, waits for them, and re-layouts: 47.2 us -> 58.9 us
  Pallas kernels: 109 us -> 114 us
    ppermute x50, waiting for transfers between devices: 147 us -> 132 us  [hop(): return lax.ppermute(x, 'gran', [(i, i ^ r) for i in range(g)])]
    ppermute x4, waiting for transfers between devices: 23.9 us -> 16.4 us  [pair(): return lax.ppermute(x, 'batch', [(i, i ^ 1) for i in range(n)])]
    pallas_call x17, Pallas kernels: 103 us -> 109 us  [call(): pl.pallas_call(kernel, out_shape=[jax.ShapeDtypeStruct(shape, dtype) for...]
    cond x57 -> x68, local copies, waits for them, and re-layouts: 8.92 us -> 11.1 us
  transfers between devices with their start and end apart: 84 -> 84, of which waited for: 33 -> 30; matrix products, arithmetic and copies ran while one was open for 14% -> 18% of each run, Pallas kernels for 21% -> 22%
where the time goes in v7:
time: 475 us; the launch traced here: 469 us
  waiting for transfers between devices  152 us (32%)
  Pallas kernels  114 us (24%)
  starting transfers between devices  91.2 us (19%)
  local copies, waits for them, and re-layouts  58.9 us (12%)
  other arithmetic  35.6 us (7%)
  between operations  15.2 us (3%)
    ppermute x50, waiting for transfers between devices, hop(): return lax.ppermute(x, 'gran', [(i, i ^ r) for i in range(g)])  132 us
    pallas_call x17, Pallas kernels, call(): pl.pallas_call(kernel, out_shape=[jax.ShapeDtypeStruct(shape, dtype) for...  109 us
    ppermute x50, starting transfers between devices, hop(): return lax.ppermute(x, 'gran', [(i, i ^ r) for i in range(g)])  54.6 us
    ppermute x12, starting transfers between devices, ring(): return lax.ppermute(x, 'batch', [(i, (i + s) % n) for i in range(n)])  31.1 us
    ppermute x4, waiting for transfers between devices, pair(): return lax.ppermute(x, 'batch', [(i, i ^ 1) for i in range(n)])  16.4 us
    cond x68, local copies, waits for them, and re-layouts  11.1 us
    slice x12, local copies, waits for them, and re-layouts, gather_rest(): return [*pieces, hop(pieces[1][:half], 2), hop(pieces[2][half:], 1)]  10.5 us
  transfers between devices with their start and end apart: 84, of which 30 were waited for; matrix products, arithmetic and copies ran while one was open for 18% of the time, Pallas kernels for 22%

profile of v7, /device:TPU:0, one launch (start us, length us, event | category | flops | bytes accessed | tf_op | source)
XLA Modules:
  0.0 468.7 jit_solution(5041185500633828430)
XLA Ops:
  19.3 47.8 %conditional.8 = (bf16[144,1536]{1,0:T(8,128)(2,1)}, bf16[144,1536]{1,0:T(8,128)(2,1)}, bf16[144,1536]{1,0:T(8,128)(2,1)}, bf16[64,1536]{1,0:T(8,128)(2,1)}, bf1...) conditional(s32[]{:T(128)} %bitcast.32, () %tuple.93, ...), branch_computations={%region_2.3_spmd, %region_3.4_spmd} | conditional | flops 442375 | bytes 49398416 | solution.py:696
  22.4 8.4 %collective-permute-done.40 = bf16[144,1536]{1,0:T(8,128)(2,1)} collective-permute-done((bf16[144,1536]{1,0:T(8,128)(2,1)}, bf16[144,1536]{1,0:T(8,128)(2,1)}, u32[]{:S(2)}, u32[]{:S(2)}) %collective-permute-start.40) | collective-permute-done | bytes 442400 | tf_op jit(solution)/shard_map/cond/branch_1_fun/ppermute | solution.py:629
  71.4 8.4 %collective-permute-start.49 = (bf16[1152,384]{1,0:T(8,128)(2,1)}, bf16[1152,384]{1,0:T(8,128)(2,1)}, u32[]{:S(2)}, u32[]{:S(2)}) collective-permute-start(bf16[1152,384]{1,0:T(8,128)(2,1)} %copy.107), channel_id=1, source_target_pairs={{0,24},{8,0},{16,8},{24,16},{1,25},{9,1},{17,9},{25,17},{2,26},{10... | collective-permute-start | bytes 2654216 | tf_op jit(solution)/shard_map/ppermute | solution.py:638
  79.8 35.4 %conditional.9 = (bf16[512,1536]{1,0:T(8,128)(2,1)}, bf16[1536,1152]{1,0:T(8,128)(2,1)}, bf16[384,1536]{1,0:T(8,128)(2,1)}, bf16[512,384]{1,0:T(8,128)(2,1)}, bf...) conditional(s32[]{:T(128)} %bitcast.32, () %tuple.96, ...), branch_computations={%region_4.5_spmd, %region_5.6_spmd} | conditional | flops 2949507 | bytes 25320180 | solution.py:696
  89.8 11.6 %branch_1_fun.13 = (bf16[512,1536]{1,0:T(8,128)(2,1)}, bf16[1536,1152]{1,0:T(8,128)(2,1)}, bf16[512,384]{1,0:T(8,128)(2,1)}, bf16[512,384]{1,0:T(8,128)(2,1)}, b...) custom-call(s32[3]{0:T(128)S(1)} %copy-done.51, ...), custom_call_target="tpu_custom_call" | custom-call | flops 1 | bytes 1 | tf_op jit(solution)/shard_map/cond/branch_1_fun/pallas_call | solution.py:70
  119.0 64.4 %conditional.10 = (f32[128,1536]{1,0:T(8,128)}, f32[128,1536]{1,0:T(8,128)S(1)}, f32[128,1]{0,1:T(1,128)S(1)}, bf16[128,1536]{1,0:T(8,128)(2,1)}, bf16[128,1536]...) conditional(s32[]{:T(128)} %bitcast.32, () %tuple.92, ...), branch_computations={%region_6.7_spmd, %region_7.9_spmd} | conditional | flops 2359425 | bytes 41899308 | solution.py:696
  123.3 16.6 %collective-permute-done.10.got_one = bf16[128,1536]{1,0:T(8,128)(2,1)S(1)} collective-permute-done((bf16[128,1536]{1,0:T(8,128)(2,1)}, bf16[128,1536]{1,0:T(8,128)(2,1)S(1)}, u32[]{:S(2)}, u32[]{:S(2)}) %collective-permute-start.10) | collective-permute-done | bytes 393248 | tf_op jit(solution)/shard_map/cond/branch_1_fun/ppermute | solution.py:629
  157.1 9.6 %collective-permute-done.21 = bf16[128,1536]{1,0:T(8,128)(2,1)} collective-permute-done((bf16[128,1536]{1,0:T(8,128)(2,1)}, bf16[128,1536]{1,0:T(8,128)(2,1)}, u32[]{:S(2)}, u32[]{:S(2)}) %collective-permute-start.21) | collective-permute-done | bytes 393248 | tf_op jit(solution)/shard_map/cond/branch_1_fun/ppermute | solution.py:632
  172.8 10.7 %collective-permute-done.19 = bf16[64,1536]{1,0:T(8,128)(2,1)} collective-permute-done((bf16[64,1536]{1,0:T(8,128)(2,1)S(1)}, bf16[64,1536]{1,0:T(8,128)(2,1)}, u32[]{:S(2)}, u32[]{:S(2)}) %collective-permute-start.19) | collective-permute-done | bytes 196640 | tf_op jit(solution)/shard_map/cond/branch_1_fun/ppermute | solution.py:629
  189.2 15.8 %conditional.11 = ((bf16[128,1536]{1,0:T(8,128)(2,1)}, bf16[128,1536]{1,0:T(8,128)(2,1)}, f32[128,1536]{1,0:T(8,128)}, bf16[64,1536]{1,0:T(8,128)(2,1)}, bf16[64...) conditional(s32[]{:T(128)} %bitcast.32, () %tuple.101, ...), branch_computations={%region_9.10_spmd, %region_10.11_spmd} | conditional | flops 769 | bytes 9437336 | solution.py:696
  191.2 13.7 %branch_1_fun.17 = (bf16[128,1536]{1,0:T(8,128)(2,1)}, bf16[128,1536]{1,0:T(8,128)(2,1)}, f32[128,1536]{1,0:T(8,128)}, bf16[64,1536]{1,0:T(8,128)(2,1)}, bf16[64...) custom-call(s32[3]{0:T(128)S(1)} %get-tuple-element.279.place, ...), custom_call_target="tpu_custom_call" | custom-call | flops 1 | bytes 1 | tf_op jit(solution)/shard_map/cond/branch_1_fun/pallas_call | solution.py:70
  207.9 15.3 %conditional.12 = ((bf16[128,1536]{1,0:T(8,128)(2,1)}, bf16[128,1536]{1,0:T(8,128)(2,1)}, f32[128,1536]{1,0:T(8,128)}, bf16[64,1536]{1,0:T(8,128)(2,1)}, bf16[64...) conditional(s32[]{:T(128)} %bitcast.32, () %tuple.105, ...), branch_computations={%region_11.12_spmd, %region_12.13_spmd} | conditional | flops 769 | bytes 9437336 | solution.py:696
  209.3 13.9 %branch_1_fun.18 = (bf16[128,1536]{1,0:T(8,128)(2,1)}, bf16[128,1536]{1,0:T(8,128)(2,1)}, f32[128,1536]{1,0:T(8,128)}, bf16[64,1536]{1,0:T(8,128)(2,1)}, bf16[64...) custom-call(s32[3]{0:T(128)S(1)} %get-tuple-element.295.place, ...), custom_call_target="tpu_custom_call" | custom-call | flops 1 | bytes 1 | tf_op jit(solution)/shard_map/cond/branch_1_fun/pallas_call | solution.py:70
  229.6 13.0 %conditional.13 = ((bf16[4,1152,384]{2,1,0:T(8,128)(2,1)}, bf16[4,1152,384]{2,1,0:T(8,128)(2,1)})) conditional(s32[]{:T(128)} %bitcast.32, () %tuple.108, (bf16[512,1536]{1,0:T(8,128)(2,1)}, bf16[512,1536]{1,0:T(8,128)(2,1)}, bf16[512,768]{1,0:T(8,128)(2,1)}, bf16[512,1536]{1,0:T(8,128)(2,1)}, bf16[512,1536]{1,0:T(8,128)(2,1)}, ...), branch_computations={%region_13.14_spmd, %region_14.15_spmd} | conditional | flops 1 | bytes 7077916 | solution.py:696
  229.7 12.9 %branch_1_fun.19 = (bf16[4,1152,384]{2,1,0:T(8,128)(2,1)}, bf16[4,1152,384]{2,1,0:T(8,128)(2,1)}) custom-call(bf16[512,1536]{1,0:T(8,128)(2,1)} %get-tuple-element.311.refs_0_, bf16[512,1536]{1,0:T(8,128)(2,1)} %get-tuple-element.312.refs_1_, bf16[512,768]{1,0:T(8,128)(2,1)} %get-tuple-element.313.refs_2_, bf16[512,1536]{1,0:T(8,128)(2,1)} %get-tuple-element.314.refs_3_, ...), custom_call_target="tpu_custom_call" | custom-call | flops 1 | bytes 1 | tf_op jit(solution)/shard_map/cond/branch_1_fun/pallas_call | solution.py:70
  278.7 76.8 %conditional.14 = (f32[128,1536]{1,0:T(8,128)S(1)}, f32[128,1536]{1,0:T(8,128)}, bf16[64,1536]{1,0:T(8,128)(2,1)}, bf16[64,1536]{1,0:T(8,128)(2,1)}, bf16[768,38...) conditional(s32[]{:T(128)} %bitcast.32, () %tuple.113, ...), branch_computations={%region_15.16_spmd, %region_16.18_spmd} | conditional | flops 8650772 | bytes 57634372 | solution.py:696
  284.1 6.7 %collective-permute-done.24.refs_1_ = bf16[128,1536]{1,0:T(8,128)(2,1)S(1)} collective-permute-done((bf16[128,1536]{1,0:T(8,128)(2,1)S(1)}, bf16[128,1536]{1,0:T(8,128)(2,1)S(1)}, u32[]{:S(2)}, u32[]{:S(2)}) %collective-permute-start.24) | collective-permute-done | bytes 393248 | tf_op jit(solution)/shard_map/cond/branch_1_fun/ppermute | solution.py:629
  305.8 12.4 %branch_1_fun.21 = (bf16[512,1536]{1,0:T(8,128)(2,1)}, bf16[512,1152]{1,0:T(8,128)(2,1)S(1)}, bf16[128,1536]{1,0:T(8,128)(2,1)S(1)}, bf16[128,1536]{1,0:T(8,128)...) custom-call(bf16[128,1536]{1,0:T(8,128)(2,1)S(1)} %get-tuple-element.337.refs_0_, ...), custom_call_target="tpu_custom_call" | custom-call | flops 1 | bytes 1 | tf_op jit(solution)/shard_map/cond/branch_1_fun/pallas_call | solution.py:70
  338.2 9.1 %collective-permute-done.35.got_one = bf16[128,1536]{1,0:T(8,128)(2,1)S(1)} collective-permute-done((bf16[128,1536]{1,0:T(8,128)(2,1)S(1)}, bf16[128,1536]{1,0:T(8,128)(2,1)S(1)}, u32[]{:S(2)}, u32[]{:S(2)}) %collective-permute-start.35) | collective-permute-done | bytes 393248 | tf_op jit(solution)/shard_map/cond/branch_1_fun/ppermute | solution.py:629
  366.5 58.4 %conditional.15 = (bf16[2304,384]{1,0:T(8,128)(2,1)S(1)}, bf16[2304,384]{1,0:T(8,128)(2,1)}, bf16[2304,384]{1,0:T(8,128)(2,1)}, bf16[1152,384]{1,0:T(8,128)(2,1)...) conditional(s32[]{:T(128)} %bitcast.32, () %tuple.100, ...), branch_computations={%region_18.19_spmd, %region_19.22_spmd} | conditional | flops 6488192 | bytes 41317088 | solution.py:696
  373.1 30.5 %collective-permute-done.6 = bf16[2304,384]{1,0:T(8,128)(2,1)} collective-permute-done((bf16[2304,384]{1,0:T(8,128)(2,1)S(1)}, bf16[2304,384]{1,0:T(8,128)(2,1)}, u32[]{:S(2)}, u32[]{:S(2)}) %collective-permute-start.6) | collective-permute-done | bytes 1769504 | tf_op jit(solution)/shard_map/cond/branch_1_fun/ppermute | solution.py:629
  412.1 11.4 %collective-permute-done.8 = bf16[1152,384]{1,0:T(8,128)(2,1)} collective-permute-done((bf16[1152,384]{1,0:T(8,128)(2,1)S(1)}, bf16[1152,384]{1,0:T(8,128)(2,1)}, u32[]{:S(2)}, u32[]{:S(2)}) %collective-permute-start.8) | collective-permute-done | bytes 884768 | tf_op jit(solution)/shard_map/cond/branch_1_fun/ppermute | solution.py:629
  429.5 12.0 %shard_map.182 = (f32[9216,128]{1,0:T(8,128)}, f32[9216,128]{1,0:T(8,128)}, f32[384,1]{1,0:T(8,128)S(1)}) custom-call(s32[3]{0:T(128)S(1)} %copy-done.50, bf16[2304,384]{1,0:T(8,128)(2,1)} %copy-done.5, bf16[2304,384]{1,0:T(8,128)(2,1)} %get-tuple-element.808.refs_1_, bf16[2304,384]{1,0:T(8,128)(2,1)} %get-tuple-element.809.refs_2_, ...), custom_call_target="tpu_custom_call" | custom-call | flops 1 | bytes 1 | tf_op jit(solution)/shard_map/pallas_call | solution.py:70
  454.0 6.7 %shard_map.184 = (f32[384,4608]{1,0:T(8,128)}, f32[384,1536]{1,0:T(8,128)}, f32[384,1]{1,0:T(8,128)S(1)}) custom-call(s32[3]{0:T(128)S(1)} %copy-done.50, bf16[768,384]{1,0:T(8,128)(2,1)S(1)} %add_convert_fusion.10.refs_0_, bf16[768,384]{1,0:T(8,128)(2,1)S(1)} %collective-permute-done.73.refs_1_, bf16[768,384]{1,0:T(8,128)(2,1)S(1)} %collective-permute-done.74.refs_2_, ...), custom_call_target="tpu_custom_call" | custom-call | flops 1 | bytes 1 | tf_op jit(solution)/shard_map/pallas_call | solution.py:70
  (396 shorter events, 256.9 us)
Async XLA Ops:
  7.2 176.3 %all-gather.3.cloned.1.call-start = ((), (), s32[]{:S(2)}) async-start(), calls=%async_computation | async-start | bytes 4423680 | tf_op jit(solution)/shard_map/all_gather | solution.py:766
  11.0 56.1 %collective-permute-start.45 = (bf16[784,384]{1,0:T(8,128)(2,1)S(1)}, bf16[784,384]{1,0:T(8,128)(2,1)}, u32[]{:S(2)}, u32[]{:S(2)}) collective-permute-start(bf16[784,384]{1,0:T(8,128)(2,1)S(1)} %shard_map.179), channel_id=1, source_target_pairs={{0,8},{8,16},{16,24},{24,0},{1,9},{9,17},{17,25},{25,1},{2,10},{10... | collective-permute-start | bytes 1806344 | tf_op jit(solution)/shard_map/ppermute | solution.py:638
  14.1 53.0 %collective-permute-start.46 = (bf16[784,384]{1,0:T(8,128)(2,1)S(1)}, bf16[784,384]{1,0:T(8,128)(2,1)}, u32[]{:S(2)}, u32[]{:S(2)}) collective-permute-start(bf16[784,384]{1,0:T(8,128)(2,1)S(1)} %shard_map.179), channel_id=1, source_target_pairs={{0,16},{8,24},{16,0},{24,8},{1,17},{9,25},{17,1},{25,9},{2,18},{10... | collective-permute-start | bytes 1806344 | tf_op jit(solution)/shard_map/ppermute | solution.py:638
  16.7 50.4 %collective-permute-start.47 = (bf16[784,384]{1,0:T(8,128)(2,1)S(1)}, bf16[784,384]{1,0:T(8,128)(2,1)}, u32[]{:S(2)}, u32[]{:S(2)}) collective-permute-start(bf16[784,384]{1,0:T(8,128)(2,1)S(1)} %shard_map.179), channel_id=1, source_target_pairs={{0,24},{8,0},{16,8},{24,16},{1,25},{9,1},{17,9},{25,17},{2,26},{10... | collective-permute-start | bytes 1806344 | tf_op jit(solution)/shard_map/ppermute | solution.py:638
  40.7 24.4 %collective-permute-start.44 = (bf16[144,1536]{1,0:T(8,128)(2,1)}, bf16[144,1536]{1,0:T(8,128)(2,1)}, u32[]{:S(2)}, u32[]{:S(2)}) collective-permute-start(bf16[144,1536]{1,0:T(8,128)(2,1)} %get-tuple-element.223), channel_id=1, source_target_pairs={{0,8},{8,0},{16,24},{24,16},{1,9},{9,1},{17,25},{25,17},{2,10},{10... | collective-permute-start | bytes 1327112 | tf_op jit(solution)/shard_map/cond/branch_1_fun/ppermute | solution.py:632
  69.4 45.9 %collective-permute-start.48 = (bf16[1152,384]{1,0:T(8,128)(2,1)}, bf16[1152,384]{1,0:T(8,128)(2,1)}, u32[]{:S(2)}, u32[]{:S(2)}) collective-permute-start(bf16[1152,384]{1,0:T(8,128)(2,1)} %copy.107), channel_id=1, source_target_pairs={{0,8},{8,16},{16,24},{24,0},{1,9},{9,17},{17,25},{25,1},{2,10},{10... | collective-permute-start | bytes 2654216 | tf_op jit(solution)/shard_map/ppermute | solution.py:638
  71.4 43.9 %collective-permute-start.49 = (bf16[1152,384]{1,0:T(8,128)(2,1)}, bf16[1152,384]{1,0:T(8,128)(2,1)}, u32[]{:S(2)}, u32[]{:S(2)}) collective-permute-start(bf16[1152,384]{1,0:T(8,128)(2,1)} %copy.107), channel_id=1, source_target_pairs={{0,24},{8,0},{16,8},{24,16},{1,25},{9,1},{17,9},{25,17},{2,26},{10... | collective-permute-start | bytes 2654216 | tf_op jit(solution)/shard_map/ppermute | solution.py:638
  88.3 19.6 %collective-permute-start.5 = (bf16[1,2,192,384]{3,2,1,0:T(8,128)(2,1)S(1)}, bf16[1,2,192,384]{3,2,1,0:T(8,128)(2,1)S(1)}, u32[]{:S(2)}, u32[]{:S(2)}) collective-permute-start(bf16[1,2,192,384]{3,2,1,0:T(8,128)(2,1)S(1)} %maximum_bitcast_fusion.3), channel_id=1, source_target_pairs={{0,6},{2,4},{4,2},{6,0},{1,7},{3,5},{5,3},{7,1},{8,14},{10,12},{12... | collective-permute-start | bytes 884744 | tf_op jit(solution)/shard_map/cond/branch_1_fun/ppermute | solution.py:629
  116.6 66.9 %collective-permute-start.50 = (bf16[1152,384]{1,0:T(8,128)(2,1)}, bf16[1152,384]{1,0:T(8,128)(2,1)}, u32[]{:S(2)}, u32[]{:S(2)}) collective-permute-start(bf16[1152,384]{1,0:T(8,128)(2,1)} %copy.110), channel_id=1, source_target_pairs={{0,16},{8,24},{16,0},{24,8},{1,17},{9,25},{17,1},{25,9},{2,18},{10... | collective-permute-start | bytes 2654216 | tf_op jit(solution)/shard_map/ppermute | solution.py:638
  119.0 22.1 %collective-permute-start.12 = (bf16[1152,384]{1,0:T(8,128)(2,1)}, bf16[1152,384]{1,0:T(8,128)(2,1)S(1)}, u32[]{:S(2)}, u32[]{:S(2)}) collective-permute-start(bf16[1152,384]{1,0:T(8,128)(2,1)} %get-tuple-element.261), channel_id=1, source_target_pairs={{0,1},{1,0},{2,3},{3,2},{4,5},{5,4},{6,7},{7,6},{8,9},{9,8},{10,11... | collective-permute-start | bytes 2654216 | tf_op jit(solution)/shard_map/cond/branch_1_fun/ppermute | solution.py:635
  119.1 22.1 %collective-permute-start.13 = (bf16[1152,384]{1,0:T(8,128)(2,1)}, bf16[1152,384]{1,0:T(8,128)(2,1)}, u32[]{:S(2)}, u32[]{:S(2)}) collective-permute-start(bf16[1152,384]{1,0:T(8,128)(2,1)} %get-tuple-element.262), channel_id=1, source_target_pairs={{0,1},{1,0},{2,3},{3,2},{4,5},{5,4},{6,7},{7,6},{8,9},{9,8},{10,11... | collective-permute-start | bytes 2654216 | tf_op jit(solution)/shard_map/cond/branch_1_fun/ppermute | solution.py:635
  119.6 20.3 %collective-permute-start.10 = (bf16[128,1536]{1,0:T(8,128)(2,1)}, bf16[128,1536]{1,0:T(8,128)(2,1)S(1)}, u32[]{:S(2)}, u32[]{:S(2)}) collective-permute-start(bf16[128,1536]{1,0:T(8,128)(2,1)} %get-tuple-element.258), channel_id=1, source_target_pairs={{0,2},{2,0},{4,6},{6,4},{1,3},{3,1},{5,7},{7,5},{8,10},{10,8},{12,... | collective-permute-start | bytes 1179656 | tf_op jit(solution)/shard_map/cond/branch_1_fun/ppermute | solution.py:629
  121.0 20.2 %collective-permute-start.11 = (bf16[128,1536]{1,0:T(8,128)(2,1)}, bf16[128,1536]{1,0:T(8,128)(2,1)S(1)}, u32[]{:S(2)}, u32[]{:S(2)}) collective-permute-start(bf16[128,1536]{1,0:T(8,128)(2,1)} %get-tuple-element.259), channel_id=1, source_target_pairs={{0,4},{2,6},{4,0},{6,2},{1,5},{3,7},{5,1},{7,3},{8,12},{10,14},{12... | collective-permute-start | bytes 1179656 | tf_op jit(solution)/shard_map/cond/branch_1_fun/ppermute | solution.py:629
  185.4 19.5 %collective-permute-start.52 = (bf16[64,1536]{1,0:T(8,128)(2,1)}, bf16[64,1536]{1,0:T(8,128)(2,1)}, u32[]{:S(2)}, u32[]{:S(2)}) collective-permute-start(bf16[64,1536]{1,0:T(8,128)(2,1)} %slice.149), channel_id=1, source_target_pairs={{0,4},{2,6},{4,0},{6,2},{1,5},{3,7},{5,1},{7,3},{8,12},{10,14},{12... | collective-permute-start | bytes 589832 | tf_op jit(solution)/shard_map/ppermute | solution.py:629
  223.2 19.4 %collective-permute-start.58 = (bf16[128,1536]{1,0:T(8,128)(2,1)}, bf16[128,1536]{1,0:T(8,128)(2,1)S(1)}, u32[]{:S(2)}, u32[]{:S(2)}) collective-permute-start(bf16[128,1536]{1,0:T(8,128)(2,1)} %get-tuple-element.710), channel_id=1, source_target_pairs={{0,2},{2,0},{4,6},{6,4},{1,3},{3,1},{5,7},{7,5},{8,10},{10,8},{12,... | collective-permute-start | bytes 1179656 | tf_op jit(solution)/shard_map/ppermute | solution.py:629
  269.0 86.5 %collective-permute-start.64 = (bf16[1152,384]{1,0:T(8,128)(2,1)}, bf16[1152,384]{1,0:T(8,128)(2,1)}, u32[]{:S(2)}, u32[]{:S(2)}) collective-permute-start(bf16[1152,384]{1,0:T(8,128)(2,1)} %get-tuple-element.737), channel_id=1, source_target_pairs={{0,8},{8,16},{16,24},{24,0},{1,9},{9,17},{17,25},{25,1},{2,10},{10... | collective-permute-start | bytes 2654216 | tf_op jit(solution)/shard_map/ppermute | solution.py:638
  269.3 86.2 %collective-permute-start.65 = (bf16[1152,384]{1,0:T(8,128)(2,1)}, bf16[1152,384]{1,0:T(8,128)(2,1)}, u32[]{:S(2)}, u32[]{:S(2)}) collective-permute-start(bf16[1152,384]{1,0:T(8,128)(2,1)} %get-tuple-element.738), channel_id=1, source_target_pairs={{0,16},{8,24},{16,0},{24,8},{1,17},{9,25},{17,1},{25,9},{2,18},{10... | collective-permute-start | bytes 2654216 | tf_op jit(solution)/shard_map/ppermute | solution.py:638
  272.8 82.7 %collective-permute-start.66 = (bf16[1152,384]{1,0:T(8,128)(2,1)}, bf16[1152,384]{1,0:T(8,128)(2,1)}, u32[]{:S(2)}, u32[]{:S(2)}) collective-permute-start(bf16[1152,384]{1,0:T(8,128)(2,1)} %get-tuple-element.739), channel_id=1, source_target_pairs={{0,24},{8,0},{16,8},{24,16},{1,25},{9,1},{17,9},{25,17},{2,26},{10... | collective-permute-start | bytes 2654216 | tf_op jit(solution)/shard_map/ppermute | solution.py:638
  355.5 69.4 %collective-permute-start.70 = (bf16[768,384]{1,0:T(8,128)(2,1)}, bf16[768,384]{1,0:T(8,128)(2,1)}, u32[]{:S(2)}, u32[]{:S(2)}) collective-permute-start(bf16[768,384]{1,0:T(8,128)(2,1)} %get-tuple-element.791), channel_id=1, source_target_pairs={{0,8},{8,16},{16,24},{24,0},{1,9},{9,17},{17,25},{25,1},{2,10},{10... | collective-permute-start | bytes 1769480 | tf_op jit(solution)/shard_map/ppermute | solution.py:638
  357.3 67.7 %collective-permute-start.71 = (bf16[768,384]{1,0:T(8,128)(2,1)}, bf16[768,384]{1,0:T(8,128)(2,1)}, u32[]{:S(2)}, u32[]{:S(2)}) collective-permute-start(bf16[768,384]{1,0:T(8,128)(2,1)} %get-tuple-element.792), channel_id=1, source_target_pairs={{0,16},{8,24},{16,0},{24,8},{1,17},{9,25},{17,1},{25,9},{2,18},{10... | collective-permute-start | bytes 1769480 | tf_op jit(solution)/shard_map/ppermute | solution.py:638
  359.4 65.6 %collective-permute-start.72 = (bf16[768,384]{1,0:T(8,128)(2,1)}, bf16[768,384]{1,0:T(8,128)(2,1)}, u32[]{:S(2)}, u32[]{:S(2)}) collective-permute-start(bf16[768,384]{1,0:T(8,128)(2,1)} %get-tuple-element.793), channel_id=1, source_target_pairs={{0,24},{8,0},{16,8},{24,16},{1,25},{9,1},{17,9},{25,17},{2,26},{10... | collective-permute-start | bytes 1769480 | tf_op jit(solution)/shard_map/ppermute | solution.py:638
  366.5 37.1 %collective-permute-start.6 = (bf16[2304,384]{1,0:T(8,128)(2,1)S(1)}, bf16[2304,384]{1,0:T(8,128)(2,1)}, u32[]{:S(2)}, u32[]{:S(2)}) collective-permute-start(bf16[2304,384]{1,0:T(8,128)(2,1)S(1)} %get-tuple-element.1357), channel_id=1, source_target_pairs={{0,2},{2,0},{4,6},{6,4},{1,3},{3,1},{5,7},{7,5},{8,10},{10,8},{12,... | collective-permute-start | bytes 5308424 | tf_op jit(solution)/shard_map/cond/branch_1_fun/ppermute | solution.py:629
  367.9 38.5 %collective-permute-start.7 = (bf16[2304,384]{1,0:T(8,128)(2,1)S(1)}, bf16[2304,384]{1,0:T(8,128)(2,1)}, u32[]{:S(2)}, u32[]{:S(2)}) collective-permute-start(bf16[2304,384]{1,0:T(8,128)(2,1)S(1)} %get-tuple-element.1357), channel_id=1, source_target_pairs={{0,4},{2,6},{4,0},{6,2},{1,5},{3,7},{5,1},{7,3},{8,12},{10,14},{12... | collective-permute-start | bytes 5308424 | tf_op jit(solution)/shard_map/cond/branch_1_fun/ppermute | solution.py:629
  429.5 21.3 %collective-permute-start.69 = (bf16[128,1536]{1,0:T(8,128)(2,1)}, bf16[128,1536]{1,0:T(8,128)(2,1)S(1)}, u32[]{:S(2)}, u32[]{:S(2)}) collective-permute-start(bf16[128,1536]{1,0:T(8,128)(2,1)} %get-tuple-element.783), channel_id=1, source_target_pairs={{0,8},{8,0},{16,24},{24,16},{1,9},{9,1},{17,25},{25,17},{2,10},{10... | collective-permute-start | bytes 1179656 | tf_op jit(solution)/shard_map/ppermute | solution.py:632
  (116 other events, 1094.9 us)
Sparse Core Ops, SparseCore 0:
  67.3 75.5 all-gather.2
